TPU v7x, 128 devices: a whole 4x4x4 slice. The times are simulated.
128 devices in a mesh: clu: 32 (over y, z, core), col: 4 (over x).
Axes of the slice: x: 4, y: 4, z: 4, core: 2. Of those that a mesh axis runs over, the one named last changes fastest.
Arguments:
- track_dest: int32 [131072, 1], P(('clu', 'col')), may hold values from 0 to 31; in each aligned block of 1024 rows (0 to 1023, 1024 to 2047, ...) at most 80 rows name the same one
- obs_count: int32 [131072], P(('clu', 'col')), may hold values from 1 to 8
- track_jac: bfloat16 [131072, 1728], P(('clu', 'col'))
- point_info: float32 [3, 3, 131072], P(None, None, ('clu', 'col')), as said below
- point_grad: float32 [3, 131072], P(None, ('clu', 'col')), may hold values from -6 to 6
- camera_grad: float32 [32, 576], P('clu', 'col'), may hold values from -6 to 6
- camera_diag: float32 [32, 576], P('clu', 'col'), may hold values from 6 to 12
- step_scale: float32 [32, 576], P('clu', 'col'), may hold values from 0.03 to 0.09
- covis_blocks: bfloat16 [32, 4, 576, 576], P('clu', None, None, 'col'), may hold values from -0.625 to 0.625
- cluster_colour: int32 [32], replicated, may hold values from 0 to 3, as said below
- round_partner: int32 [4, 4, 32], replicated, may hold values from 0 to 31, as said below
Outputs:
- solution: float32 [32, 576], P('clu', 'col')
- reduced_rhs: float32 [32, 576], P('clu', 'col')
Inputs may be any that keep to these rules, and one draw needn't show every extreme that they name: `track_dest`: among the tracks of one device at most 80 name one cluster, and in every draw some cluster is named by exactly 80 of some device's tracks. `point_info`: each 3 x 3 block is symmetric with a dominant positive diagonal. `cluster_colour`: each colour holds 8 clusters. `round_partner`: each round is a matching: the partner of a cluster's partner is the cluster itself; a cluster of colour k has a partner of another colour in every round of colour k; clusters left out of a round name themselves.
All inputs are finite; a program needn't handle non-finite values.
Results may differ from a plain program's by a relative error of at most 0.0003.
Values may be sent and summed in bfloat16 or wider, within the bound.
No kernel may reach another device: no remote copies, remote signals or barrier semaphores. Data moves between devices by JAX's collectives and lax.ppermute only.
A program may use at most 128 MiB of HBM per device.

v0:
```python
import jax
import jax.numpy as jnp
from jax import lax
from jax.sharding import PartitionSpec as P

ROUNDS = 4
COLOURS = 4
COLOUR_PASSES = 2


def weigh(coefs, jac):
    rows = []
    for a in range(3):
        acc = coefs[3 * a][:, None] * jac[:, 0, :].astype(jnp.float32)
        acc = acc + coefs[3 * a + 1][:, None] * jac[:, 1, :].astype(jnp.float32)
        acc = acc + coefs[3 * a + 2][:, None] * jac[:, 2, :].astype(jnp.float32)
        rows.append(acc)
    return jnp.stack(rows, 1).astype(jnp.bfloat16)


def pick_entry(table, position):
    return jnp.sum(
        jnp.where(jnp.arange(table.shape[-1], dtype=jnp.int32) == position, table, 0), axis=-1
    )


def split_three(vector):
    q_high = lax.optimization_barrier(vector.astype(jnp.bfloat16))
    remainder = vector - q_high.astype(jnp.float32)
    q_middle = lax.optimization_barrier(remainder.astype(jnp.bfloat16))
    leftover = remainder - q_middle.astype(jnp.float32)
    q_lowest = leftover.astype(jnp.bfloat16)
    return jnp.stack([q_high, q_middle, q_lowest], 0)


def join_three(pieces):
    wide = pieces.astype(jnp.float32)
    return wide[0] + wide[1] + wide[2]


def per_device(
    track_dest,
    obs_count,
    track_jac,
    point_info,
    point_grad,
    camera_grad,
    camera_diag,
    step_scale,
    covis_blocks,
    cluster_colour,
    round_partner,
):
    n_clu = lax.axis_size("clu")
    n_col = lax.axis_size("col")
    myself = lax.axis_index("clu")
    width = track_jac.shape[1] // 3
    trk = track_dest.shape[0]
    capacity = n_col * ((5 * trk + 2 * n_clu * n_col - 1) // (2 * n_clu * n_col))
    dest = track_dest[:, 0]
    onehot = (dest[:, None] == jnp.arange(n_clu, dtype=jnp.int32)[None, :]).astype(jnp.int32)
    rank = jnp.sum((jnp.cumsum(onehot, 0) - onehot) * onehot, 1)
    coef = obs_count.astype(jnp.float32)[None, None, :] * point_info
    qvec = jnp.sum(coef * point_grad[None, :, :], axis=1)
    small = jnp.concatenate([coef.reshape(9, trk), qvec], 0)
    small_parts = split_three(small).reshape(36, trk)
    wbuf = jnp.zeros((n_clu, capacity, 3 * width), jnp.bfloat16).at[dest, rank].set(track_jac)
    sbuf = (
        jnp.zeros((n_clu, 36, capacity), jnp.bfloat16)
        .at[dest, :, rank]
        .set(jnp.transpose(small_parts))
    )
    wrecv, srecv = (
        lax.all_to_all(wbuf, "clu", split_axis=0, concat_axis=0, tiled=True),
        lax.all_to_all(sbuf, "clu", split_axis=0, concat_axis=0, tiled=True),
    )
    rows = wrecv.shape[0] * wrecv.shape[1]
    jac = wrecv.reshape(rows, 3, width)
    smalls = join_three(jnp.transpose(srecv, (1, 0, 2)).reshape(3, 12, rows))
    weighted = weigh(smalls[:9], jac)
    jac2 = jac.reshape(rows * 3, width)
    wgt2 = weighted.reshape(rows * 3, width)
    share = width // n_col
    eliminated_rows = lax.psum_scatter(
        lax.dot_general(wgt2, jac2, (((0,), (0,)), ((), ())), preferred_element_type=jnp.float32),
        "col",
        scatter_dimension=0,
        tiled=True,
    )
    qv = jnp.transpose(smalls[9:12]).reshape(rows * 3)
    q_parts = split_three(qv)
    rhs_part = jnp.sum(jnp.dot(q_parts, jac2, preferred_element_type=jnp.float32), 0)
    reduced_rhs = camera_grad[0] - lax.psum_scatter(
        rhs_part, "col", scatter_dimension=0, tiled=True
    )
    my_colour = pick_entry(cluster_colour, myself)
    blocks = covis_blocks[0].astype(jnp.float32)
    lanes = jnp.arange(n_clu, dtype=jnp.int32)
    solution = jnp.zeros((share,), jnp.float32)
    for sweep in range(COLOUR_PASSES):
        for colour in range(COLOURS):
            partners = pick_entry(round_partner[colour], myself)
            near_list = []
            for round_now in range(ROUNDS):
                outgoing = jnp.where(
                    (lanes == partners[round_now])[:, None], solution[None, :], 0.0
                )
                incoming = lax.all_to_all(outgoing, "clu", split_axis=0, concat_axis=0, tiled=True)
                selector = (lanes == partners[round_now]).astype(jnp.float32)
                near_list.append(jnp.dot(selector, incoming, precision=lax.Precision.HIGHEST))
            near = jnp.stack(near_list, 0)
            self_partner = jnp.dot(solution, eliminated_rows, precision=lax.Precision.HIGHEST)
            coupled = jnp.einsum("rij,rj->i", blocks, near, precision=lax.Precision.HIGHEST)
            summed = lax.psum_scatter(
                self_partner - coupled, "col", scatter_dimension=0, tiled=True
            )
            resid = reduced_rhs - camera_diag[0] * solution + summed
            solution = jnp.where(my_colour == colour, solution + step_scale[0] * resid, solution)
    return (solution[None, :], reduced_rhs[None, :])


def solution(mesh):
    in_specs = (
        P(("clu", "col"), None),
        P(("clu", "col")),
        P(("clu", "col"), None),
        P(None, None, ("clu", "col")),
        P(None, ("clu", "col")),
        P("clu", "col"),
        P("clu", "col"),
        P("clu", "col"),
        P("clu", None, None, "col"),
        P(),
        P(),
    )
    out_specs = (P("clu", "col"), P("clu", "col"))
    return jax.shard_map(
        per_device, mesh=mesh, in_specs=in_specs, out_specs=out_specs, check_vma=False
    )
```

profile of v0, /device:TPU:1, one launch (start us, length us, event | category | flops | bytes accessed | tf_op | source)
XLA Modules:
  0.0 813.2 jit_solution(16298972954712815292)
XLA Ops:
  8.0 9.0 %reduce-window.6 = s32[32,8,128]{2,1,0:T(8,128)S(1)} reduce-window(s32[32,8,128]{2,1,0:T(8,128)S(1)} %fusion.24, s32[]{:T(128)} %constant.12.clone.1), window={size=1x1x128 pad=0_0x0_0x127_0}, to_apply=%region_1.2 | reduce-window | flops 4161536 | bytes 262148 | tf_op jit(solution)/shard_map/reduce-window
  26.7 9.6 %all-to-all-start = ((bf16[32,36,80]{2,1,0:T(8,128)(2,1)}), bf16[32,36,80]{2,1,0:T(8,128)(2,1)S(1)}, u32[]{:S(2)}, u32[]{:S(2)}) async-start(bf16[32,36,80]{2,1,0:T(8,128)(2,1)} %bitcast.12), calls=%async_computation | async-start | bytes 655360 | tf_op jit(solution)/shard_map/all_to_all | solution.py:75
  42.2 12.1 %scatter_custom_fusion.1 = bf16[2560,1728]{1,0:T(8,128)(2,1)} fusion(s32[1024]{0:T(1024)S(1)} %broadcast_select_fusion.28, bf16[1024,1728]{1,0:T(8,128)(2,1)} %copy.36, bf16[]{:T(256)} %constant.6.clone.1), kind=kCustom, calls=%fused_computation.21 | custom fusion | bytes 8847872
  54.3 7.6 all-to-all-start.1
  74.4 108.9 %all-to-all-done.1 = bf16[32,80,1728]{2,1,0:T(8,128)(2,1)} async-done(((bf16[32,80,1728]{2,1,0:T(8,128)(2,1)}), bf16[32,80,1728]{2,1,0:T(8,128)(2,1)}, u32[]{:S(2)}, u32[]{:S(2)}) %all-to-all-start.1) | async-done | bytes 8847392 | tf_op jit(solution)/shard_map/all_to_all | solution.py:74
  183.3 22.7 %reshape.1496 = bf16[2560,3,576]{2,1,0:T(4,128)(2,1)} reshape(bf16[32,80,1728]{2,1,0:T(8,128)(2,1)} %all-to-all-done.1) | data formatting | bytes 17694720 | tf_op jit(solution)/shard_map/reshape | solution.py:78
  206.0 24.9 %fusion.186 = (bf16[2560,1,576]{2,1,0:T(2,128)(2,1)}, bf16[2560,1,576]{2,1,0:T(2,128)(2,1)}, bf16[2560,1,576]{2,1,0:T(2,128)(2,1)}) fusion(bf16[2560,3,576]{2,1,0:T(4,128)(2,1)} %reshape.1496), kind=kLoop, calls=%fused_computation.319 | loop fusion | bytes 17694720 | tf_op jit(solution)/shard_map/slice | solution.py:16
  230.9 13.4 %copy.76 = bf16[2560,1,576]{0,2,1:T(8,128)(2,1)} copy(bf16[2560,1,576]{2,1,0:T(2,128)(2,1)} %get-tuple-element.23) | data formatting | bytes 5898240
  244.3 13.4 %copy.77 = bf16[2560,1,576]{0,2,1:T(8,128)(2,1)} copy(bf16[2560,1,576]{2,1,0:T(2,128)(2,1)} %get-tuple-element.22) | data formatting | bytes 5898240
  257.8 13.4 %copy.78 = bf16[2560,1,576]{0,2,1:T(8,128)(2,1)} copy(bf16[2560,1,576]{2,1,0:T(2,128)(2,1)} %get-tuple-element.21) | data formatting | bytes 5898240
  281.3 20.0 %copy.38 = bf16[2560,3,576]{2,1,0:T(4,128)(2,1)} copy(bf16[2560,3,576]{0,2,1:T(8,128)(2,1)} %pad_maximum_fusion) | data formatting | bytes 17694720 | tf_op jit(solution)/shard_map/stack | solution.py:18
  301.2 23.9 %convert_element_type.133 = bf16[7680,576]{1,0:T(8,128)(2,1)} reshape(bf16[2560,3,576]{2,1,0:T(4,128)(2,1)} %copy.38) | data formatting | bytes 17694720 | tf_op jit(solution)/shard_map/convert_element_type | solution.py:18
  325.1 18.0 %reshape_reshape.3 = bf16[7680,576]{1,0:T(8,128)(2,1)} reshape(bf16[32,80,1728]{2,1,0:T(8,128)(2,1)} %all-to-all-done.1) | data formatting | bytes 17694720 | tf_op jit(solution)/shard_map/reshape;reshape | solution.py:81
  343.0 12.6 %fusion.191 = f32[576,576]{1,0:T(8,128)} fusion(bf16[7680,576]{1,0:T(8,128)(2,1)} %convert_element_type.133, bf16[7680,576]{1,0:T(8,128)(2,1)} %reshape_reshape.3), kind=kOutput, calls=%fused_computation.324 | convolution fusion | flops 5096079360 | bytes 19021824 | tf_op jit(solution)/shard_map/dot_general | solution.py:85
  371.0 28.9 %reduce-scatter.2.cloned.1.call-done = f32[144,576]{1,0:T(8,128)} async-done(((f32[576,576]{1,0:T(8,128)}), f32[144,576]{1,0:T(8,128)}) %reduce-scatter.2.cloned.1.call-update) | async-done | bytes 331792 | tf_op jit(solution)/shard_map/reduce_scatter | solution.py:84
  401.2 8.3 %all-reduce.9 = (f32[576]{0:T(1024)S(1)}, f32[576]{0:T(1024)S(1)}) all-reduce(f32[576]{0:T(1024)S(1)} %sub.73, f32[576]{0:T(1024)S(1)} %convolution_reduce_fusion), channel_id=4, replica_groups=mesh['clu'=32,'col'=4] {'col'}, use_global_device_ids=true, to_apply=%region_11.12.clone | all-reduce | flops 1152 | bytes 9216
  410.5 9.9 %all-to-all-start.5 = ((f32[32,1,144]{2,1,0:T(1,128)}), f32[32,1,144]{2,1,0:T(1,128)S(1)}, u32[]{:S(2)}, u32[]{:S(2)}) async-start(f32[32,1,144]{2,1,0:T(1,128)} %get-tuple-element.52), calls=%async_computation.6 | async-start | bytes 65536 | tf_op jit(solution)/shard_map/all_to_all | solution.py:108
  518.5 6.9 all-reduce.3
  588.6 7.1 all-to-all-done.17
  630.6 6.9 all-reduce.5
  644.7 7.1 all-to-all-done.21
  700.4 7.1 all-to-all-done.25
  742.6 6.9 all-reduce.7
  756.5 7.1 all-to-all-done.29
  (227 shorter events, 389.3 us)
Async XLA Ops:
  26.7 27.6 %all-to-all-start = ((bf16[32,36,80]{2,1,0:T(8,128)(2,1)}), bf16[32,36,80]{2,1,0:T(8,128)(2,1)S(1)}, u32[]{:S(2)}, u32[]{:S(2)}) async-start(bf16[32,36,80]{2,1,0:T(8,128)(2,1)} %bitcast.12), calls=%async_computation | async-start | bytes 655360 | tf_op jit(solution)/shard_map/all_to_all | solution.py:75
  54.3 129.0 %all-to-all-start.1 = ((bf16[32,80,1728]{2,1,0:T(8,128)(2,1)}), bf16[32,80,1728]{2,1,0:T(8,128)(2,1)}, u32[]{:S(2)}, u32[]{:S(2)}) async-start(bf16[32,80,1728]{2,1,0:T(8,128)(2,1)} %bitcast.340), calls=%async_computation.1 | async-start | bytes 18350080 | tf_op jit(solution)/shard_map/all_to_all | solution.py:74
  61.9 338.0 %reduce-scatter.2.cloned.1.call-start = ((), (), s32[]{:S(2)}) async-start(), calls=%async_computation.31 | async-start | bytes 1843200 | tf_op jit(solution)/shard_map/reduce_scatter | solution.py:84
  410.5 17.2 %all-to-all-start.5 = ((f32[32,1,144]{2,1,0:T(1,128)}), f32[32,1,144]{2,1,0:T(1,128)S(1)}, u32[]{:S(2)}, u32[]{:S(2)}) async-start(f32[32,1,144]{2,1,0:T(1,128)} %get-tuple-element.52), calls=%async_computation.6 | async-start | bytes 65536 | tf_op jit(solution)/shard_map/all_to_all | solution.py:108
  427.7 11.2 %all-to-all-start.4 = ((f32[32,1,144]{2,1,0:T(1,128)}), f32[32,1,144]{2,1,0:T(1,128)S(1)}, u32[]{:S(2)}, u32[]{:S(2)}) async-start(f32[32,1,144]{2,1,0:T(1,128)} %get-tuple-element.54), calls=%async_computation.5 | async-start | bytes 65536 | tf_op jit(solution)/shard_map/all_to_all | solution.py:108
  450.2 11.3 %all-to-all-start.2 = ((f32[32,1,144]{2,1,0:T(1,128)}), f32[32,1,144]{2,1,0:T(1,128)S(1)}, u32[]{:S(2)}, u32[]{:S(2)}) async-start(f32[32,1,144]{2,1,0:T(1,128)} %get-tuple-element.51), calls=%async_computation.3 | async-start | bytes 65536 | tf_op jit(solution)/shard_map/all_to_all | solution.py:108
  470.3 13.2 %all-to-all-start.9 = ((f32[32,1,144]{2,1,0:T(1,128)}), f32[32,1,144]{2,1,0:T(1,128)S(1)}, u32[]{:S(2)}, u32[]{:S(2)}) async-start(f32[32,1,144]{2,1,0:T(1,128)} %get-tuple-element.48), calls=%async_computation.10 | async-start | bytes 65536 | tf_op jit(solution)/shard_map/all_to_all | solution.py:108
  483.5 11.2 %all-to-all-start.8 = ((f32[32,1,144]{2,1,0:T(1,128)}), f32[32,1,144]{2,1,0:T(1,128)S(1)}, u32[]{:S(2)}, u32[]{:S(2)}) async-start(f32[32,1,144]{2,1,0:T(1,128)} %get-tuple-element.50), calls=%async_computation.9 | async-start | bytes 65536 | tf_op jit(solution)/shard_map/all_to_all | solution.py:108
  506.0 11.3 %all-to-all-start.6 = ((f32[32,1,144]{2,1,0:T(1,128)}), f32[32,1,144]{2,1,0:T(1,128)S(1)}, u32[]{:S(2)}, u32[]{:S(2)}) async-start(f32[32,1,144]{2,1,0:T(1,128)} %get-tuple-element.47), calls=%async_computation.7 | async-start | bytes 65536 | tf_op jit(solution)/shard_map/all_to_all | solution.py:108
  526.3 13.2 %all-to-all-start.13 = ((f32[32,1,144]{2,1,0:T(1,128)}), f32[32,1,144]{2,1,0:T(1,128)S(1)}, u32[]{:S(2)}, u32[]{:S(2)}) async-start(f32[32,1,144]{2,1,0:T(1,128)} %get-tuple-element.44), calls=%async_computation.14 | async-start | bytes 65536 | tf_op jit(solution)/shard_map/all_to_all | solution.py:108
  539.5 11.2 %all-to-all-start.12 = ((f32[32,1,144]{2,1,0:T(1,128)}), f32[32,1,144]{2,1,0:T(1,128)S(1)}, u32[]{:S(2)}, u32[]{:S(2)}) async-start(f32[32,1,144]{2,1,0:T(1,128)} %get-tuple-element.46), calls=%async_computation.13 | async-start | bytes 65536 | tf_op jit(solution)/shard_map/all_to_all | solution.py:108
  562.0 11.3 %all-to-all-start.10 = ((f32[32,1,144]{2,1,0:T(1,128)}), f32[32,1,144]{2,1,0:T(1,128)S(1)}, u32[]{:S(2)}, u32[]{:S(2)}) async-start(f32[32,1,144]{2,1,0:T(1,128)} %get-tuple-element.43), calls=%async_computation.11 | async-start | bytes 65536 | tf_op jit(solution)/shard_map/all_to_all | solution.py:108
  582.4 13.3 %all-to-all-start.17 = ((f32[32,1,144]{2,1,0:T(1,128)}), f32[32,1,144]{2,1,0:T(1,128)S(1)}, u32[]{:S(2)}, u32[]{:S(2)}) async-start(f32[32,1,144]{2,1,0:T(1,128)} %get-tuple-element.40), calls=%async_computation.18 | async-start | bytes 65536 | tf_op jit(solution)/shard_map/all_to_all | solution.py:108
  618.1 11.3 %all-to-all-start.14 = ((f32[32,1,144]{2,1,0:T(1,128)}), f32[32,1,144]{2,1,0:T(1,128)S(1)}, u32[]{:S(2)}, u32[]{:S(2)}) async-start(f32[32,1,144]{2,1,0:T(1,128)} %get-tuple-element.39), calls=%async_computation.15 | async-start | bytes 65536 | tf_op jit(solution)/shard_map/all_to_all | solution.py:108
  638.4 13.3 %all-to-all-start.21 = ((f32[32,1,144]{2,1,0:T(1,128)}), f32[32,1,144]{2,1,0:T(1,128)S(1)}, u32[]{:S(2)}, u32[]{:S(2)}) async-start(f32[32,1,144]{2,1,0:T(1,128)} %get-tuple-element.36), calls=%async_computation.22 | async-start | bytes 65536 | tf_op jit(solution)/shard_map/all_to_all | solution.py:108
  651.7 11.2 %all-to-all-start.20 = ((f32[32,1,144]{2,1,0:T(1,128)}), f32[32,1,144]{2,1,0:T(1,128)S(1)}, u32[]{:S(2)}, u32[]{:S(2)}) async-start(f32[32,1,144]{2,1,0:T(1,128)} %get-tuple-element.38), calls=%async_computation.21 | async-start | bytes 65536 | tf_op jit(solution)/shard_map/all_to_all | solution.py:108
  674.2 11.3 %all-to-all-start.18 = ((f32[32,1,144]{2,1,0:T(1,128)}), f32[32,1,144]{2,1,0:T(1,128)S(1)}, u32[]{:S(2)}, u32[]{:S(2)}) async-start(f32[32,1,144]{2,1,0:T(1,128)} %get-tuple-element.35), calls=%async_computation.19 | async-start | bytes 65536 | tf_op jit(solution)/shard_map/all_to_all | solution.py:108
  694.3 13.3 %all-to-all-start.25 = ((f32[32,1,144]{2,1,0:T(1,128)}), f32[32,1,144]{2,1,0:T(1,128)S(1)}, u32[]{:S(2)}, u32[]{:S(2)}) async-start(f32[32,1,144]{2,1,0:T(1,128)} %get-tuple-element.32), calls=%async_computation.26 | async-start | bytes 65536 | tf_op jit(solution)/shard_map/all_to_all | solution.py:108
  707.5 11.3 %all-to-all-start.24 = ((f32[32,1,144]{2,1,0:T(1,128)}), f32[32,1,144]{2,1,0:T(1,128)S(1)}, u32[]{:S(2)}, u32[]{:S(2)}) async-start(f32[32,1,144]{2,1,0:T(1,128)} %get-tuple-element.34), calls=%async_computation.25 | async-start | bytes 65536 | tf_op jit(solution)/shard_map/all_to_all | solution.py:108
  718.8 11.3 %all-to-all-start.23 = ((f32[32,1,144]{2,1,0:T(1,128)}), f32[32,1,144]{2,1,0:T(1,128)S(1)}, u32[]{:S(2)}, u32[]{:S(2)}) async-start(f32[32,1,144]{2,1,0:T(1,128)} %get-tuple-element.33), calls=%async_computation.24 | async-start | bytes 65536 | tf_op jit(solution)/shard_map/all_to_all | solution.py:108
  730.1 11.3 %all-to-all-start.22 = ((f32[32,1,144]{2,1,0:T(1,128)}), f32[32,1,144]{2,1,0:T(1,128)S(1)}, u32[]{:S(2)}, u32[]{:S(2)}) async-start(f32[32,1,144]{2,1,0:T(1,128)} %get-tuple-element.31), calls=%async_computation.23 | async-start | bytes 65536 | tf_op jit(solution)/shard_map/all_to_all | solution.py:108
  750.3 13.3 %all-to-all-start.29 = ((f32[32,1,144]{2,1,0:T(1,128)}), f32[32,1,144]{2,1,0:T(1,128)S(1)}, u32[]{:S(2)}, u32[]{:S(2)}) async-start(f32[32,1,144]{2,1,0:T(1,128)} %get-tuple-element.28), calls=%async_computation.30 | async-start | bytes 65536 | tf_op jit(solution)/shard_map/all_to_all | solution.py:108
  763.6 11.3 %all-to-all-start.28 = ((f32[32,1,144]{2,1,0:T(1,128)}), f32[32,1,144]{2,1,0:T(1,128)S(1)}, u32[]{:S(2)}, u32[]{:S(2)}) async-start(f32[32,1,144]{2,1,0:T(1,128)} %get-tuple-element.30), calls=%async_computation.29 | async-start | bytes 65536 | tf_op jit(solution)/shard_map/all_to_all | solution.py:108
  774.9 11.3 %all-to-all-start.27 = ((f32[32,1,144]{2,1,0:T(1,128)}), f32[32,1,144]{2,1,0:T(1,128)S(1)}, u32[]{:S(2)}, u32[]{:S(2)}) async-start(f32[32,1,144]{2,1,0:T(1,128)} %get-tuple-element.29), calls=%async_computation.28 | async-start | bytes 65536 | tf_op jit(solution)/shard_map/all_to_all | solution.py:108
  (16 other events, 1182.0 us)
Sparse Core Ops, SparseCore 0:
  355.7 44.0 reduce-scatter.1
where the time goes:
time: 828 us; the launch traced here: 813 us
  waiting for transfers between devices  324 us (39%)
  local copies, waits for them, and re-layouts  177 us (21%)
  starting transfers between devices  144 us (17%)
  blocking collectives  55.5 us (7%)
  matrix products  51.9 us (6%)
  other arithmetic  42.7 us (5%)
  between operations  18.5 us (2%)
    all_to_all x28, waiting for transfers between devices, per_device(): lax.all_to_all(outgoing, 'clu', split_axis=0, concat_axis=0, tiled=True)  186 us
    all_to_all x28, starting transfers between devices, per_device(): lax.all_to_all(outgoing, 'clu', split_axis=0, concat_axis=0, tiled=True)  126 us
    all_to_all x1, waiting for transfers between devices, per_device(): lax.all_to_all(wbuf, 'clu', split_axis=0, concat_axis=0, tiled=True)  109 us
    unnamed x26, local copies, waits for them, and re-layouts  63.3 us
    unnamed x8, blocking collectives  55.5 us
    reduce_scatter x1, waiting for transfers between devices, per_device(): lax.psum_scatter(lax.dot_general(wgt2, jac2, (((0,), (0,)), ((), ())), pr...  28.9 us
    slice x1, local copies, waits for them, and re-layouts, weigh(): acc = acc + coefs[3 * a + 2][:, None] * jac[:, 2, :].astype(jnp.float32)  24.9 us
    convert_element_type x1, local copies, waits for them, and re-layouts, weigh(): return jnp.stack(rows, 1).astype(jnp.bfloat16)  23.9 us
  transfers between devices with their start and end apart: 31, of which 30 were waited for; matrix products, arithmetic and copies ran while one was open for 8% of the time, Pallas kernels for 0%

commit v1 on v0

v1 whole, which is shorter than its diff:
```python
import functools

import jax
import jax.numpy as jnp
from jax import lax
from jax.experimental import pallas as pl
from jax.experimental.pallas import tpu as pltpu
from jax.sharding import PartitionSpec as P

CLUSTERS = 32
ROUNDS = 4
COLOURS = 4
COLS = 4
CAM = 576
SHARE = 144
WIDE = 640
SLOT = 256
TRK = 1024
NT = (((1,), (1,)), ((), ()))
NN = (((1,), (0,)), ((), ()))

MY_COLOUR, PARTNER, PARTNER_COLOUR, MY_COL, MY_CLU = 0, 1, 5, 9, 10

F32 = jnp.float32
BF16 = jnp.bfloat16


def smem():
    return pl.BlockSpec(memory_space=pltpu.SMEM)


def vmem():
    return pl.BlockSpec(memory_space=pltpu.VMEM)


def two_parts(v):
    high = v.astype(BF16)
    low = (v - high.astype(F32)).astype(BF16)
    return high, low


def widen(v, width=WIDE):
    return jnp.concatenate([v, jnp.zeros((v.shape[0], width - v.shape[1]), F32)], 1)


def place_share(share, col):
    total = jnp.zeros((1, WIDE), F32)
    for at in range(COLS):
        pieces = []
        if at:
            pieces.append(jnp.zeros((1, SHARE * at), F32))
        pieces.append(share)
        pieces.append(jnp.zeros((1, WIDE - SHARE * (at + 1)), F32))
        total = total + jnp.where(col == at, jnp.concatenate(pieces, 1), 0.0)
    return total


def take_share(vector, col):
    total = jnp.zeros((1, SHARE), F32)
    for at in range(COLS):
        total = total + jnp.where(col == at, vector[:, SHARE * at : SHARE * (at + 1)], 0.0)
    return total


def members(dest_ref):
    lanes = lax.broadcasted_iota(jnp.int32, (CLUSTERS, TRK), 0)
    return (lanes == dest_ref[...]).astype(F32)


def scatter_rows(onehot, row):
    high, low = two_parts(row)
    return jnp.concatenate(
        [onehot * high.astype(F32), onehot * low.astype(F32)], 0
    ).astype(BF16)


def fold(both):
    return both[:CLUSTERS] + both[CLUSTERS:]


def rhs_kernel(
    cc_ref, rp_ref, dest_ref, obs_ref, info_ref, grad_ref, jac_ref, cg_ref, step_ref,
    out_ref, ids_ref, total,
):
    a = pl.program_id(0)
    me = lax.axis_index("clu")
    col = lax.axis_index("col")
    obs = obs_ref[...].astype(F32)
    q = jnp.zeros((1, TRK), F32)
    for b in range(3):
        q = q + obs * info_ref[0, b : b + 1, :] * grad_ref[b : b + 1, :]
    part = fold(
        lax.dot_general(
            scatter_rows(members(dest_ref), q), jac_ref[...], NT, preferred_element_type=F32
        )
    )

    @pl.when(a == 0)
    def _():
        rows = lax.broadcasted_iota(jnp.int32, (CLUSTERS, WIDE), 0)
        total[...] = jnp.where(rows == me, place_share(cg_ref[...], col), 0.0)

    total[:, :CAM] = total[:, :CAM] - part

    @pl.when(a == 2)
    def _():
        mine = cc_ref[me]
        ids_ref[MY_COLOUR] = mine
        ids_ref[MY_COL] = col
        ids_ref[MY_CLU] = me
        for r in range(ROUNDS):
            p = rp_ref[mine, r, me]
            ids_ref[PARTNER + r] = p
            ids_ref[PARTNER_COLOUR + r] = cc_ref[p]
        share = widen(step_ref[...], SLOT)
        for c in range(CLUSTERS):
            colour = cc_ref[c]
            out_ref[c, :, 0:WIDE] = total[c : c + 1, :]
            for r in range(ROUNDS):
                p = rp_ref[colour, r, c]
                out_ref[c, :, WIDE * (r + 1) : WIDE * (r + 2)] = total[pl.ds(p, 1), :]
            out_ref[c, :, WIDE * 5 : WIDE * 5 + SLOT] = share


def gather_kernel(ids_ref, recv_ref, diag_ref, out_ref):
    vectors = recv_ref[0, :, : WIDE * 5]
    for c in range(1, CLUSTERS):
        vectors = vectors + recv_ref[c, :, : WIDE * 5]
    diag = widen(diag_ref[...], SLOT)
    shares = [recv_ref[ids_ref[MY_CLU], :, WIDE * 5 :]]
    for r in range(ROUNDS):
        shares.append(recv_ref[ids_ref[PARTNER + r], :, WIDE * 5 :])
    shares.append(diag)
    row = jnp.concatenate([vectors] + shares, 1)
    for k in range(COLS):
        out_ref[k] = row


def couple(ids_ref, vectors, blocks, columns):
    columns[...] = jnp.concatenate(vectors + [jnp.zeros((4, WIDE), F32)], 0).T
    col = ids_ref[MY_COL]
    acc = jnp.zeros((16, CAM), F32)
    for k in range(COLS):
        base = lax.rem(col + k, COLS) * SHARE
        for m in range(SHARE // 16):
            xs = columns[pl.ds(pl.multiple_of(base + 16 * m, 16), 16), :]
            for r in range(ROUNDS):
                acc = acc + blocks[k][r, 16 * m : 16 * m + 16, :].astype(F32) * xs[:, r : r + 1]
    return widen(jnp.sum(acc, 0, keepdims=True))


def first_step_kernel(
    ids_ref, recv_ref, b0, b1, b2, b3, state_ref, out_ref, rhs_ref, columns
):
    col = ids_ref[MY_COL]
    vectors = recv_ref[0, :, : WIDE * 5]
    for k in range(1, COLS):
        vectors = vectors + recv_ref[k, :, : WIDE * 5]

    def full(v):
        at = WIDE * 5 + SLOT * v
        return widen(jnp.concatenate([recv_ref[k, :, at : at + SHARE] for k in range(COLS)], 1))

    rhs = vectors[:, :WIDE]
    step, diag = full(0), full(5)
    near = []
    for r in range(ROUNDS):
        x = full(r + 1) * vectors[:, WIDE * (r + 1) : WIDE * (r + 2)]
        near.append(jnp.where(ids_ref[PARTNER_COLOUR + r] == 0, x, 0.0))
    coupled = couple(ids_ref, near, (b0, b1, b2, b3), columns)
    mine = ids_ref[MY_COLOUR]
    x = jnp.where(mine == 0, step * rhs, jnp.where(mine == 1, step * (rhs - coupled), 0.0))
    state_ref[0:1, :] = x
    state_ref[1:2, :] = rhs
    state_ref[2:3, :] = step
    state_ref[3:4, :] = diag
    rhs_ref[...] = take_share(rhs, col)
    for c in range(CLUSTERS):
        out_ref[c] = x


def step_kernel(colour, sweep, n_elim, has_send, has_recv, last, *refs):
    refs = list(refs)
    ids_ref, recv_ref, state_ref = refs[:3]
    blocks = refs[3:7]
    at = 7
    elim = jnp.zeros((1, WIDE), F32)
    for _ in range(n_elim):
        elim = elim + refs[at][...]
        at += 1
    if has_send:
        send_ref = refs[at]
        at += 1
    if last:
        share_ref = refs[at]
        at += 1
    else:
        new_ref, out_ref = refs[at : at + 2]
        at += 2
        if has_recv:
            sum_ref = refs[at]
            at += 1
    columns = refs[at]
    near = [recv_ref[ids_ref[PARTNER + r], :, :WIDE] for r in range(ROUNDS)]
    coupled = couple(ids_ref, near, blocks, columns)
    x, rhs, step, diag = (state_ref[i : i + 1, :] for i in range(4))
    resid = rhs - coupled
    if sweep:
        resid = resid - diag * x + elim
    x = jnp.where(ids_ref[MY_COLOUR] == colour, x + step * resid, x)
    if last:
        share_ref[...] = take_share(x, ids_ref[MY_COL])
        return
    new_ref[0:1, :] = x
    new_ref[1:4, :] = state_ref[1:4, :]
    for c in range(CLUSTERS):
        out_ref[c, :, :WIDE] = x
    if has_send:
        out_ref[:, :, WIDE:] = send_ref[...]
    if has_recv:
        total = recv_ref[0, :, WIDE:]
        for c in range(1, CLUSTERS):
            total = total + recv_ref[c, :, WIDE:]
        sum_ref[...] = total


def elim_kernel(dest_ref, obs_ref, info_ref, recv_ref, jac_ref, out_ref):
    onehot = members(dest_ref)
    obs = obs_ref[...].astype(F32)
    x = recv_ref[:, 0, :CAM]
    high, low = two_parts(x)
    both = jnp.concatenate([high, low], 0)
    along = []
    for b in range(3):
        every = lax.dot_general(
            both, jac_ref[CAM * b : CAM * (b + 1), :], NN, preferred_element_type=F32
        )
        along.append(jnp.sum(fold(every) * onehot, 0, keepdims=True))
    total = jnp.zeros((2 * CLUSTERS, CAM), F32)
    for a in range(3):
        u = jnp.zeros((1, TRK), F32)
        for b in range(3):
            u = u + obs * info_ref[a, b : b + 1, :] * along[b]
        total = total + lax.dot_general(
            scatter_rows(onehot, u),
            jac_ref[CAM * a : CAM * (a + 1), :],
            NT,
            preferred_element_type=F32,
        )
    out_ref[:, 0, :] = widen(fold(total))


def shape(*dims, dtype=F32):
    return jax.ShapeDtypeStruct(dims, dtype)


def per_device(
    track_dest, obs_count, track_jac, point_info, point_grad, camera_grad, camera_diag,
    step_scale, covis_blocks, cluster_colour, round_partner,
):
    dest = jnp.transpose(track_dest)
    obs = obs_count[None, :]
    jac = jnp.transpose(track_jac)
    own = jnp.transpose(covis_blocks[0], (0, 2, 1))
    blocks = [own] + [
        lax.ppermute(own, "col", [((i + k) % COLS, i) for i in range(COLS)]) for k in (1, 2, 3)
    ]
    limit = pltpu.CompilerParams(vmem_limit_bytes=24 << 20)

    whole = lambda *block: pl.BlockSpec(block, lambda a: (0,) * len(block))
    payload, ids = pl.pallas_call(
        rhs_kernel,
        grid=(3,),
        in_specs=[
            smem(), smem(), whole(1, TRK), whole(1, TRK),
            pl.BlockSpec((1, 3, TRK), lambda a: (a, 0, 0)), whole(3, TRK),
            pl.BlockSpec((CAM, TRK), lambda a: (a, 0)), whole(1, SHARE), whole(1, SHARE),
        ],
        out_specs=[whole(CLUSTERS, 1, 5 * WIDE + SLOT), smem()],
        out_shape=[shape(CLUSTERS, 1, 5 * WIDE + SLOT), shape(16, dtype=jnp.int32)],
        scratch_shapes=[pltpu.VMEM((CLUSTERS, WIDE), F32)],
        compiler_params=limit,
        name="rhs",
    )(cluster_colour, round_partner, dest, obs, point_info, point_grad, jac, camera_grad, step_scale)

    def over_clu(v):
        return lax.all_to_all(v, "clu", split_axis=0, concat_axis=0, tiled=True)

    recv = over_clu(payload)
    payload = pl.pallas_call(
        gather_kernel,
        in_specs=[smem(), vmem(), vmem()],
        out_specs=vmem(),
        out_shape=shape(COLS, 1, 5 * WIDE + 6 * SLOT),
        compiler_params=limit,
        name="gather",
    )(ids, recv, camera_diag)
    recv = lax.all_to_all(payload, "col", split_axis=0, concat_axis=0, tiled=True)
    columns = pltpu.VMEM((WIDE, 8), F32)
    state, payload, reduced_rhs = pl.pallas_call(
        first_step_kernel,
        in_specs=[smem()] + [vmem()] * 5,
        out_specs=[vmem()] * 3,
        out_shape=[shape(4, WIDE), shape(CLUSTERS, 1, WIDE), shape(1, SHARE)],
        scratch_shapes=[columns],
        compiler_params=limit,
        name="first_step",
    )(ids, recv, *blocks)

    def eliminate(recv):
        return pl.pallas_call(
            elim_kernel,
            in_specs=[vmem()] * 5,
            out_specs=vmem(),
            out_shape=shape(CLUSTERS, 1, WIDE),
            compiler_params=limit,
            cost_estimate=pl.CostEstimate(
                flops=12 * 64 * 1024 * 576, bytes_accessed=1 << 22, transcendentals=0
            ),
            name="elim",
        )(dest, obs, point_info, recv, jac)

    def update(number, recv, state, elim=(), send=None, has_recv=False):
        last = number == 7
        outs = [shape(1, SHARE)]
        if not last:
            outs = [shape(4, WIDE), shape(CLUSTERS, 1, WIDE if send is None else 2 * WIDE)]
            if has_recv:
                outs.append(shape(1, WIDE))
        extra = list(elim) + ([] if send is None else [send])
        return pl.pallas_call(
            functools.partial(
                step_kernel, number % COLOURS, number // COLOURS, len(elim),
                send is not None, has_recv, last,
            ),
            in_specs=[smem()] + [vmem()] * (6 + len(extra)),
            out_specs=[vmem()] * len(outs),
            out_shape=outs,
            scratch_shapes=[columns],
            compiler_params=limit,
            name="step",
        )(ids, recv, state, *blocks, *extra)

    def over_col(v):
        return [v] + [
            lax.ppermute(v, "col", [((i + k) % COLS, i) for i in range(COLS)]) for k in (1, 2, 3)
        ]

    recv = over_clu(payload)
    first = eliminate(recv)
    state, payload = update(2, recv, state, send=first)
    recv = over_clu(payload)
    state, payload, part = update(3, recv, state, has_recv=True)
    elim_early = over_col(part)
    second = eliminate(recv)
    recv = over_clu(payload)
    state, payload = update(4, recv, state, elim=elim_early, send=second)
    third = eliminate(recv)
    recv = over_clu(payload)
    state, payload, part = update(5, recv, state, elim=elim_early, send=third, has_recv=True)
    elim_second = over_col(part)
    recv = over_clu(payload)
    state, payload, part = update(6, recv, state, elim=elim_second, has_recv=True)
    elim_third = over_col(part)
    recv = over_clu(payload)
    (solution,) = update(7, recv, state, elim=elim_third)
    return solution, reduced_rhs


def solution(mesh):
    in_specs = (
        P(("clu", "col"), None),
        P(("clu", "col")),
        P(("clu", "col"), None),
        P(None, None, ("clu", "col")),
        P(None, ("clu", "col")),
        P("clu", "col"),
        P("clu", "col"),
        P("clu", "col"),
        P("clu", None, None, "col"),
        P(),
        P(),
    )
    out_specs = (P("clu", "col"), P("clu", "col"))
    return jax.shard_map(
        per_device, mesh=mesh, in_specs=in_specs, out_specs=out_specs, check_vma=False
    )
```

time: 828 us -> 160 us (0.19); the launches traced: 813 us -> 158 us
  waiting for transfers between devices: 324 us -> 10.3 us
  local copies, waits for them, and re-layouts: 177 us -> 31.8 us
  starting transfers between devices: 144 us -> 40.2 us
  matrix products: 51.9 us -> 0 us
  other arithmetic: 42.7 us -> 0 us
  Pallas kernels: 0 us -> 24.5 us
  between operations: 18.5 us -> 0.92 us
    all_to_all x30 -> x4, waiting for transfers between devices: 295 us -> 6.76 us  [over_clu(): return lax.all_to_all(v, 'clu', split_axis=0, concat_axis=0, tiled=True)]
    all_to_all x30 -> x4, starting transfers between devices: 143 us -> 22.7 us  [over_clu(): return lax.all_to_all(v, 'clu', split_axis=0, concat_axis=0, tiled=True)]
    unnamed x8 -> x0, blocking collectives: 55.5 us -> none
    dot_general x50 -> x0, matrix products: 51.9 us -> none  [the longest x32 23.8 us: per_device(): jnp.dot(selector, incoming, precision=lax.Precision.HIGHEST)]
    all_to_all x0 -> x4, blocking collectives: none -> 50.5 us  [the longest x3 43.5 us: over_clu(): return lax.all_to_all(v, 'clu', split_axis=0, concat_axis=0, tiled=True)]
    another operation x7 -> x0, local copies, waits for them, and re-layouts: 38.1 us -> none  [the longest x1 20 us: weigh(): return jnp.stack(rows, 1).astype(jnp.bfloat16)]
    unnamed x26 -> x106, local copies, waits for them, and re-layouts: 63.3 us -> 31.8 us
    reduce_scatter x1 -> x0, waiting for transfers between devices: 28.9 us -> none  [per_device(): lax.psum_scatter(lax.dot_general(wgt2, jac2, (((0,), (0,)), ((), ())), pr...]
  transfers between devices with their start and end apart: 31 -> 16, of which waited for: 30 -> 8; matrix products, arithmetic and copies ran while one was open for 8% -> 0% of each run, Pallas kernels for 0% -> 6%
where the time goes in v1:
time: 160 us; the launch traced here: 158 us
  blocking collectives  50.5 us (32%)
  starting transfers between devices  40.2 us (25%)
  local copies, waits for them, and re-layouts  31.8 us (20%)
  Pallas kernels  24.5 us (15%)
  waiting for transfers between devices  10.3 us (6%)
    all_to_all x3, blocking collectives, over_clu(): return lax.all_to_all(v, 'clu', split_axis=0, concat_axis=0, tiled=True)  43.5 us
    unnamed x106, local copies, waits for them, and re-layouts  31.8 us
    all_to_all x4, starting transfers between devices, over_clu(): return lax.all_to_all(v, 'clu', split_axis=0, concat_axis=0, tiled=True)  22.7 us
    ppermute x9, starting transfers between devices, over_col(): lax.ppermute(v, 'col', [((i + k) % COLS, i) for i in range(COLS)])  11.7 us
    pallas_call x6, Pallas kernels, update(): pl.pallas_call(functools.partial(step_kernel, number % COLOURS, number //...  11.4 us
    pallas_call x3, Pallas kernels, eliminate(): pl.pallas_call(elim_kernel, in_specs=[vmem()] * 5, out_specs=vmem(), out_...  7.17 us
    all_to_all x1, blocking collectives, per_device(): lax.all_to_all(payload, 'col', split_axis=0, concat_axis=0, tiled=True)  7.01 us
    all_to_all x4, waiting for transfers between devices, over_clu(): return lax.all_to_all(v, 'clu', split_axis=0, concat_axis=0, tiled=True)  6.76 us
  transfers between devices with their start and end apart: 16, of which 8 were waited for; matrix products, arithmetic and copies ran while one was open for 0% of the time, Pallas kernels for 6%

profile of v1, /device:TPU:1, one launch (start us, length us, event | category | flops | bytes accessed | tf_op | source)
XLA Modules:
  0.0 158.2 jit_solution(3507534413233974258)
XLA Ops:
  0.6 2.1 %collective-permute-start.2 = (bf16[4,144,576]{2,1,0:T(8,128)(2,1)}, bf16[4,144,576]{2,1,0:T(8,128)(2,1)S(1)}, u32[]{:S(2)}, u32[]{:S(2)}) collective-permute-start(bf16[4,144,576]{2,1,0:T(8,128)(2,1)} %bitcast.10), channel_id=1, source_target_pairs={{3,0},{0,1},{1,2},{2,3},{7,4},{4,5},{5,6},{6,7},{11,8},{8,9},{9,10... | collective-permute-start | bytes 1990664 | tf_op jit(solution)/shard_map/ppermute | solution.py:266
  2.8 2.5 %collective-permute-start.1 = (bf16[4,144,576]{2,1,0:T(8,128)(2,1)}, bf16[4,144,576]{2,1,0:T(8,128)(2,1)S(1)}, u32[]{:S(2)}, u32[]{:S(2)}) collective-permute-start(bf16[4,144,576]{2,1,0:T(8,128)(2,1)} %bitcast.11), channel_id=1, source_target_pairs={{2,0},{3,1},{0,2},{1,3},{6,4},{7,5},{4,6},{5,7},{10,8},{11,9},{8,1... | collective-permute-start | bytes 1990664 | tf_op jit(solution)/shard_map/ppermute | solution.py:266
  6.4 2.0 %copy-done = bf16[1024,1728]{0,1:T(8,128)(2,1)S(1)} copy-done((bf16[1024,1728]{0,1:T(8,128)(2,1)S(1)}, bf16[1024,1728]{0,1:T(8,128)(2,1)}, u32[]{:S(2)}) %copy-start) | copy-done | bytes 3538968
  14.0 3.2 %rhs.1 = (f32[32,1,3456]{2,1,0:T(1,128)S(1)}, s32[16]{0:T(128)S(1)}) custom-call(s32[32]{0:T(128)S(1)} %copy-done.52, s32[4,4,32]{2,1,0:T(4,128)S(1)} %copy-done.48, s32[1,1024]{1,0:T(1,128)S(1)} %bitcast.20, s32[1,1024]{1,0:T(1,128)S(1)} %bitcast.24, f32[3,3,1024]{2,1,0:T(4,128)S(1)} %copy-done.20, f32[3,1024]{1,0:T(4,128)S(1)} %copy-done.34, ...), custom_call_target="tpu_custom_call" | custom-call | tf_op jit(solution)/shard_map/rhs/pallas_call | solution.py:271
  17.2 20.2 %all_to_all.40.recv_ref = f32[32,1,3456]{2,1,0:T(1,128)S(1)} all-to-all(f32[32,1,3456]{2,1,0:T(1,128)S(1)} %get-tuple-element.21), channel_id=1, replica_groups=mesh['clu'=32,'col'=4] {'clu'}, dimensions={0} | all-to-all | bytes 884736 | tf_op jit(solution)/shard_map/all_to_all | solution.py:287
  38.0 7.0 %all_to_all.41.recv_ref = f32[4,1,4736]{2,1,0:T(1,128)S(1)} all-to-all(f32[4,1,4736]{2,1,0:T(1,128)S(1)} %gather.1), channel_id=1, replica_groups=mesh['clu'=32,'col'=4] {'col'}, dimensions={0} | all-to-all | bytes 151552 | tf_op jit(solution)/shard_map/all_to_all | solution.py:298
  45.0 2.2 %first_step.1 = (f32[4,640]{1,0:T(4,128)S(1)}, f32[32,1,640]{2,1,0:T(1,128)S(1)}, f32[1,144]{1,0:T(1,128)}) custom-call(s32[16]{0:T(128)S(1)} %get-tuple-element.20.ids_ref.refs_0_, f32[4,1,4736]{2,1,0:T(1,128)S(1)} %all_to_all.41.recv_ref, bf16[4,144,576]{2,1,0:T(8,128)(2,1)S(1)} %bitcast.13, bf16[4,144,576]{2,1,0:T(8,128)(2,1)S(1)} %collective-permute-done.b1.refs_4_, ...), custom_call_target="tpu_custom_call" | custom-call | tf_op jit(solution)/shard_map/first_step/pallas_call | solution.py:300
  47.2 11.8 %all_to_all.42.recv_ref.refs_1_ = f32[32,1,640]{2,1,0:T(1,128)S(1)} all-to-all(f32[32,1,640]{2,1,0:T(1,128)S(1)} %get-tuple-element.22), channel_id=1, replica_groups=mesh['clu'=32,'col'=4] {'clu'}, dimensions={0} | all-to-all | bytes 163840 | tf_op jit(solution)/shard_map/all_to_all | solution.py:287
  59.0 2.1 %elim.3.refs_7_ = f32[32,1,640]{2,1,0:T(1,128)S(1)} custom-call(s32[1,1024]{1,0:T(1,128)S(1)} %bitcast.21, s32[1,1024]{1,0:T(1,128)S(1)} %bitcast.25, f32[3,3,1024]{2,1,0:T(4,128)S(1)} %copy-done.21, f32[32,1,640]{2,1,0:T(1,128)S(1)} %all_to_all.42.recv_ref.refs_1_, bf16[1728,1024]{1,0:T(8,128)(2,1)S(1)} %bitcast.7), custom_call_target="tpu_custom_call" | custom-call | flops 452984832 | bytes 4194304 | tf_op jit(solution)/shard_map/elim/pallas_call | solution.py:311
  62.6 11.5 %all_to_all.43.refs_1_.recv_ref = f32[32,1,1280]{2,1,0:T(1,128)S(1)} all-to-all(f32[32,1,1280]{2,1,0:T(1,128)S(1)} %get-tuple-element.24), channel_id=1, replica_groups=mesh['clu'=32,'col'=4] {'clu'}, dimensions={0} | all-to-all | bytes 327680 | tf_op jit(solution)/shard_map/all_to_all | solution.py:287
  76.8 4.5 %all-to-all-start.4 = ((f32[32,1,640]{2,1,0:T(1,128)}), f32[32,1,640]{2,1,0:T(1,128)}, u32[]{:S(2)}, u32[]{:S(2)}) async-start(f32[32,1,640]{2,1,0:T(1,128)} %copy-done.29), calls=%async_computation.4 | async-start | bytes 163840 | tf_op jit(solution)/shard_map/all_to_all | solution.py:287
  81.7 1.8 %collective-permute-start.4 = (f32[1,640]{1,0:T(1,128)S(1)}, f32[1,640]{1,0:T(1,128)S(1)}, u32[]{:S(2)}, u32[]{:S(2)}) collective-permute-start(f32[1,640]{1,0:T(1,128)S(1)} %get-tuple-element.28.refs_7_), channel_id=1, source_target_pairs={{2,0},{3,1},{0,2},{1,3},{6,4},{7,5},{4,6},{5,7},{10,8},{11,9},{8,1... | collective-permute-start | bytes 7688 | tf_op jit(solution)/shard_map/ppermute | solution.py:346
  85.9 2.1 %elim.4.refs_11_ = f32[32,1,640]{2,1,0:T(1,128)S(1)} custom-call(s32[1,1024]{1,0:T(1,128)S(1)} %bitcast.22, s32[1,1024]{1,0:T(1,128)S(1)} %bitcast.26, f32[3,3,1024]{2,1,0:T(4,128)S(1)} %copy-done.22, f32[32,1,1280]{2,1,0:T(1,128)S(1)} %copy-done.19, bf16[1728,1024]{1,0:T(8,128)(2,1)S(1)} %bitcast.8), custom_call_target="tpu_custom_call" | custom-call | flops 452984832 | bytes 4194304 | tf_op jit(solution)/shard_map/elim/pallas_call | solution.py:311
  101.5 8.4 %all-to-all-start.5 = ((f32[32,1,1280]{2,1,0:T(1,128)}), f32[32,1,1280]{2,1,0:T(1,128)}, u32[]{:S(2)}, u32[]{:S(2)}) async-start(f32[32,1,1280]{2,1,0:T(1,128)} %copy-done.28), calls=%async_computation.5 | async-start | bytes 327680 | tf_op jit(solution)/shard_map/all_to_all | solution.py:287
  110.7 3.0 %elim.5.refs_11_ = f32[32,1,640]{2,1,0:T(1,128)S(1)} custom-call(s32[1,1024]{1,0:T(1,128)S(1)} %bitcast.23, s32[1,1024]{1,0:T(1,128)S(1)} %bitcast.27, f32[3,3,1024]{2,1,0:T(4,128)S(1)} %copy-done.23, f32[32,1,640]{2,1,0:T(1,128)} %all-to-all-done.4.refs_1_.recv_ref, bf16[1728,1024]{1,0:T(8,128)(2,1)S(1)} %bitcast.9), custom_call_target="tpu_custom_call" | custom-call | flops 452984832 | bytes 4194304 | tf_op jit(solution)/shard_map/elim/pallas_call | solution.py:311
  114.3 3.6 %all-to-all-done.5.refs_1_ = f32[32,1,1280]{2,1,0:T(1,128)} async-done(((f32[32,1,1280]{2,1,0:T(1,128)}), f32[32,1,1280]{2,1,0:T(1,128)}, u32[]{:S(2)}, u32[]{:S(2)}) %all-to-all-start.5) | async-done | bytes 163872 | tf_op jit(solution)/shard_map/all_to_all | solution.py:287
  126.1 2.6 %step.9 = (f32[4,640]{1,0:T(4,128)S(1)}, f32[32,1,1280]{2,1,0:T(1,128)}, f32[1,640]{1,0:T(1,128)S(1)}) custom-call(s32[16]{0:T(128)S(1)} %get-tuple-element.20.ids_ref.refs_0_, f32[32,1,1280]{2,1,0:T(1,128)} %all-to-all-done.5.refs_1_, f32[4,640]{1,0:T(4,128)S(1)} %copy-done.47, bf16[4,144,576]{2,1,0:T(8,128)(2,1)S(1)} %bitcast.17, ...), custom_call_target="tpu_custom_call" | custom-call | tf_op jit(solution)/shard_map/step/pallas_call | solution.py:331
  128.7 3.9 %all-to-all-start.6 = ((f32[32,1,1280]{2,1,0:T(1,128)}), f32[32,1,1280]{2,1,0:T(1,128)S(1)}, u32[]{:S(2)}, u32[]{:S(2)}) async-start(f32[32,1,1280]{2,1,0:T(1,128)} %get-tuple-element.31), calls=%async_computation.6 | async-start | bytes 327680 | tf_op jit(solution)/shard_map/all_to_all | solution.py:287
  135.0 2.0 %collective-permute-start.6 = (f32[1,640]{1,0:T(1,128)S(1)}, f32[1,640]{1,0:T(1,128)S(1)}, u32[]{:S(2)}, u32[]{:S(2)}) collective-permute-start(f32[1,640]{1,0:T(1,128)S(1)} %get-tuple-element.33.refs_7_), channel_id=1, source_target_pairs={{1,0},{2,1},{3,2},{0,3},{5,4},{6,5},{7,6},{4,7},{9,8},{10,9},{11,1... | collective-permute-start | bytes 7688 | tf_op jit(solution)/shard_map/ppermute | solution.py:346
  137.8 2.9 %all-to-all-done.6.refs_1_ = f32[32,1,1280]{2,1,0:T(1,128)S(1)} async-done(((f32[32,1,1280]{2,1,0:T(1,128)}), f32[32,1,1280]{2,1,0:T(1,128)S(1)}, u32[]{:S(2)}, u32[]{:S(2)}) %all-to-all-start.6) | async-done | bytes 163872 | tf_op jit(solution)/shard_map/all_to_all | solution.py:287
  140.7 2.1 %step.10 = (f32[4,640]{1,0:T(4,128)S(1)}, f32[32,1,640]{2,1,0:T(1,128)}, f32[1,640]{1,0:T(1,128)S(1)}) custom-call(s32[16]{0:T(128)S(1)} %get-tuple-element.20.ids_ref.refs_0_, f32[32,1,1280]{2,1,0:T(1,128)S(1)} %all-to-all-done.6.refs_1_, f32[4,640]{1,0:T(4,128)S(1)} %get-tuple-element.32.refs_2_, bf16[4,144,576]{2,1,0:T(8,128)(2,1)S(1)} %bitcast.18, ...), custom_call_target="tpu_custom_call" | custom-call | tf_op jit(solution)/shard_map/step/pallas_call | solution.py:331
  142.8 6.0 %all-to-all-start.7 = ((f32[32,1,640]{2,1,0:T(1,128)}), f32[32,1,640]{2,1,0:T(1,128)S(1)}, u32[]{:S(2)}, u32[]{:S(2)}) async-start(f32[32,1,640]{2,1,0:T(1,128)} %get-tuple-element.34), calls=%async_computation.7 | async-start | bytes 163840 | tf_op jit(solution)/shard_map/all_to_all | solution.py:287
  149.7 3.5 %collective-permute-start.10 = (f32[1,640]{1,0:T(1,128)S(1)}, f32[1,640]{1,0:T(1,128)S(1)}, u32[]{:S(2)}, u32[]{:S(2)}) collective-permute-start(f32[1,640]{1,0:T(1,128)S(1)} %get-tuple-element.36.refs_7_), channel_id=1, source_target_pairs={{2,0},{3,1},{0,2},{1,3},{6,4},{7,5},{4,6},{5,7},{10,8},{11,9},{8,1... | collective-permute-start | bytes 7688 | tf_op jit(solution)/shard_map/ppermute | solution.py:346
  156.1 2.1 %step.11 = f32[1,144]{1,0:T(1,128)} custom-call(s32[16]{0:T(128)S(1)} %get-tuple-element.20.ids_ref.refs_0_, f32[32,1,640]{2,1,0:T(1,128)S(1)} %all-to-all-done.7.refs_1_, f32[4,640]{1,0:T(4,128)S(1)} %get-tuple-element.35.refs_2_, bf16[4,144,576]{2,1,0:T(8,128)(2,1)S(1)} %bitcast.19, bf16[4,144,576]{2,1,0:T(8,128)(2,1)S(1)} %copy-done.17, ...), custom_call_target="tpu_custom_call" | custom-call | tf_op jit(solution)/shard_map/step/pallas_call | solution.py:331
  (130 shorter events, 44.4 us)
Async XLA Ops:
  0.6 36.7 %copy-start.51 = (f32[1,144]{1,0:T(1,128)S(1)}, f32[1,144]{1,0:T(1,128)}, u32[]{:S(2)}) copy-start(f32[1,144]{1,0:T(1,128)} %diag_ref.1) | copy-start | bytes 1732
  0.6 44.4 %collective-permute-start.2 = (bf16[4,144,576]{2,1,0:T(8,128)(2,1)}, bf16[4,144,576]{2,1,0:T(8,128)(2,1)S(1)}, u32[]{:S(2)}, u32[]{:S(2)}) collective-permute-start(bf16[4,144,576]{2,1,0:T(8,128)(2,1)} %bitcast.10), channel_id=1, source_target_pairs={{3,0},{0,1},{1,2},{2,3},{7,4},{4,5},{5,6},{6,7},{11,8},{8,9},{9,10... | collective-permute-start | bytes 1990664 | tf_op jit(solution)/shard_map/ppermute | solution.py:266
  2.8 42.2 %collective-permute-start.1 = (bf16[4,144,576]{2,1,0:T(8,128)(2,1)}, bf16[4,144,576]{2,1,0:T(8,128)(2,1)S(1)}, u32[]{:S(2)}, u32[]{:S(2)}) collective-permute-start(bf16[4,144,576]{2,1,0:T(8,128)(2,1)} %bitcast.11), channel_id=1, source_target_pairs={{2,0},{3,1},{0,2},{1,3},{6,4},{7,5},{4,6},{5,7},{10,8},{11,9},{8,1... | collective-permute-start | bytes 1990664 | tf_op jit(solution)/shard_map/ppermute | solution.py:266
  5.2 39.8 %collective-permute-start = (bf16[4,144,576]{2,1,0:T(8,128)(2,1)}, bf16[4,144,576]{2,1,0:T(8,128)(2,1)S(1)}, u32[]{:S(2)}, u32[]{:S(2)}) collective-permute-start(bf16[4,144,576]{2,1,0:T(8,128)(2,1)} %bitcast.12), channel_id=1, source_target_pairs={{1,0},{2,1},{3,2},{0,3},{5,4},{6,5},{7,6},{4,7},{9,8},{10,9},{11,1... | collective-permute-start | bytes 1990664 | tf_op jit(solution)/shard_map/ppermute | solution.py:266
  14.0 31.1 %copy-start.2 = (bf16[1,4,576,144]{2,3,1,0:T(8,128)(2,1)S(1)}, bf16[1,4,576,144]{2,3,1,0:T(8,128)(2,1)}, u32[]{:S(2)}) copy-start(bf16[1,4,576,144]{2,3,1,0:T(8,128)(2,1)} %param.19) | copy-start | bytes 1990660
  14.0 45.1 %copy-start.1 = (bf16[1024,1728]{0,1:T(8,128)(2,1)S(1)}, bf16[1024,1728]{0,1:T(8,128)(2,1)}, u32[]{:S(2)}) copy-start(bf16[1024,1728]{0,1:T(8,128)(2,1)} %param.13) | copy-start | bytes 10616836
  14.0 45.1 %copy-start.21 = (f32[3,3,1024]{2,1,0:T(4,128)S(1)}, f32[3,3,1024]{2,1,0:T(4,128)}, u32[]{:S(2)}) copy-start(f32[3,3,1024]{2,1,0:T(4,128)} %info_ref.7) | copy-start | bytes 110596
  14.0 45.1 %copy-start.31 = (s32[1024,1]{0,1:T(1,128)S(1)}, s32[1024,1]{0,1:T(1,128)}, u32[]{:S(2)}) copy-start(s32[1024,1]{0,1:T(1,128)} %param.11) | copy-start | bytes 12292
  14.0 45.1 %copy-start.33 = (s32[1024]{0:T(1024)S(1)}, s32[1024]{0:T(1024)}, u32[]{:S(2)}) copy-start(s32[1024]{0:T(1024)} %param.12) | copy-start | bytes 12292
  45.0 29.1 %copy-start.6 = (bf16[4,144,576]{2,1,0:T(8,128)(2,1)}, bf16[4,144,576]{2,1,0:T(8,128)(2,1)S(1)}, u32[]{:S(2)}) copy-start(bf16[4,144,576]{2,1,0:T(8,128)(2,1)S(1)} %collective-permute-done.2.b3.refs_6_) | copy-start | bytes 1990660
  45.0 29.1 %copy-start.10 = (bf16[4,144,576]{2,1,0:T(8,128)(2,1)}, bf16[4,144,576]{2,1,0:T(8,128)(2,1)S(1)}, u32[]{:S(2)}) copy-start(bf16[4,144,576]{2,1,0:T(8,128)(2,1)S(1)} %collective-permute-done.1.b2.refs_5_) | copy-start | bytes 1990660
  76.8 13.6 %all-to-all-start.4 = ((f32[32,1,640]{2,1,0:T(1,128)}), f32[32,1,640]{2,1,0:T(1,128)}, u32[]{:S(2)}, u32[]{:S(2)}) async-start(f32[32,1,640]{2,1,0:T(1,128)} %copy-done.29), calls=%async_computation.4 | async-start | bytes 163840 | tf_op jit(solution)/shard_map/all_to_all | solution.py:287
  81.3 7.3 %collective-permute-start.5 = (f32[1,640]{1,0:T(1,128)S(1)}, f32[1,640]{1,0:T(1,128)S(1)}, u32[]{:S(2)}, u32[]{:S(2)}) collective-permute-start(f32[1,640]{1,0:T(1,128)S(1)} %get-tuple-element.28.refs_7_), channel_id=1, source_target_pairs={{3,0},{0,1},{1,2},{2,3},{7,4},{4,5},{5,6},{6,7},{11,8},{8,9},{9,10... | collective-permute-start | bytes 7688 | tf_op jit(solution)/shard_map/ppermute | solution.py:346
  81.7 7.5 %collective-permute-start.4 = (f32[1,640]{1,0:T(1,128)S(1)}, f32[1,640]{1,0:T(1,128)S(1)}, u32[]{:S(2)}, u32[]{:S(2)}) collective-permute-start(f32[1,640]{1,0:T(1,128)S(1)} %get-tuple-element.28.refs_7_), channel_id=1, source_target_pairs={{2,0},{3,1},{0,2},{1,3},{6,4},{7,5},{4,6},{5,7},{10,8},{11,9},{8,1... | collective-permute-start | bytes 7688 | tf_op jit(solution)/shard_map/ppermute | solution.py:346
  83.4 6.3 %collective-permute-start.3 = (f32[1,640]{1,0:T(1,128)S(1)}, f32[1,640]{1,0:T(1,128)S(1)}, u32[]{:S(2)}, u32[]{:S(2)}) collective-permute-start(f32[1,640]{1,0:T(1,128)S(1)} %get-tuple-element.28.refs_7_), channel_id=1, source_target_pairs={{1,0},{2,1},{3,2},{0,3},{5,4},{6,5},{7,6},{4,7},{9,8},{10,9},{11,1... | collective-permute-start | bytes 7688 | tf_op jit(solution)/shard_map/ppermute | solution.py:346
  101.5 16.4 %all-to-all-start.5 = ((f32[32,1,1280]{2,1,0:T(1,128)}), f32[32,1,1280]{2,1,0:T(1,128)}, u32[]{:S(2)}, u32[]{:S(2)}) async-start(f32[32,1,1280]{2,1,0:T(1,128)} %copy-done.28), calls=%async_computation.5 | async-start | bytes 327680 | tf_op jit(solution)/shard_map/all_to_all | solution.py:287
  128.7 12.0 %all-to-all-start.6 = ((f32[32,1,1280]{2,1,0:T(1,128)}), f32[32,1,1280]{2,1,0:T(1,128)S(1)}, u32[]{:S(2)}, u32[]{:S(2)}) async-start(f32[32,1,1280]{2,1,0:T(1,128)} %get-tuple-element.31), calls=%async_computation.6 | async-start | bytes 327680 | tf_op jit(solution)/shard_map/all_to_all | solution.py:287
  132.6 4.4 %collective-permute-start.8 = (f32[1,640]{1,0:T(1,128)S(1)}, f32[1,640]{1,0:T(1,128)S(1)}, u32[]{:S(2)}, u32[]{:S(2)}) collective-permute-start(f32[1,640]{1,0:T(1,128)S(1)} %get-tuple-element.33.refs_7_), channel_id=1, source_target_pairs={{3,0},{0,1},{1,2},{2,3},{7,4},{4,5},{5,6},{6,7},{11,8},{8,9},{9,10... | collective-permute-start | bytes 7688 | tf_op jit(solution)/shard_map/ppermute | solution.py:346
  133.4 4.2 %collective-permute-start.7 = (f32[1,640]{1,0:T(1,128)S(1)}, f32[1,640]{1,0:T(1,128)S(1)}, u32[]{:S(2)}, u32[]{:S(2)}) collective-permute-start(f32[1,640]{1,0:T(1,128)S(1)} %get-tuple-element.33.refs_7_), channel_id=1, source_target_pairs={{2,0},{3,1},{0,2},{1,3},{6,4},{7,5},{4,6},{5,7},{10,8},{11,9},{8,1... | collective-permute-start | bytes 7688 | tf_op jit(solution)/shard_map/ppermute | solution.py:346
  135.0 2.7 %collective-permute-start.6 = (f32[1,640]{1,0:T(1,128)S(1)}, f32[1,640]{1,0:T(1,128)S(1)}, u32[]{:S(2)}, u32[]{:S(2)}) collective-permute-start(f32[1,640]{1,0:T(1,128)S(1)} %get-tuple-element.33.refs_7_), channel_id=1, source_target_pairs={{1,0},{2,1},{3,2},{0,3},{5,4},{6,5},{7,6},{4,7},{9,8},{10,9},{11,1... | collective-permute-start | bytes 7688 | tf_op jit(solution)/shard_map/ppermute | solution.py:346
  142.8 13.4 %all-to-all-start.7 = ((f32[32,1,640]{2,1,0:T(1,128)}), f32[32,1,640]{2,1,0:T(1,128)S(1)}, u32[]{:S(2)}, u32[]{:S(2)}) async-start(f32[32,1,640]{2,1,0:T(1,128)} %get-tuple-element.34), calls=%async_computation.7 | async-start | bytes 163840 | tf_op jit(solution)/shard_map/all_to_all | solution.py:287
  148.7 4.6 %collective-permute-start.11 = (f32[1,640]{1,0:T(1,128)S(1)}, f32[1,640]{1,0:T(1,128)S(1)}, u32[]{:S(2)}, u32[]{:S(2)}) collective-permute-start(f32[1,640]{1,0:T(1,128)S(1)} %get-tuple-element.36.refs_7_), channel_id=1, source_target_pairs={{3,0},{0,1},{1,2},{2,3},{7,4},{4,5},{5,6},{6,7},{11,8},{8,9},{9,10... | collective-permute-start | bytes 7688 | tf_op jit(solution)/shard_map/ppermute | solution.py:346
  149.7 4.8 %collective-permute-start.10 = (f32[1,640]{1,0:T(1,128)S(1)}, f32[1,640]{1,0:T(1,128)S(1)}, u32[]{:S(2)}, u32[]{:S(2)}) collective-permute-start(f32[1,640]{1,0:T(1,128)S(1)} %get-tuple-element.36.refs_7_), channel_id=1, source_target_pairs={{2,0},{3,1},{0,2},{1,3},{6,4},{7,5},{4,6},{5,7},{10,8},{11,9},{8,1... | collective-permute-start | bytes 7688 | tf_op jit(solution)/shard_map/ppermute | solution.py:346
  153.2 2.7 %collective-permute-start.9 = (f32[1,640]{1,0:T(1,128)S(1)}, f32[1,640]{1,0:T(1,128)S(1)}, u32[]{:S(2)}, u32[]{:S(2)}) collective-permute-start(f32[1,640]{1,0:T(1,128)S(1)} %get-tuple-element.36.refs_7_), channel_id=1, source_target_pairs={{1,0},{2,1},{3,2},{0,3},{5,4},{6,5},{7,6},{4,7},{9,8},{10,9},{11,1... | collective-permute-start | bytes 7688 | tf_op jit(solution)/shard_map/ppermute | solution.py:346
  (45 other events, 120.9 us)

commit v2 on v1

--- a/solution.py
+++ b/solution.py
@@ -174,54 +174,54 @@
     state_ref[1:2, :] = rhs
     state_ref[2:3, :] = step
     state_ref[3:4, :] = diag
+    state_ref[4:8, :] = jnp.zeros((4, WIDE), F32)
     rhs_ref[...] = take_share(rhs, col)
     for c in range(CLUSTERS):
         out_ref[c] = x
 
 
-def step_kernel(colour, sweep, n_elim, has_send, has_recv, last, *refs):
-    refs = list(refs)
+def step_kernel(number, has_send, has_recv, *refs):
     ids_ref, recv_ref, state_ref = refs[:3]
     blocks = refs[3:7]
-    at = 7
-    elim = jnp.zeros((1, WIDE), F32)
-    for _ in range(n_elim):
-        elim = elim + refs[at][...]
-        at += 1
-    if has_send:
-        send_ref = refs[at]
-        at += 1
-    if last:
-        share_ref = refs[at]
-        at += 1
-    else:
-        new_ref, out_ref = refs[at : at + 2]
-        at += 2
-        if has_recv:
-            sum_ref = refs[at]
-            at += 1
-    columns = refs[at]
+    send_ref = refs[7] if has_send else None
+    new_ref, out_ref, columns = refs[-3:]
     near = [recv_ref[ids_ref[PARTNER + r], :, :WIDE] for r in range(ROUNDS)]
     coupled = couple(ids_ref, near, blocks, columns)
-    x, rhs, step, diag = (state_ref[i : i + 1, :] for i in range(4))
-    resid = rhs - coupled
-    if sweep:
-        resid = resid - diag * x + elim
-    x = jnp.where(ids_ref[MY_COLOUR] == colour, x + step * resid, x)
-    if last:
-        share_ref[...] = take_share(x, ids_ref[MY_COL])
-        return
-    new_ref[0:1, :] = x
-    new_ref[1:4, :] = state_ref[1:4, :]
-    for c in range(CLUSTERS):
-        out_ref[c, :, :WIDE] = x
-    if has_send:
-        out_ref[:, :, WIDE:] = send_ref[...]
+    x, rhs, step, diag, elim = (state_ref[i : i + 1, :] for i in range(5))
+    mine = ids_ref[MY_COLOUR]
     if has_recv:
         total = recv_ref[0, :, WIDE:]
         for c in range(1, CLUSTERS):
             total = total + recv_ref[c, :, WIDE:]
-        sum_ref[...] = total
+        elim = jnp.where(mine >= (2 if number > COLOURS else 0), total, elim)
+    if number == COLOURS:
+        x, rhs, coupled = 0.25 * x, 0.25 * rhs, 0.25 * coupled
+    resid = rhs - coupled
+    if number >= COLOURS:
+        resid = resid - diag * x + elim
+    x = jnp.where(mine == number % COLOURS, x + step * resid, x)
+    for i, v in enumerate((x, rhs, step, diag, elim)):
+        new_ref[i : i + 1, :] = v
+    if number == 2 * COLOURS - 2:
+        x = jnp.where(mine == COLOURS - 1, x + step * (rhs - diag * x + elim), x)
+    for c in range(out_ref.shape[0]):
+        out_ref[c, :, :WIDE] = x
+    if has_send:
+        out_ref[:, :, WIDE:] = send_ref[...]
+
+
+def last_step_kernel(ids_ref, recv_ref, state_ref, b0, b1, b2, b3, out_ref, columns):
+    def total(c):
+        v = recv_ref[COLS * c]
+        for k in range(1, COLS):
+            v = v + recv_ref[COLS * c + k]
+        return v
+
+    near = [total(ids_ref[PARTNER + r]) for r in range(ROUNDS)]
+    coupled = couple(ids_ref, near, (b0, b1, b2, b3), columns)
+    x = total(ids_ref[MY_CLU])
+    x = jnp.where(ids_ref[MY_COLOUR] == COLOURS - 1, x - state_ref[2:3, :] * coupled, x)
+    out_ref[...] = take_share(x, ids_ref[MY_COL])
 
 
 def elim_kernel(dest_ref, obs_ref, info_ref, recv_ref, jac_ref, out_ref):
@@ -279,7 +279,7 @@
         out_specs=[whole(CLUSTERS, 1, 5 * WIDE + SLOT), smem()],
         out_shape=[shape(CLUSTERS, 1, 5 * WIDE + SLOT), shape(16, dtype=jnp.int32)],
         scratch_shapes=[pltpu.VMEM((CLUSTERS, WIDE), F32)],
-        compiler_params=limit,
+        compiler_params=pltpu.CompilerParams(vmem_limit_bytes=56 << 20),
         name="rhs",
     )(cluster_colour, round_partner, dest, obs, point_info, point_grad, jac, camera_grad, step_scale)
 
@@ -301,7 +301,7 @@
         first_step_kernel,
         in_specs=[smem()] + [vmem()] * 5,
         out_specs=[vmem()] * 3,
-        out_shape=[shape(4, WIDE), shape(CLUSTERS, 1, WIDE), shape(1, SHARE)],
+        out_shape=[shape(8, WIDE), shape(CLUSTERS, 1, WIDE), shape(1, SHARE)],
         scratch_shapes=[columns],
         compiler_params=limit,
         name="first_step",
@@ -320,50 +320,38 @@
             name="elim",
         )(dest, obs, point_info, recv, jac)
 
-    def update(number, recv, state, elim=(), send=None, has_recv=False):
-        last = number == 7
-        outs = [shape(1, SHARE)]
-        if not last:
-            outs = [shape(4, WIDE), shape(CLUSTERS, 1, WIDE if send is None else 2 * WIDE)]
-            if has_recv:
-                outs.append(shape(1, WIDE))
-        extra = list(elim) + ([] if send is None else [send])
+    def update(number, recv, state, send=None, has_recv=False):
+        rows = CLUSTERS * COLS if number == 2 * COLOURS - 2 else CLUSTERS
         return pl.pallas_call(
-            functools.partial(
-                step_kernel, number % COLOURS, number // COLOURS, len(elim),
-                send is not None, has_recv, last,
-            ),
-            in_specs=[smem()] + [vmem()] * (6 + len(extra)),
-            out_specs=[vmem()] * len(outs),
-            out_shape=outs,
+            functools.partial(step_kernel, number, send is not None, has_recv),
+            in_specs=[smem()] + [vmem()] * (6 if send is None else 7),
+            out_specs=[vmem()] * 2,
+            out_shape=[shape(8, WIDE), shape(rows, 1, WIDE if send is None else 2 * WIDE)],
             scratch_shapes=[columns],
             compiler_params=limit,
             name="step",
-        )(ids, recv, state, *blocks, *extra)
-
-    def over_col(v):
-        return [v] + [
-            lax.ppermute(v, "col", [((i + k) % COLS, i) for i in range(COLS)]) for k in (1, 2, 3)
-        ]
-
-    recv = over_clu(payload)
-    first = eliminate(recv)
-    state, payload = update(2, recv, state, send=first)
-    recv = over_clu(payload)
-    state, payload, part = update(3, recv, state, has_recv=True)
-    elim_early = over_col(part)
-    second = eliminate(recv)
-    recv = over_clu(payload)
-    state, payload = update(4, recv, state, elim=elim_early, send=second)
-    third = eliminate(recv)
-    recv = over_clu(payload)
-    state, payload, part = update(5, recv, state, elim=elim_early, send=third, has_recv=True)
-    elim_second = over_col(part)
-    recv = over_clu(payload)
-    state, payload, part = update(6, recv, state, elim=elim_second, has_recv=True)
-    elim_third = over_col(part)
-    recv = over_clu(payload)
-    (solution,) = update(7, recv, state, elim=elim_third)
+        )(ids, recv, state, *blocks, *(() if send is None else (send,)))
+
+    recv = over_clu(payload)
+    state, payload = update(2, recv, state, send=eliminate(recv))
+    recv = over_clu(payload)
+    state, payload = update(3, recv, state, has_recv=True)
+    recv = over_clu(payload)
+    state, payload = update(4, recv, state, send=eliminate(recv))
+    recv = over_clu(payload)
+    state, payload = update(5, recv, state, has_recv=True)
+    recv = over_clu(payload)
+    state, payload = update(6, recv, state)
+    recv = lax.all_to_all(payload, ("clu", "col"), split_axis=0, concat_axis=0, tiled=True)
+    solution = pl.pallas_call(
+        last_step_kernel,
+        in_specs=[smem()] + [vmem()] * 6,
+        out_specs=vmem(),
+        out_shape=shape(1, SHARE),
+        scratch_shapes=[columns],
+        compiler_params=limit,
+        name="last_step",
+    )(ids, recv, state, *blocks)
     return solution, reduced_rhs
 
 

time: 160 us -> 133 us (0.83)
  blocking collectives: 50.5 us -> 104 us
  starting transfers between devices: 40.2 us -> 5.71 us
  local copies, waits for them, and re-layouts: 31.8 us -> 0.68 us
  waiting for transfers between devices: 10.3 us -> 0.01 us
  Pallas kernels: 24.5 us -> 21.1 us
    all_to_all x3 -> x6, blocking collectives: 43.5 us -> 80.3 us  [over_clu(): return lax.all_to_all(v, 'clu', split_axis=0, concat_axis=0, tiled=True)]
    unnamed x106 -> x14, local copies, waits for them, and re-layouts: 31.8 us -> 0.68 us
    all_to_all x4 -> x0, starting transfers between devices: 22.7 us -> none  [over_clu(): return lax.all_to_all(v, 'clu', split_axis=0, concat_axis=0, tiled=True)]
    all_to_all x0 -> x1, blocking collectives: none -> 16.8 us  [per_device(): lax.all_to_all(payload, ('clu', 'col'), split_axis=0, concat_axis=0, tile...]
    ppermute x9 -> x0, starting transfers between devices: 11.7 us -> none  [over_col(): lax.ppermute(v, 'col', [((i + k) % COLS, i) for i in range(COLS)])]
    all_to_all x4 -> x0, waiting for transfers between devices: 6.76 us -> none  [over_clu(): return lax.all_to_all(v, 'clu', split_axis=0, concat_axis=0, tiled=True)]
    ppermute x9 -> x0, waiting for transfers between devices: 3.5 us -> none  [over_col(): lax.ppermute(v, 'col', [((i + k) % COLS, i) for i in range(COLS)])]
    pallas_call x3 -> x2, Pallas kernels: 7.17 us -> 4.2 us  [eliminate(): pl.pallas_call(elim_kernel, in_specs=[vmem()] * 5, out_specs=vmem(), out_...]
  transfers between devices with their start and end apart: 16 -> 3, of which waited for: 8 -> 0; matrix products, arithmetic and copies ran while one was open for 0% -> 0% of each run, Pallas kernels for 6% -> 4%
where the time goes in v2:
time: 133 us; the launch traced here: 132 us
  blocking collectives  104 us (78%)
  Pallas kernels  21.1 us (16%)
  starting transfers between devices  5.71 us (4%)
    all_to_all x6, blocking collectives, over_clu(): return lax.all_to_all(v, 'clu', split_axis=0, concat_axis=0, tiled=True)  80.3 us
    all_to_all x1, blocking collectives, per_device(): lax.all_to_all(payload, ('clu', 'col'), split_axis=0, concat_axis=0, tile...  16.8 us
    pallas_call x5, Pallas kernels, update(): pl.pallas_call(functools.partial(step_kernel, number, send is not None, h...  7.2 us
    all_to_all x1, blocking collectives, per_device(): lax.all_to_all(payload, 'col', split_axis=0, concat_axis=0, tiled=True)  7.01 us
    ppermute x3, starting transfers between devices, per_device(): lax.ppermute(own, 'col', [((i + k) % COLS, i) for i in range(COLS)])  5.71 us
    pallas_call x1, Pallas kernels, per_device(): pl.pallas_call(rhs_kernel, grid=(3,), in_specs=[smem(), smem(), whole(1,...  4.91 us
    pallas_call x2, Pallas kernels, eliminate(): pl.pallas_call(elim_kernel, in_specs=[vmem()] * 5, out_specs=vmem(), out_...  4.2 us
  transfers between devices with their start and end apart: 3, of which 0 were waited for; matrix products, arithmetic and copies ran while one was open for 0% of the time, Pallas kernels for 4%

profile of v2, /device:TPU:1, one launch (start us, length us, event | category | flops | bytes accessed | tf_op | source)
XLA Modules:
  0.0 132.4 jit_solution(13688382712644330202)
XLA Ops:
  0.7 2.1 %collective-permute-start.2 = (bf16[4,144,576]{2,1,0:T(8,128)(2,1)}, bf16[4,144,576]{2,1,0:T(8,128)(2,1)S(1)}, u32[]{:S(2)}, u32[]{:S(2)}) collective-permute-start(bf16[4,144,576]{2,1,0:T(8,128)(2,1)} %bitcast.6), channel_id=1, source_target_pairs={{3,0},{0,1},{1,2},{2,3},{7,4},{4,5},{5,6},{6,7},{11,8},{8,9},{9,10... | collective-permute-start | bytes 1990664 | tf_op jit(solution)/shard_map/ppermute | solution.py:266
  2.8 2.5 %collective-permute-start.1 = (bf16[4,144,576]{2,1,0:T(8,128)(2,1)}, bf16[4,144,576]{2,1,0:T(8,128)(2,1)S(1)}, u32[]{:S(2)}, u32[]{:S(2)}) collective-permute-start(bf16[4,144,576]{2,1,0:T(8,128)(2,1)} %bitcast.7), channel_id=1, source_target_pairs={{2,0},{3,1},{0,2},{1,3},{6,4},{7,5},{4,6},{5,7},{10,8},{11,9},{8,1... | collective-permute-start | bytes 1990664 | tf_op jit(solution)/shard_map/ppermute | solution.py:266
  5.2 1.2 collective-permute-start
  6.4 4.9 %rhs.1 = (f32[32,1,3456]{2,1,0:T(1,128)}, s32[16]{0:T(128)}) custom-call(s32[32]{0:T(128)} %cc_ref.1, s32[4,4,32]{2,1,0:T(4,128)} %rp_ref.1, s32[1,1024]{1,0:T(1,128)} %bitcast.19, s32[1,1024]{1,0:T(1,128)} %bitcast.22, f32[3,3,1024]{2,1,0:T(4,128)} %info_ref.5, f32[3,1024]{1,0:T(4,128)} %grad_ref.1, bf16[1728,1024]{1,0:T(8,128)(2,1)} %bitcast.16, ...), custom_call_target="tpu_custom_call" | custom-call | tf_op jit(solution)/shard_map/rhs/pallas_call | solution.py:271
  11.3 20.4 %all_to_all.40.recv_ref = f32[32,1,3456]{2,1,0:T(1,128)S(1)} all-to-all(f32[32,1,3456]{2,1,0:T(1,128)} %get-tuple-element.18), channel_id=1, replica_groups=mesh['clu'=32,'col'=4] {'clu'}, dimensions={0} | all-to-all | bytes 884736 | tf_op jit(solution)/shard_map/all_to_all | solution.py:287
  31.7 0.7 copy-done.5
  32.4 0.6 gather.1
  33.0 7.0 %all_to_all.41.recv_ref = f32[4,1,4736]{2,1,0:T(1,128)S(1)} all-to-all(f32[4,1,4736]{2,1,0:T(1,128)S(1)} %gather.1), channel_id=1, replica_groups=mesh['clu'=32,'col'=4] {'col'}, dimensions={0} | all-to-all | bytes 151552 | tf_op jit(solution)/shard_map/all_to_all | solution.py:298
  40.0 0.0 collective-permute-done.1.b2.refs_5_
  40.0 2.2 %first_step.1 = (f32[8,640]{1,0:T(8,128)S(1)}, f32[32,1,640]{2,1,0:T(1,128)S(1)}, f32[1,144]{1,0:T(1,128)}) custom-call(s32[16]{0:T(128)S(1)} %copy-done.5, f32[4,1,4736]{2,1,0:T(1,128)S(1)} %all_to_all.41.recv_ref, bf16[4,144,576]{2,1,0:T(8,128)(2,1)S(1)} %bitcast.9, bf16[4,144,576]{2,1,0:T(8,128)(2,1)S(1)} %collective-permute-done.b1.refs_4_, ...), custom_call_target="tpu_custom_call" | custom-call | tf_op jit(solution)/shard_map/first_step/pallas_call | solution.py:300
  42.2 14.8 %all_to_all.42.recv_ref.refs_1_ = f32[32,1,640]{2,1,0:T(1,128)S(1)} all-to-all(f32[32,1,640]{2,1,0:T(1,128)S(1)} %get-tuple-element.19), channel_id=1, replica_groups=mesh['clu'=32,'col'=4] {'clu'}, dimensions={0} | all-to-all | bytes 163840 | tf_op jit(solution)/shard_map/all_to_all | solution.py:287
  57.0 2.1 %elim.2.refs_7_ = f32[32,1,640]{2,1,0:T(1,128)S(1)} custom-call(s32[1,1024]{1,0:T(1,128)S(1)} %bitcast.20, s32[1,1024]{1,0:T(1,128)S(1)} %bitcast.23, f32[3,3,1024]{2,1,0:T(4,128)S(1)} %copy-done.2, f32[32,1,640]{2,1,0:T(1,128)S(1)} %all_to_all.42.recv_ref.refs_1_, bf16[1728,1024]{1,0:T(8,128)(2,1)S(1)} %bitcast.17), custom_call_target="tpu_custom_call" | custom-call | flops 452984832 | bytes 4194304 | tf_op jit(solution)/shard_map/elim/pallas_call | solution.py:311
  59.1 1.4 %step.5 = (f32[8,640]{1,0:T(8,128)S(1)}, f32[32,1,1280]{2,1,0:T(1,128)S(1)}) custom-call(s32[16]{0:T(128)S(1)} %copy-done.5, f32[32,1,640]{2,1,0:T(1,128)S(1)} %all_to_all.42.recv_ref.refs_1_, f32[8,640]{1,0:T(8,128)S(1)} %get-tuple-element.20.refs_2_, bf16[4,144,576]{2,1,0:T(8,128)(2,1)S(1)} %bitcast.10, ...), custom_call_target="tpu_custom_call" | custom-call | tf_op jit(solution)/shard_map/step/pallas_call | solution.py:325
  60.6 11.5 %all_to_all.43.refs_1_ = f32[32,1,1280]{2,1,0:T(1,128)S(1)} all-to-all(f32[32,1,1280]{2,1,0:T(1,128)S(1)} %get-tuple-element.21), channel_id=1, replica_groups=mesh['clu'=32,'col'=4] {'clu'}, dimensions={0} | all-to-all | bytes 327680 | tf_op jit(solution)/shard_map/all_to_all | solution.py:287
  72.1 1.4 %step.6 = (f32[8,640]{1,0:T(8,128)S(1)}, f32[32,1,640]{2,1,0:T(1,128)S(1)}) custom-call(s32[16]{0:T(128)S(1)} %copy-done.5, f32[32,1,1280]{2,1,0:T(1,128)S(1)} %all_to_all.43.refs_1_, f32[8,640]{1,0:T(8,128)S(1)} %get-tuple-element.22.refs_2_, bf16[4,144,576]{2,1,0:T(8,128)(2,1)S(1)} %bitcast.11, bf16[4,144,576]{2,1,0:T(8,128)(2,1)S(1)} %collective-permute-done.b1.refs_4_, ...), custom_call_target="tpu_custom_call" | custom-call | tf_op jit(solution)/shard_map/step/pallas_call | solution.py:325
  73.5 11.0 %all_to_all.44.recv_ref.refs_1_ = f32[32,1,640]{2,1,0:T(1,128)S(1)} all-to-all(f32[32,1,640]{2,1,0:T(1,128)S(1)} %get-tuple-element.23), channel_id=1, replica_groups=mesh['clu'=32,'col'=4] {'clu'}, dimensions={0} | all-to-all | bytes 163840 | tf_op jit(solution)/shard_map/all_to_all | solution.py:287
  84.5 2.1 %elim.3.refs_7_ = f32[32,1,640]{2,1,0:T(1,128)S(1)} custom-call(s32[1,1024]{1,0:T(1,128)S(1)} %bitcast.21, s32[1,1024]{1,0:T(1,128)S(1)} %bitcast.24, f32[3,3,1024]{2,1,0:T(4,128)S(1)} %copy-done.2, f32[32,1,640]{2,1,0:T(1,128)S(1)} %all_to_all.44.recv_ref.refs_1_, bf16[1728,1024]{1,0:T(8,128)(2,1)S(1)} %bitcast.18), custom_call_target="tpu_custom_call" | custom-call | flops 452984832 | bytes 4194304 | tf_op jit(solution)/shard_map/elim/pallas_call | solution.py:311
  86.6 1.4 %step.7 = (f32[8,640]{1,0:T(8,128)S(1)}, f32[32,1,1280]{2,1,0:T(1,128)S(1)}) custom-call(s32[16]{0:T(128)S(1)} %copy-done.5, f32[32,1,640]{2,1,0:T(1,128)S(1)} %all_to_all.44.recv_ref.refs_1_, f32[8,640]{1,0:T(8,128)S(1)} %get-tuple-element.24.refs_2_, bf16[4,144,576]{2,1,0:T(8,128)(2,1)S(1)} %bitcast.12, ...), custom_call_target="tpu_custom_call" | custom-call | tf_op jit(solution)/shard_map/step/pallas_call | solution.py:325
  88.1 11.5 %all_to_all.45.refs_1_ = f32[32,1,1280]{2,1,0:T(1,128)S(1)} all-to-all(f32[32,1,1280]{2,1,0:T(1,128)S(1)} %get-tuple-element.25), channel_id=1, replica_groups=mesh['clu'=32,'col'=4] {'clu'}, dimensions={0} | all-to-all | bytes 327680 | tf_op jit(solution)/shard_map/all_to_all | solution.py:287
  99.6 1.4 %step.8 = (f32[8,640]{1,0:T(8,128)S(1)}, f32[32,1,640]{2,1,0:T(1,128)S(1)}) custom-call(s32[16]{0:T(128)S(1)} %copy-done.5, f32[32,1,1280]{2,1,0:T(1,128)S(1)} %all_to_all.45.refs_1_, f32[8,640]{1,0:T(8,128)S(1)} %get-tuple-element.26.refs_2_, bf16[4,144,576]{2,1,0:T(8,128)(2,1)S(1)} %bitcast.13, bf16[4,144,576]{2,1,0:T(8,128)(2,1)S(1)} %collective-permute-done.b1.refs_4_, ...), custom_call_target="tpu_custom_call" | custom-call | tf_op jit(solution)/shard_map/step/pallas_call | solution.py:325
  101.0 11.0 %all_to_all.46.refs_1_ = f32[32,1,640]{2,1,0:T(1,128)S(1)} all-to-all(f32[32,1,640]{2,1,0:T(1,128)S(1)} %get-tuple-element.27), channel_id=1, replica_groups=mesh['clu'=32,'col'=4] {'clu'}, dimensions={0} | all-to-all | bytes 163840 | tf_op jit(solution)/shard_map/all_to_all | solution.py:287
  112.0 1.5 %step.9 = (f32[8,640]{1,0:T(8,128)S(1)}, f32[128,1,640]{2,1,0:T(1,128)S(1)}) custom-call(s32[16]{0:T(128)S(1)} %copy-done.5, f32[32,1,640]{2,1,0:T(1,128)S(1)} %all_to_all.46.refs_1_, f32[8,640]{1,0:T(8,128)S(1)} %get-tuple-element.28.refs_2_, bf16[4,144,576]{2,1,0:T(8,128)(2,1)S(1)} %bitcast.14, bf16[4,144,576]{2,1,0:T(8,128)(2,1)S(1)} %collective-permute-done.b1.refs_4_, ...), custom_call_target="tpu_custom_call" | custom-call | tf_op jit(solution)/shard_map/step/pallas_call | solution.py:325
  113.5 16.8 %all_to_all.47.recv_ref = f32[128,1,640]{2,1,0:T(1,128)S(1)} all-to-all(f32[128,1,640]{2,1,0:T(1,128)S(1)} %get-tuple-element.29), channel_id=1, replica_groups=mesh['clu'=32,'col'=4] {'clu','col'}, dimensions={0} | all-to-all | bytes 655360 | tf_op jit(solution)/shard_map/all_to_all | solution.py:345
  130.3 2.1 %last_step.1 = f32[1,144]{1,0:T(1,128)} custom-call(s32[16]{0:T(128)S(1)} %copy-done.5, f32[128,1,640]{2,1,0:T(1,128)S(1)} %all_to_all.47.recv_ref, f32[8,640]{1,0:T(8,128)S(1)} %get-tuple-element.30.state_ref, bf16[4,144,576]{2,1,0:T(8,128)(2,1)S(1)} %bitcast.15, bf16[4,144,576]{2,1,0:T(8,128)(2,1)S(1)} %collective-permute-done.b1.refs_4_, ...), custom_call_target="tpu_custom_call" | custom-call | tf_op jit(solution)/shard_map/last_step/pallas_call | solution.py:346
  (15 shorter events, 0.0 us)
Async XLA Ops:
  0.6 39.4 %copy-start = (bf16[1,4,576,144]{2,3,1,0:T(8,128)(2,1)S(1)}, bf16[1,4,576,144]{2,3,1,0:T(8,128)(2,1)}, u32[]{:S(2)}) copy-start(bf16[1,4,576,144]{2,3,1,0:T(8,128)(2,1)} %param.19) | copy-start | bytes 1990660
  0.6 31.1 %copy-start.6 = (f32[1,144]{1,0:T(1,128)S(1)}, f32[1,144]{1,0:T(1,128)}, u32[]{:S(2)}) copy-start(f32[1,144]{1,0:T(1,128)} %diag_ref.1) | copy-start | bytes 1732
  0.7 39.3 %collective-permute-start.2 = (bf16[4,144,576]{2,1,0:T(8,128)(2,1)}, bf16[4,144,576]{2,1,0:T(8,128)(2,1)S(1)}, u32[]{:S(2)}, u32[]{:S(2)}) collective-permute-start(bf16[4,144,576]{2,1,0:T(8,128)(2,1)} %bitcast.6), channel_id=1, source_target_pairs={{3,0},{0,1},{1,2},{2,3},{7,4},{4,5},{5,6},{6,7},{11,8},{8,9},{9,10... | collective-permute-start | bytes 1990664 | tf_op jit(solution)/shard_map/ppermute | solution.py:266
  2.8 37.2 %collective-permute-start.1 = (bf16[4,144,576]{2,1,0:T(8,128)(2,1)}, bf16[4,144,576]{2,1,0:T(8,128)(2,1)S(1)}, u32[]{:S(2)}, u32[]{:S(2)}) collective-permute-start(bf16[4,144,576]{2,1,0:T(8,128)(2,1)} %bitcast.7), channel_id=1, source_target_pairs={{2,0},{3,1},{0,2},{1,3},{6,4},{7,5},{4,6},{5,7},{10,8},{11,9},{8,1... | collective-permute-start | bytes 1990664 | tf_op jit(solution)/shard_map/ppermute | solution.py:266
  5.2 34.8 %collective-permute-start = (bf16[4,144,576]{2,1,0:T(8,128)(2,1)}, bf16[4,144,576]{2,1,0:T(8,128)(2,1)S(1)}, u32[]{:S(2)}, u32[]{:S(2)}) collective-permute-start(bf16[4,144,576]{2,1,0:T(8,128)(2,1)} %bitcast.8), channel_id=1, source_target_pairs={{1,0},{2,1},{3,2},{0,3},{5,4},{6,5},{7,6},{4,7},{9,8},{10,9},{11,1... | collective-permute-start | bytes 1990664 | tf_op jit(solution)/shard_map/ppermute | solution.py:266
  6.4 50.6 %copy-start.1 = (bf16[1024,1728]{0,1:T(8,128)(2,1)S(1)}, bf16[1024,1728]{0,1:T(8,128)(2,1)}, u32[]{:S(2)}) copy-start(bf16[1024,1728]{0,1:T(8,128)(2,1)} %param.13) | copy-start | bytes 10616836
  6.4 50.6 %copy-start.2 = (f32[3,3,1024]{2,1,0:T(4,128)S(1)}, f32[3,3,1024]{2,1,0:T(4,128)}, u32[]{:S(2)}) copy-start(f32[3,3,1024]{2,1,0:T(4,128)} %info_ref.5) | copy-start | bytes 110596
  6.4 50.6 %copy-start.3 = (s32[1024,1]{0,1:T(1,128)S(1)}, s32[1024,1]{0,1:T(1,128)}, u32[]{:S(2)}) copy-start(s32[1024,1]{0,1:T(1,128)} %param.11) | copy-start | bytes 12292
  6.4 50.6 %copy-start.4 = (s32[1024]{0:T(1024)S(1)}, s32[1024]{0:T(1024)}, u32[]{:S(2)}) copy-start(s32[1024]{0:T(1024)} %param.12) | copy-start | bytes 12292
  31.7 0.7 copy-start.5

commit v3 on v2

--- a/solution.py
+++ b/solution.py
@@ -15,6 +15,7 @@
 SHARE = 144
 WIDE = 640
 SLOT = 256
+PAIR = 384
 TRK = 1024
 NT = (((1,), (1,)), ((), ()))
 NN = (((1,), (0,)), ((), ()))
@@ -79,7 +80,7 @@
 
 
 def rhs_kernel(
-    cc_ref, rp_ref, dest_ref, obs_ref, info_ref, grad_ref, jac_ref, cg_ref, step_ref,
+    cc_ref, rp_ref, dest_ref, obs_ref, info_ref, grad_ref, jac_ref, cg_ref, step_ref, diag_ref,
     out_ref, ids_ref, total,
 ):
     a = pl.program_id(0)
@@ -112,28 +113,26 @@
             p = rp_ref[mine, r, me]
             ids_ref[PARTNER + r] = p
             ids_ref[PARTNER_COLOUR + r] = cc_ref[p]
-        share = widen(step_ref[...], SLOT)
+        share = widen(jnp.concatenate([step_ref[...], diag_ref[...]], 1), PAIR)
         for c in range(CLUSTERS):
             colour = cc_ref[c]
             out_ref[c, :, 0:WIDE] = total[c : c + 1, :]
             for r in range(ROUNDS):
                 p = rp_ref[colour, r, c]
                 out_ref[c, :, WIDE * (r + 1) : WIDE * (r + 2)] = total[pl.ds(p, 1), :]
-            out_ref[c, :, WIDE * 5 : WIDE * 5 + SLOT] = share
-
-
-def gather_kernel(ids_ref, recv_ref, diag_ref, out_ref):
+            out_ref[c, :, WIDE * 5 :] = share
+
+
+def gather_kernel(ids_ref, recv_ref, out_ref):
     vectors = recv_ref[0, :, : WIDE * 5]
     for c in range(1, CLUSTERS):
         vectors = vectors + recv_ref[c, :, : WIDE * 5]
-    diag = widen(diag_ref[...], SLOT)
-    shares = [recv_ref[ids_ref[MY_CLU], :, WIDE * 5 :]]
-    for r in range(ROUNDS):
-        shares.append(recv_ref[ids_ref[PARTNER + r], :, WIDE * 5 :])
-    shares.append(diag)
-    row = jnp.concatenate([vectors] + shares, 1)
-    for k in range(COLS):
-        out_ref[k] = row
+    out_ref[:, : WIDE * 5] = vectors
+    sources = [ids_ref[MY_CLU]] + [ids_ref[PARTNER + r] for r in range(ROUNDS)]
+    shares = [recv_ref[c, :, WIDE * 5 : WIDE * 5 + SHARE] for c in sources]
+    shares.append(recv_ref[sources[0], :, WIDE * 5 + SHARE : WIDE * 5 + 2 * SHARE])
+    for at, share in enumerate(shares):
+        out_ref[:, WIDE * 5 + SLOT * at : WIDE * 5 + SLOT * (at + 1)] = widen(share, SLOT)
 
 
 def couple(ids_ref, vectors, blocks, columns):
@@ -141,7 +140,7 @@
     col = ids_ref[MY_COL]
     acc = jnp.zeros((16, CAM), F32)
     for k in range(COLS):
-        base = lax.rem(col + k, COLS) * SHARE
+        base = jnp.bitwise_xor(col, k) * SHARE
         for m in range(SHARE // 16):
             xs = columns[pl.ds(pl.multiple_of(base + 16 * m, 16), 16), :]
             for r in range(ROUNDS):
@@ -150,16 +149,20 @@
 
 
 def first_step_kernel(
-    ids_ref, recv_ref, b0, b1, b2, b3, state_ref, out_ref, rhs_ref, columns
+    ids_ref, v0, v1, v2, v3, b0, b1, b2, b3, state_ref, out_ref, rhs_ref, columns
 ):
     col = ids_ref[MY_COL]
-    vectors = recv_ref[0, :, : WIDE * 5]
-    for k in range(1, COLS):
-        vectors = vectors + recv_ref[k, :, : WIDE * 5]
+    rows = [v[...] for v in (v0, v1, v2, v3)]
+    vectors = (rows[0] + rows[1] + rows[2] + rows[3])[:, : WIDE * 5]
+    shares = []
+    for at in range(COLS):
+        share = jnp.zeros((1, SLOT * 6), F32)
+        for k in range(COLS):
+            share = jnp.where(jnp.bitwise_xor(col, k) == at, rows[k][:, WIDE * 5 :], share)
+        shares.append(share)
 
     def full(v):
-        at = WIDE * 5 + SLOT * v
-        return widen(jnp.concatenate([recv_ref[k, :, at : at + SHARE] for k in range(COLS)], 1))
+        return widen(jnp.concatenate([s[:, SLOT * v : SLOT * v + SHARE] for s in shares], 1))
 
     rhs = vectors[:, :WIDE]
     step, diag = full(0), full(5)
@@ -262,9 +265,12 @@
     obs = obs_count[None, :]
     jac = jnp.transpose(track_jac)
     own = jnp.transpose(covis_blocks[0], (0, 2, 1))
-    blocks = [own] + [
-        lax.ppermute(own, "col", [((i + k) % COLS, i) for i in range(COLS)]) for k in (1, 2, 3)
-    ]
+
+    def over_col(v):
+        return [v] + [lax.ppermute(v, "col", [(i, i ^ k) for i in range(COLS)]) for k in (1, 3, 2)]
+
+    own, first, third, second = over_col(own)
+    blocks = [own, first, second, third]
     limit = pltpu.CompilerParams(vmem_limit_bytes=24 << 20)
 
     whole = lambda *block: pl.BlockSpec(block, lambda a: (0,) * len(block))
@@ -275,37 +281,41 @@
             smem(), smem(), whole(1, TRK), whole(1, TRK),
             pl.BlockSpec((1, 3, TRK), lambda a: (a, 0, 0)), whole(3, TRK),
             pl.BlockSpec((CAM, TRK), lambda a: (a, 0)), whole(1, SHARE), whole(1, SHARE),
+            whole(1, SHARE),
         ],
-        out_specs=[whole(CLUSTERS, 1, 5 * WIDE + SLOT), smem()],
-        out_shape=[shape(CLUSTERS, 1, 5 * WIDE + SLOT), shape(16, dtype=jnp.int32)],
+        out_specs=[whole(CLUSTERS, 1, 5 * WIDE + PAIR), smem()],
+        out_shape=[shape(CLUSTERS, 1, 5 * WIDE + PAIR), shape(16, dtype=jnp.int32)],
         scratch_shapes=[pltpu.VMEM((CLUSTERS, WIDE), F32)],
         compiler_params=pltpu.CompilerParams(vmem_limit_bytes=56 << 20),
         name="rhs",
-    )(cluster_colour, round_partner, dest, obs, point_info, point_grad, jac, camera_grad, step_scale)
+    )(
+        cluster_colour, round_partner, dest, obs, point_info, point_grad, jac,
+        camera_grad, step_scale, camera_diag,
+    )
 
     def over_clu(v):
         return lax.all_to_all(v, "clu", split_axis=0, concat_axis=0, tiled=True)
 
     recv = over_clu(payload)
-    payload = pl.pallas_call(
+    row = pl.pallas_call(
         gather_kernel,
-        in_specs=[smem(), vmem(), vmem()],
+        in_specs=[smem(), vmem()],
         out_specs=vmem(),
-        out_shape=shape(COLS, 1, 5 * WIDE + 6 * SLOT),
+        out_shape=shape(1, 5 * WIDE + 6 * SLOT),
         compiler_params=limit,
         name="gather",
-    )(ids, recv, camera_diag)
-    recv = lax.all_to_all(payload, "col", split_axis=0, concat_axis=0, tiled=True)
+    )(ids, recv)
+    row, first, third, second = over_col(row)
     columns = pltpu.VMEM((WIDE, 8), F32)
     state, payload, reduced_rhs = pl.pallas_call(
         first_step_kernel,
-        in_specs=[smem()] + [vmem()] * 5,
+        in_specs=[smem()] + [vmem()] * 8,
         out_specs=[vmem()] * 3,
         out_shape=[shape(8, WIDE), shape(CLUSTERS, 1, WIDE), shape(1, SHARE)],
         scratch_shapes=[columns],
         compiler_params=limit,
         name="first_step",
-    )(ids, recv, *blocks)
+    )(ids, row, first, second, third, *blocks)
 
     def eliminate(recv):
         return pl.pallas_call(

time: 133 us -> 136 us (1.023)
  waiting for transfers between devices: 0.01 us -> 4.02 us
  blocking collectives: 104 us -> 101 us
  starting transfers between devices: 5.71 us -> 7.35 us
    all_to_all x1 -> x0, blocking collectives: 7.01 us -> none  [per_device(): lax.all_to_all(payload, 'col', split_axis=0, concat_axis=0, tiled=True)]
    ppermute x3 -> x6, waiting for transfers between devices: 0.01 us -> 4.02 us  [over_col(): lax.ppermute(v, 'col', [(i, i ^ k) for i in range(COLS)])]
    all_to_all x6, blocking collectives: 80.3 us -> 83.9 us  [over_clu(): return lax.all_to_all(v, 'clu', split_axis=0, concat_axis=0, tiled=True)]
    ppermute x3 -> x6, starting transfers between devices: 5.71 us -> 7.35 us  [over_col(): lax.ppermute(v, 'col', [(i, i ^ k) for i in range(COLS)])]
  transfers between devices with their start and end apart: 3 -> 6, of which waited for: 0 -> 3; matrix products, arithmetic and copies ran while one was open for 0% -> 0% of each run, Pallas kernels for 4% -> 4%
where the time goes in v3:
time: 136 us; the launch traced here: 135 us
  blocking collectives  101 us (74%)
  Pallas kernels  21.3 us (16%)
  starting transfers between devices  7.35 us (5%)
  waiting for transfers between devices  4.02 us (3%)
    all_to_all x6, blocking collectives, over_clu(): return lax.all_to_all(v, 'clu', split_axis=0, concat_axis=0, tiled=True)  83.9 us
    all_to_all x1, blocking collectives, per_device(): lax.all_to_all(payload, ('clu', 'col'), split_axis=0, concat_axis=0, tile...  17.4 us
    ppermute x6, starting transfers between devices, over_col(): lax.ppermute(v, 'col', [(i, i ^ k) for i in range(COLS)])  7.35 us
    pallas_call x5, Pallas kernels, update(): pl.pallas_call(functools.partial(step_kernel, number, send is not None, h...  7.29 us
    pallas_call x1, Pallas kernels, per_device(): pl.pallas_call(rhs_kernel, grid=(3,), in_specs=[smem(), smem(), whole(1,...  4.93 us
    pallas_call x2, Pallas kernels, eliminate(): pl.pallas_call(elim_kernel, in_specs=[vmem()] * 5, out_specs=vmem(), out_...  4.2 us
    ppermute x6, waiting for transfers between devices, over_col(): lax.ppermute(v, 'col', [(i, i ^ k) for i in range(COLS)])  4.02 us
  transfers between devices with their start and end apart: 6, of which 3 were waited for; matrix products, arithmetic and copies ran while one was open for 0% of the time, Pallas kernels for 4%

profile of v3, /device:TPU:1, one launch (start us, length us, event | category | flops | bytes accessed | tf_op | source)
XLA Modules:
  0.0 135.3 jit_solution(9593096163652891284)
XLA Ops:
  0.6 3.4 %collective-permute-start.5 = (bf16[4,144,576]{2,1,0:T(8,128)(2,1)}, bf16[4,144,576]{2,1,0:T(8,128)(2,1)S(1)}, u32[]{:S(2)}, u32[]{:S(2)}) collective-permute-start(bf16[4,144,576]{2,1,0:T(8,128)(2,1)} %bitcast.6), channel_id=1, source_target_pairs={{0,3},{1,2},{2,1},{3,0},{4,7},{5,6},{6,5},{7,4},{8,11},{9,10},{10,... | collective-permute-start | bytes 1990664 | tf_op jit(solution)/shard_map/ppermute | solution.py:270
  4.7 4.9 %rhs.1 = (f32[32,1,3584]{2,1,0:T(1,128)}, s32[16]{0:T(128)}) custom-call(s32[32]{0:T(128)} %cc_ref.1, s32[4,4,32]{2,1,0:T(4,128)} %rp_ref.1, s32[1,1024]{1,0:T(1,128)} %bitcast.19, s32[1,1024]{1,0:T(1,128)} %bitcast.22, f32[3,3,1024]{2,1,0:T(4,128)} %info_ref.5, f32[3,1024]{1,0:T(4,128)} %grad_ref.1, bf16[1728,1024]{1,0:T(8,128)(2,1)} %bitcast.16, ...), custom_call_target="tpu_custom_call" | custom-call | tf_op jit(solution)/shard_map/rhs/pallas_call | solution.py:277
  9.7 20.7 %all_to_all.35.recv_ref = f32[32,1,3584]{2,1,0:T(1,128)S(1)} all-to-all(f32[32,1,3584]{2,1,0:T(1,128)} %get-tuple-element.18), channel_id=1, replica_groups=mesh['clu'=32,'col'=4] {'clu'}, dimensions={0} | all-to-all | bytes 917504 | tf_op jit(solution)/shard_map/all_to_all | solution.py:297
  30.3 0.7 copy-done.5
  31.0 0.6 gather.1.v0
  31.6 2.5 %collective-permute-start.2 = (f32[1,4736]{1,0:T(1,128)S(1)}, f32[1,4736]{1,0:T(1,128)S(1)}, u32[]{:S(2)}, u32[]{:S(2)}) collective-permute-start(f32[1,4736]{1,0:T(1,128)S(1)} %gather.1.v0), channel_id=1, source_target_pairs={{0,3},{1,2},{2,1},{3,0},{4,7},{5,6},{6,5},{7,4},{8,11},{9,10},{10,... | collective-permute-start | bytes 56840 | tf_op jit(solution)/shard_map/ppermute | solution.py:270
  34.1 0.5 collective-permute-start.1
  34.7 1.6 %collective-permute-done.2.v3 = f32[1,4736]{1,0:T(1,128)S(1)} collective-permute-done((f32[1,4736]{1,0:T(1,128)S(1)}, f32[1,4736]{1,0:T(1,128)S(1)}, u32[]{:S(2)}, u32[]{:S(2)}) %collective-permute-start.2) | collective-permute-done | bytes 18976 | tf_op jit(solution)/shard_map/ppermute | solution.py:270
  36.5 2.2 %collective-permute-done.1.v2 = f32[1,4736]{1,0:T(1,128)S(1)} collective-permute-done((f32[1,4736]{1,0:T(1,128)S(1)}, f32[1,4736]{1,0:T(1,128)S(1)}, u32[]{:S(2)}, u32[]{:S(2)}) %collective-permute-start.1) | collective-permute-done | bytes 18976 | tf_op jit(solution)/shard_map/ppermute | solution.py:270
  39.0 2.1 %first_step.1 = (f32[8,640]{1,0:T(8,128)S(1)}, f32[32,1,640]{2,1,0:T(1,128)S(1)}, f32[1,144]{1,0:T(1,128)}) custom-call(s32[16]{0:T(128)S(1)} %copy-done.5, f32[1,4736]{1,0:T(1,128)S(1)} %gather.1.v0, f32[1,4736]{1,0:T(1,128)S(1)} %collective-permute-done.v1, f32[1,4736]{1,0:T(1,128)S(1)} %collective-permute-done.1.v2, ...), custom_call_target="tpu_custom_call" | custom-call | tf_op jit(solution)/shard_map/first_step/pallas_call | solution.py:310
  41.1 18.2 %all_to_all.36.recv_ref.refs_1_ = f32[32,1,640]{2,1,0:T(1,128)S(1)} all-to-all(f32[32,1,640]{2,1,0:T(1,128)S(1)} %get-tuple-element.19), channel_id=1, replica_groups=mesh['clu'=32,'col'=4] {'clu'}, dimensions={0} | all-to-all | bytes 163840 | tf_op jit(solution)/shard_map/all_to_all | solution.py:297
  59.3 2.1 %elim.2.refs_7_ = f32[32,1,640]{2,1,0:T(1,128)S(1)} custom-call(s32[1,1024]{1,0:T(1,128)S(1)} %bitcast.20, s32[1,1024]{1,0:T(1,128)S(1)} %bitcast.23, f32[3,3,1024]{2,1,0:T(4,128)S(1)} %copy-done.2, f32[32,1,640]{2,1,0:T(1,128)S(1)} %all_to_all.36.recv_ref.refs_1_, bf16[1728,1024]{1,0:T(8,128)(2,1)S(1)} %bitcast.17), custom_call_target="tpu_custom_call" | custom-call | flops 452984832 | bytes 4194304 | tf_op jit(solution)/shard_map/elim/pallas_call | solution.py:321
  61.4 1.5 %step.5 = (f32[8,640]{1,0:T(8,128)S(1)}, f32[32,1,1280]{2,1,0:T(1,128)S(1)}) custom-call(s32[16]{0:T(128)S(1)} %copy-done.5, f32[32,1,640]{2,1,0:T(1,128)S(1)} %all_to_all.36.recv_ref.refs_1_, f32[8,640]{1,0:T(8,128)S(1)} %get-tuple-element.20.refs_2_, bf16[4,144,576]{2,1,0:T(8,128)(2,1)S(1)} %bitcast.10, ...), custom_call_target="tpu_custom_call" | custom-call | tf_op jit(solution)/shard_map/step/pallas_call | solution.py:335
  62.9 11.5 %all_to_all.37.refs_1_ = f32[32,1,1280]{2,1,0:T(1,128)S(1)} all-to-all(f32[32,1,1280]{2,1,0:T(1,128)S(1)} %get-tuple-element.21), channel_id=1, replica_groups=mesh['clu'=32,'col'=4] {'clu'}, dimensions={0} | all-to-all | bytes 327680 | tf_op jit(solution)/shard_map/all_to_all | solution.py:297
  74.4 1.4 %step.6 = (f32[8,640]{1,0:T(8,128)S(1)}, f32[32,1,640]{2,1,0:T(1,128)S(1)}) custom-call(s32[16]{0:T(128)S(1)} %copy-done.5, f32[32,1,1280]{2,1,0:T(1,128)S(1)} %all_to_all.37.refs_1_, f32[8,640]{1,0:T(8,128)S(1)} %get-tuple-element.22.refs_2_, bf16[4,144,576]{2,1,0:T(8,128)(2,1)S(1)} %bitcast.11, bf16[4,144,576]{2,1,0:T(8,128)(2,1)S(1)} %collective-permute-done.3.b1.refs_4_, ...), custom_call_target="tpu_custom_call" | custom-call | tf_op jit(solution)/shard_map/step/pallas_call | solution.py:335
  75.9 11.0 %all_to_all.38.recv_ref.refs_1_ = f32[32,1,640]{2,1,0:T(1,128)S(1)} all-to-all(f32[32,1,640]{2,1,0:T(1,128)S(1)} %get-tuple-element.23), channel_id=1, replica_groups=mesh['clu'=32,'col'=4] {'clu'}, dimensions={0} | all-to-all | bytes 163840 | tf_op jit(solution)/shard_map/all_to_all | solution.py:297
  86.9 2.1 %elim.3.refs_7_ = f32[32,1,640]{2,1,0:T(1,128)S(1)} custom-call(s32[1,1024]{1,0:T(1,128)S(1)} %bitcast.21, s32[1,1024]{1,0:T(1,128)S(1)} %bitcast.24, f32[3,3,1024]{2,1,0:T(4,128)S(1)} %copy-done.2, f32[32,1,640]{2,1,0:T(1,128)S(1)} %all_to_all.38.recv_ref.refs_1_, bf16[1728,1024]{1,0:T(8,128)(2,1)S(1)} %bitcast.18), custom_call_target="tpu_custom_call" | custom-call | flops 452984832 | bytes 4194304 | tf_op jit(solution)/shard_map/elim/pallas_call | solution.py:321
  89.0 1.5 %step.7 = (f32[8,640]{1,0:T(8,128)S(1)}, f32[32,1,1280]{2,1,0:T(1,128)S(1)}) custom-call(s32[16]{0:T(128)S(1)} %copy-done.5, f32[32,1,640]{2,1,0:T(1,128)S(1)} %all_to_all.38.recv_ref.refs_1_, f32[8,640]{1,0:T(8,128)S(1)} %get-tuple-element.24.refs_2_, bf16[4,144,576]{2,1,0:T(8,128)(2,1)S(1)} %bitcast.12, ...), custom_call_target="tpu_custom_call" | custom-call | tf_op jit(solution)/shard_map/step/pallas_call | solution.py:335
  90.4 11.5 %all_to_all.39.refs_1_ = f32[32,1,1280]{2,1,0:T(1,128)S(1)} all-to-all(f32[32,1,1280]{2,1,0:T(1,128)S(1)} %get-tuple-element.25), channel_id=1, replica_groups=mesh['clu'=32,'col'=4] {'clu'}, dimensions={0} | all-to-all | bytes 327680 | tf_op jit(solution)/shard_map/all_to_all | solution.py:297
  102.0 1.5 %step.8 = (f32[8,640]{1,0:T(8,128)S(1)}, f32[32,1,640]{2,1,0:T(1,128)S(1)}) custom-call(s32[16]{0:T(128)S(1)} %copy-done.5, f32[32,1,1280]{2,1,0:T(1,128)S(1)} %all_to_all.39.refs_1_, f32[8,640]{1,0:T(8,128)S(1)} %get-tuple-element.26.refs_2_, bf16[4,144,576]{2,1,0:T(8,128)(2,1)S(1)} %bitcast.13, bf16[4,144,576]{2,1,0:T(8,128)(2,1)S(1)} %collective-permute-done.3.b1.refs_4_, ...), custom_call_target="tpu_custom_call" | custom-call | tf_op jit(solution)/shard_map/step/pallas_call | solution.py:335
  103.4 11.0 %all_to_all.40.refs_1_ = f32[32,1,640]{2,1,0:T(1,128)S(1)} all-to-all(f32[32,1,640]{2,1,0:T(1,128)S(1)} %get-tuple-element.27), channel_id=1, replica_groups=mesh['clu'=32,'col'=4] {'clu'}, dimensions={0} | all-to-all | bytes 163840 | tf_op jit(solution)/shard_map/all_to_all | solution.py:297
  114.4 1.5 %step.9 = (f32[8,640]{1,0:T(8,128)S(1)}, f32[128,1,640]{2,1,0:T(1,128)S(1)}) custom-call(s32[16]{0:T(128)S(1)} %copy-done.5, f32[32,1,640]{2,1,0:T(1,128)S(1)} %all_to_all.40.refs_1_, f32[8,640]{1,0:T(8,128)S(1)} %get-tuple-element.28.refs_2_, bf16[4,144,576]{2,1,0:T(8,128)(2,1)S(1)} %bitcast.14, bf16[4,144,576]{2,1,0:T(8,128)(2,1)S(1)} %collective-permute-done.3.b1.refs_4_, ...), custom_call_target="tpu_custom_call" | custom-call | tf_op jit(solution)/shard_map/step/pallas_call | solution.py:335
  115.9 17.4 %all_to_all.41.recv_ref = f32[128,1,640]{2,1,0:T(1,128)S(1)} all-to-all(f32[128,1,640]{2,1,0:T(1,128)S(1)} %get-tuple-element.29), channel_id=1, replica_groups=mesh['clu'=32,'col'=4] {'clu','col'}, dimensions={0} | all-to-all | bytes 655360 | tf_op jit(solution)/shard_map/all_to_all | solution.py:355
  133.3 2.1 %last_step.1 = f32[1,144]{1,0:T(1,128)} custom-call(s32[16]{0:T(128)S(1)} %copy-done.5, f32[128,1,640]{2,1,0:T(1,128)S(1)} %all_to_all.41.recv_ref, f32[8,640]{1,0:T(8,128)S(1)} %get-tuple-element.30.state_ref, bf16[4,144,576]{2,1,0:T(8,128)(2,1)S(1)} %bitcast.15, bf16[4,144,576]{2,1,0:T(8,128)(2,1)S(1)} %collective-permute-done.3.b1.refs_4_, ...), custom_call_target="tpu_custom_call" | custom-call | tf_op jit(solution)/shard_map/last_step/pallas_call | solution.py:356
  (18 shorter events, 1.1 us)
Async XLA Ops:
  0.6 38.3 %copy-start = (bf16[1,4,576,144]{2,3,1,0:T(8,128)(2,1)S(1)}, bf16[1,4,576,144]{2,3,1,0:T(8,128)(2,1)}, u32[]{:S(2)}) copy-start(bf16[1,4,576,144]{2,3,1,0:T(8,128)(2,1)} %param.19) | copy-start | bytes 1990660
  0.6 38.3 %collective-permute-start.5 = (bf16[4,144,576]{2,1,0:T(8,128)(2,1)}, bf16[4,144,576]{2,1,0:T(8,128)(2,1)S(1)}, u32[]{:S(2)}, u32[]{:S(2)}) collective-permute-start(bf16[4,144,576]{2,1,0:T(8,128)(2,1)} %bitcast.6), channel_id=1, source_target_pairs={{0,3},{1,2},{2,1},{3,0},{4,7},{5,6},{6,5},{7,4},{8,11},{9,10},{10,... | collective-permute-start | bytes 1990664 | tf_op jit(solution)/shard_map/ppermute | solution.py:270
  4.0 34.9 %collective-permute-start.4 = (bf16[4,144,576]{2,1,0:T(8,128)(2,1)}, bf16[4,144,576]{2,1,0:T(8,128)(2,1)S(1)}, u32[]{:S(2)}, u32[]{:S(2)}) collective-permute-start(bf16[4,144,576]{2,1,0:T(8,128)(2,1)} %bitcast.7), channel_id=1, source_target_pairs={{0,2},{1,3},{2,0},{3,1},{4,6},{5,7},{6,4},{7,5},{8,10},{9,11},{10,... | collective-permute-start | bytes 1990664 | tf_op jit(solution)/shard_map/ppermute | solution.py:270
  4.6 34.4 %collective-permute-start.3 = (bf16[4,144,576]{2,1,0:T(8,128)(2,1)}, bf16[4,144,576]{2,1,0:T(8,128)(2,1)S(1)}, u32[]{:S(2)}, u32[]{:S(2)}) collective-permute-start(bf16[4,144,576]{2,1,0:T(8,128)(2,1)} %bitcast.8), channel_id=1, source_target_pairs={{0,1},{1,0},{2,3},{3,2},{4,5},{5,4},{6,7},{7,6},{8,9},{9,8},{10,11... | collective-permute-start | bytes 1990664 | tf_op jit(solution)/shard_map/ppermute | solution.py:270
  4.7 54.6 %copy-start.1 = (bf16[1024,1728]{0,1:T(8,128)(2,1)S(1)}, bf16[1024,1728]{0,1:T(8,128)(2,1)}, u32[]{:S(2)}) copy-start(bf16[1024,1728]{0,1:T(8,128)(2,1)} %param.13) | copy-start | bytes 10616836
  4.7 54.6 %copy-start.2 = (f32[3,3,1024]{2,1,0:T(4,128)S(1)}, f32[3,3,1024]{2,1,0:T(4,128)}, u32[]{:S(2)}) copy-start(f32[3,3,1024]{2,1,0:T(4,128)} %info_ref.5) | copy-start | bytes 110596
  4.7 54.6 %copy-start.3 = (s32[1024,1]{0,1:T(1,128)S(1)}, s32[1024,1]{0,1:T(1,128)}, u32[]{:S(2)}) copy-start(s32[1024,1]{0,1:T(1,128)} %param.11) | copy-start | bytes 12292
  4.7 54.6 %copy-start.4 = (s32[1024]{0:T(1024)S(1)}, s32[1024]{0:T(1024)}, u32[]{:S(2)}) copy-start(s32[1024]{0:T(1024)} %param.12) | copy-start | bytes 12292
  30.3 0.7 copy-start.5
  31.6 4.7 %collective-permute-start.2 = (f32[1,4736]{1,0:T(1,128)S(1)}, f32[1,4736]{1,0:T(1,128)S(1)}, u32[]{:S(2)}, u32[]{:S(2)}) collective-permute-start(f32[1,4736]{1,0:T(1,128)S(1)} %gather.1.v0), channel_id=1, source_target_pairs={{0,3},{1,2},{2,1},{3,0},{4,7},{5,6},{6,5},{7,4},{8,11},{9,10},{10,... | collective-permute-start | bytes 56840 | tf_op jit(solution)/shard_map/ppermute | solution.py:270
  34.1 4.6 %collective-permute-start.1 = (f32[1,4736]{1,0:T(1,128)S(1)}, f32[1,4736]{1,0:T(1,128)S(1)}, u32[]{:S(2)}, u32[]{:S(2)}) collective-permute-start(f32[1,4736]{1,0:T(1,128)S(1)} %gather.1.v0), channel_id=1, source_target_pairs={{0,2},{1,3},{2,0},{3,1},{4,6},{5,7},{6,4},{7,5},{8,10},{9,11},{10,... | collective-permute-start | bytes 56840 | tf_op jit(solution)/shard_map/ppermute | solution.py:270
  36.3 2.6 %collective-permute-start = (f32[1,4736]{1,0:T(1,128)S(1)}, f32[1,4736]{1,0:T(1,128)S(1)}, u32[]{:S(2)}, u32[]{:S(2)}) collective-permute-start(f32[1,4736]{1,0:T(1,128)S(1)} %gather.1.v0), channel_id=1, source_target_pairs={{0,1},{1,0},{2,3},{3,2},{4,5},{5,4},{6,7},{7,6},{8,9},{9,8},{10,11... | collective-permute-start | bytes 56840 | tf_op jit(solution)/shard_map/ppermute | solution.py:270

commit v4 on v3

--- a/solution.py
+++ b/solution.py
@@ -144,12 +144,16 @@
         for m in range(SHARE // 16):
             xs = columns[pl.ds(pl.multiple_of(base + 16 * m, 16), 16), :]
             for r in range(ROUNDS):
-                acc = acc + blocks[k][r, 16 * m : 16 * m + 16, :].astype(F32) * xs[:, r : r + 1]
+                if k == 2:
+                    block = blocks[2 + r // 2][r % 2, 16 * m : 16 * m + 16, :]
+                else:
+                    block = blocks[k + k // 3][r, 16 * m : 16 * m + 16, :]
+                acc = acc + block.astype(F32) * xs[:, r : r + 1]
     return widen(jnp.sum(acc, 0, keepdims=True))
 
 
 def first_step_kernel(
-    ids_ref, v0, v1, v2, v3, b0, b1, b2, b3, state_ref, out_ref, rhs_ref, columns
+    ids_ref, v0, v1, v2, v3, b0, b1, b2, b3, b4, state_ref, out_ref, rhs_ref, columns
 ):
     col = ids_ref[MY_COL]
     rows = [v[...] for v in (v0, v1, v2, v3)]
@@ -170,7 +174,7 @@
     for r in range(ROUNDS):
         x = full(r + 1) * vectors[:, WIDE * (r + 1) : WIDE * (r + 2)]
         near.append(jnp.where(ids_ref[PARTNER_COLOUR + r] == 0, x, 0.0))
-    coupled = couple(ids_ref, near, (b0, b1, b2, b3), columns)
+    coupled = couple(ids_ref, near, (b0, b1, b2, b3, b4), columns)
     mine = ids_ref[MY_COLOUR]
     x = jnp.where(mine == 0, step * rhs, jnp.where(mine == 1, step * (rhs - coupled), 0.0))
     state_ref[0:1, :] = x
@@ -185,8 +189,8 @@
 
 def step_kernel(number, has_send, has_recv, *refs):
     ids_ref, recv_ref, state_ref = refs[:3]
-    blocks = refs[3:7]
-    send_ref = refs[7] if has_send else None
+    blocks = refs[3:8]
+    send_ref = refs[8] if has_send else None
     new_ref, out_ref, columns = refs[-3:]
     near = [recv_ref[ids_ref[PARTNER + r], :, :WIDE] for r in range(ROUNDS)]
     coupled = couple(ids_ref, near, blocks, columns)
@@ -213,7 +217,7 @@
         out_ref[:, :, WIDE:] = send_ref[...]
 
 
-def last_step_kernel(ids_ref, recv_ref, state_ref, b0, b1, b2, b3, out_ref, columns):
+def last_step_kernel(ids_ref, recv_ref, state_ref, b0, b1, b2, b3, b4, out_ref, columns):
     def total(c):
         v = recv_ref[COLS * c]
         for k in range(1, COLS):
@@ -221,7 +225,7 @@
         return v
 
     near = [total(ids_ref[PARTNER + r]) for r in range(ROUNDS)]
-    coupled = couple(ids_ref, near, (b0, b1, b2, b3), columns)
+    coupled = couple(ids_ref, near, (b0, b1, b2, b3, b4), columns)
     x = total(ids_ref[MY_CLU])
     x = jnp.where(ids_ref[MY_COLOUR] == COLOURS - 1, x - state_ref[2:3, :] * coupled, x)
     out_ref[...] = take_share(x, ids_ref[MY_COL])
@@ -269,8 +273,11 @@
     def over_col(v):
         return [v] + [lax.ppermute(v, "col", [(i, i ^ k) for i in range(COLS)]) for k in (1, 3, 2)]
 
-    own, first, third, second = over_col(own)
-    blocks = [own, first, second, third]
+    def swap(v, k):
+        return lax.ppermute(v, "col", [(i, i ^ k) for i in range(COLS)])
+
+    first, third = swap(own, 1), swap(own, 3)
+    blocks = [own, first, swap(first[: ROUNDS // 2], 3), swap(third[ROUNDS // 2 :], 1), third]
     limit = pltpu.CompilerParams(vmem_limit_bytes=24 << 20)
 
     whole = lambda *block: pl.BlockSpec(block, lambda a: (0,) * len(block))
@@ -309,7 +316,7 @@
     columns = pltpu.VMEM((WIDE, 8), F32)
     state, payload, reduced_rhs = pl.pallas_call(
         first_step_kernel,
-        in_specs=[smem()] + [vmem()] * 8,
+        in_specs=[smem()] + [vmem()] * 9,
         out_specs=[vmem()] * 3,
         out_shape=[shape(8, WIDE), shape(CLUSTERS, 1, WIDE), shape(1, SHARE)],
         scratch_shapes=[columns],
@@ -334,7 +341,7 @@
         rows = CLUSTERS * COLS if number == 2 * COLOURS - 2 else CLUSTERS
         return pl.pallas_call(
             functools.partial(step_kernel, number, send is not None, has_recv),
-            in_specs=[smem()] + [vmem()] * (6 if send is None else 7),
+            in_specs=[smem()] + [vmem()] * (7 if send is None else 8),
             out_specs=[vmem()] * 2,
             out_shape=[shape(8, WIDE), shape(rows, 1, WIDE if send is None else 2 * WIDE)],
             scratch_shapes=[columns],
@@ -355,7 +362,7 @@
     recv = lax.all_to_all(payload, ("clu", "col"), split_axis=0, concat_axis=0, tiled=True)
     solution = pl.pallas_call(
         last_step_kernel,
-        in_specs=[smem()] + [vmem()] * 6,
+        in_specs=[smem()] + [vmem()] * 7,
         out_specs=vmem(),
         out_shape=shape(1, SHARE),
         scratch_shapes=[columns],

time: 136 us -> 129 us (0.949)
  blocking collectives: 101 us -> 76 us
  starting transfers between devices: 7.35 us -> 18.8 us
  waiting for transfers between devices: 4.02 us -> 9.37 us
  local copies, waits for them, and re-layouts: 0.67 us -> 2.4 us
    all_to_all x6 -> x5, blocking collectives: 83.9 us -> 58.9 us  [over_clu(): return lax.all_to_all(v, 'clu', split_axis=0, concat_axis=0, tiled=True)]
    all_to_all x0 -> x1, starting transfers between devices: none -> 9.4 us  [over_clu(): return lax.all_to_all(v, 'clu', split_axis=0, concat_axis=0, tiled=True)]
    ppermute x0 -> x4, starting transfers between devices: none -> 6.04 us  [swap(): return lax.ppermute(v, 'col', [(i, i ^ k) for i in range(COLS)])]
    all_to_all x0 -> x1, waiting for transfers between devices: none -> 4.85 us  [over_clu(): return lax.all_to_all(v, 'clu', split_axis=0, concat_axis=0, tiled=True)]
    ppermute x6 -> x3, starting transfers between devices: 7.35 us -> 3.39 us  [over_col(): lax.ppermute(v, 'col', [(i, i ^ k) for i in range(COLS)])]
    ppermute x0 -> x4, waiting for transfers between devices: none -> 1.91 us  [swap(): return lax.ppermute(v, 'col', [(i, i ^ k) for i in range(COLS)])]
    slice x0 -> x2, local copies, waits for them, and re-layouts: none -> 1.56 us  [the longest x1 0.8 us: per_device(): third[ROUNDS // 2:]]
    ppermute x6 -> x3, waiting for transfers between devices: 4.02 us -> 2.61 us  [over_col(): lax.ppermute(v, 'col', [(i, i ^ k) for i in range(COLS)])]
  transfers between devices with their start and end apart: 6 -> 8, of which waited for: 3 -> 6; matrix products, arithmetic and copies ran while one was open for 0% -> 1% of each run, Pallas kernels for 4% -> 4%
where the time goes in v4:
time: 129 us
  blocking collectives  76 us (59%)
  Pallas kernels  21.2 us (16%)
  starting transfers between devices  18.8 us (15%)
  waiting for transfers between devices  9.37 us (7%)
  local copies, waits for them, and re-layouts  2.4 us (2%)
    all_to_all x5, blocking collectives, over_clu(): return lax.all_to_all(v, 'clu', split_axis=0, concat_axis=0, tiled=True)  58.9 us
    all_to_all x1, blocking collectives, per_device(): lax.all_to_all(payload, ('clu', 'col'), split_axis=0, concat_axis=0, tile...  17 us
    all_to_all x1, starting transfers between devices, over_clu(): return lax.all_to_all(v, 'clu', split_axis=0, concat_axis=0, tiled=True)  9.4 us
    pallas_call x5, Pallas kernels, update(): pl.pallas_call(functools.partial(step_kernel, number, send is not None, h...  7.35 us
    ppermute x4, starting transfers between devices, swap(): return lax.ppermute(v, 'col', [(i, i ^ k) for i in range(COLS)])  6.04 us
    all_to_all x1, waiting for transfers between devices, over_clu(): return lax.all_to_all(v, 'clu', split_axis=0, concat_axis=0, tiled=True)  4.85 us
    pallas_call x1, Pallas kernels, per_device(): pl.pallas_call(rhs_kernel, grid=(3,), in_specs=[smem(), smem(), whole(1,...  4.77 us
    pallas_call x2, Pallas kernels, eliminate(): pl.pallas_call(elim_kernel, in_specs=[vmem()] * 5, out_specs=vmem(), out_...  4.22 us
  transfers between devices with their start and end apart: 8, of which 6 were waited for; matrix products, arithmetic and copies ran while one was open for 1% of the time, Pallas kernels for 4%

profile of v4, /device:TPU:1, one launch (start us, length us, event | category | flops | bytes accessed | tf_op | source)
XLA Modules:
  0.0 128.6 jit_solution(1749885551482437204)
XLA Ops:
  0.6 3.4 %collective-permute-start.5 = (bf16[4,144,576]{2,1,0:T(8,128)(2,1)}, bf16[4,144,576]{2,1,0:T(8,128)(2,1)S(1)}, u32[]{:S(2)}, u32[]{:S(2)}) collective-permute-start(bf16[4,144,576]{2,1,0:T(8,128)(2,1)} %bitcast.6), channel_id=1, source_target_pairs={{0,3},{1,2},{2,1},{3,0},{4,7},{5,6},{6,5},{7,4},{8,11},{9,10},{10,... | collective-permute-start | bytes 1990664 | tf_op jit(solution)/shard_map/ppermute | solution.py:277
  4.0 4.8 %rhs.1 = (f32[32,1,3584]{2,1,0:T(1,128)}, s32[16]{0:T(128)}) custom-call(s32[32]{0:T(128)} %cc_ref.1, s32[4,4,32]{2,1,0:T(4,128)} %rp_ref.1, s32[1,1024]{1,0:T(1,128)} %bitcast.18, s32[1,1024]{1,0:T(1,128)} %bitcast.21, f32[3,3,1024]{2,1,0:T(4,128)} %info_ref.5, f32[3,1024]{1,0:T(4,128)} %grad_ref.1, bf16[1728,1024]{1,0:T(8,128)(2,1)} %bitcast.15, ...), custom_call_target="tpu_custom_call" | custom-call | tf_op jit(solution)/shard_map/rhs/pallas_call | solution.py:284
  8.8 9.4 %all-to-all-start = ((f32[32,1,3584]{2,1,0:T(1,128)}), f32[32,1,3584]{2,1,0:T(1,128)S(1)}, u32[]{:S(2)}, u32[]{:S(2)}) async-start(f32[32,1,3584]{2,1,0:T(1,128)} %get-tuple-element.18), calls=%async_computation | async-start | bytes 917504 | tf_op jit(solution)/shard_map/all_to_all | solution.py:304
  18.3 1.8 %collective-permute-done.5.b4.refs_7_ = bf16[4,144,576]{2,1,0:T(8,128)(2,1)S(1)} collective-permute-done((bf16[4,144,576]{2,1,0:T(8,128)(2,1)}, bf16[4,144,576]{2,1,0:T(8,128)(2,1)S(1)}, u32[]{:S(2)}, u32[]{:S(2)}) %collective-permute-start.5) | collective-permute-done | bytes 663584 | tf_op jit(solution)/shard_map/ppermute | solution.py:277
  22.0 2.3 %collective-permute-start.4 = (bf16[2,144,576]{2,1,0:T(8,128)(2,1)}, bf16[2,144,576]{2,1,0:T(8,128)(2,1)S(1)}, u32[]{:S(2)}, u32[]{:S(2)}) collective-permute-start(bf16[2,144,576]{2,1,0:T(8,128)(2,1)} %slice.8), channel_id=1, source_target_pairs={{0,3},{1,2},{2,1},{3,0},{4,7},{5,6},{6,5},{7,4},{8,11},{9,10},{10,... | collective-permute-start | bytes 995336 | tf_op jit(solution)/shard_map/ppermute | solution.py:277
  24.4 4.8 %all-to-all-done.recv_ref = f32[32,1,3584]{2,1,0:T(1,128)S(1)} async-done(((f32[32,1,3584]{2,1,0:T(1,128)}), f32[32,1,3584]{2,1,0:T(1,128)S(1)}, u32[]{:S(2)}, u32[]{:S(2)}) %all-to-all-start) | async-done | bytes 458784 | tf_op jit(solution)/shard_map/all_to_all | solution.py:304
  31.6 2.5 %collective-permute-start.1 = (f32[1,4736]{1,0:T(1,128)S(1)}, f32[1,4736]{1,0:T(1,128)S(1)}, u32[]{:S(2)}, u32[]{:S(2)}) collective-permute-start(f32[1,4736]{1,0:T(1,128)S(1)} %gather.1.v0), channel_id=1, source_target_pairs={{0,2},{1,3},{2,0},{3,1},{4,6},{5,7},{6,4},{7,5},{8,10},{9,11},{10,... | collective-permute-start | bytes 56840 | tf_op jit(solution)/shard_map/ppermute | solution.py:274
  34.5 1.2 collective-permute-done.1.v2
  35.7 0.9 collective-permute-done.v1
  36.7 2.2 %first_step.1 = (f32[8,640]{1,0:T(8,128)S(1)}, f32[32,1,640]{2,1,0:T(1,128)S(1)}, f32[1,144]{1,0:T(1,128)}) custom-call(s32[16]{0:T(128)S(1)} %copy-done.5, f32[1,4736]{1,0:T(1,128)S(1)} %gather.1.v0, f32[1,4736]{1,0:T(1,128)S(1)} %collective-permute-done.v1, f32[1,4736]{1,0:T(1,128)S(1)} %collective-permute-done.1.v2, ...), custom_call_target="tpu_custom_call" | custom-call | tf_op jit(solution)/shard_map/first_step/pallas_call | solution.py:317
  38.8 13.9 %all_to_all.35.recv_ref.refs_1_ = f32[32,1,640]{2,1,0:T(1,128)S(1)} all-to-all(f32[32,1,640]{2,1,0:T(1,128)S(1)} %get-tuple-element.19), channel_id=1, replica_groups=mesh['clu'=32,'col'=4] {'clu'}, dimensions={0} | all-to-all | bytes 163840 | tf_op jit(solution)/shard_map/all_to_all | solution.py:304
  52.8 2.1 %elim.2.refs_8_ = f32[32,1,640]{2,1,0:T(1,128)S(1)} custom-call(s32[1,1024]{1,0:T(1,128)S(1)} %bitcast.19, s32[1,1024]{1,0:T(1,128)S(1)} %bitcast.22, f32[3,3,1024]{2,1,0:T(4,128)S(1)} %copy-done.2, f32[32,1,640]{2,1,0:T(1,128)S(1)} %all_to_all.35.recv_ref.refs_1_, bf16[1728,1024]{1,0:T(8,128)(2,1)S(1)} %bitcast.16), custom_call_target="tpu_custom_call" | custom-call | flops 452984832 | bytes 4194304 | tf_op jit(solution)/shard_map/elim/pallas_call | solution.py:328
  54.9 1.5 %step.5 = (f32[8,640]{1,0:T(8,128)S(1)}, f32[32,1,1280]{2,1,0:T(1,128)S(1)}) custom-call(s32[16]{0:T(128)S(1)} %copy-done.6, f32[32,1,640]{2,1,0:T(1,128)S(1)} %all_to_all.35.recv_ref.refs_1_, f32[8,640]{1,0:T(8,128)S(1)} %get-tuple-element.20.refs_2_, bf16[4,144,576]{2,1,0:T(8,128)(2,1)S(1)} %bitcast.9, ...), custom_call_target="tpu_custom_call" | custom-call | tf_op jit(solution)/shard_map/step/pallas_call | solution.py:342
  56.4 11.5 %all_to_all.36.refs_1_ = f32[32,1,1280]{2,1,0:T(1,128)S(1)} all-to-all(f32[32,1,1280]{2,1,0:T(1,128)S(1)} %get-tuple-element.21), channel_id=1, replica_groups=mesh['clu'=32,'col'=4] {'clu'}, dimensions={0} | all-to-all | bytes 327680 | tf_op jit(solution)/shard_map/all_to_all | solution.py:304
  67.9 1.5 %step.6 = (f32[8,640]{1,0:T(8,128)S(1)}, f32[32,1,640]{2,1,0:T(1,128)S(1)}) custom-call(s32[16]{0:T(128)S(1)} %copy-done.6, f32[32,1,1280]{2,1,0:T(1,128)S(1)} %all_to_all.36.refs_1_, f32[8,640]{1,0:T(8,128)S(1)} %get-tuple-element.22.refs_2_, bf16[4,144,576]{2,1,0:T(8,128)(2,1)S(1)} %bitcast.10, bf16[4,144,576]{2,1,0:T(8,128)(2,1)S(1)} %collective-permute-done.3.b1.refs_4_, ...), custom_call_target="tpu_custom_call" | custom-call | tf_op jit(solution)/shard_map/step/pallas_call | solution.py:342
  69.4 11.0 %all_to_all.37.recv_ref.refs_1_ = f32[32,1,640]{2,1,0:T(1,128)S(1)} all-to-all(f32[32,1,640]{2,1,0:T(1,128)S(1)} %get-tuple-element.23), channel_id=1, replica_groups=mesh['clu'=32,'col'=4] {'clu'}, dimensions={0} | all-to-all | bytes 163840 | tf_op jit(solution)/shard_map/all_to_all | solution.py:304
  80.4 2.1 %elim.3.refs_8_ = f32[32,1,640]{2,1,0:T(1,128)S(1)} custom-call(s32[1,1024]{1,0:T(1,128)S(1)} %bitcast.20, s32[1,1024]{1,0:T(1,128)S(1)} %bitcast.23, f32[3,3,1024]{2,1,0:T(4,128)S(1)} %copy-done.2, f32[32,1,640]{2,1,0:T(1,128)S(1)} %all_to_all.37.recv_ref.refs_1_, bf16[1728,1024]{1,0:T(8,128)(2,1)S(1)} %bitcast.17), custom_call_target="tpu_custom_call" | custom-call | flops 452984832 | bytes 4194304 | tf_op jit(solution)/shard_map/elim/pallas_call | solution.py:328
  82.5 1.5 %step.7 = (f32[8,640]{1,0:T(8,128)S(1)}, f32[32,1,1280]{2,1,0:T(1,128)S(1)}) custom-call(s32[16]{0:T(128)S(1)} %copy-done.6, f32[32,1,640]{2,1,0:T(1,128)S(1)} %all_to_all.37.recv_ref.refs_1_, f32[8,640]{1,0:T(8,128)S(1)} %get-tuple-element.24.refs_2_, bf16[4,144,576]{2,1,0:T(8,128)(2,1)S(1)} %bitcast.11, ...), custom_call_target="tpu_custom_call" | custom-call | tf_op jit(solution)/shard_map/step/pallas_call | solution.py:342
  84.0 11.5 %all_to_all.38.refs_1_ = f32[32,1,1280]{2,1,0:T(1,128)S(1)} all-to-all(f32[32,1,1280]{2,1,0:T(1,128)S(1)} %get-tuple-element.25), channel_id=1, replica_groups=mesh['clu'=32,'col'=4] {'clu'}, dimensions={0} | all-to-all | bytes 327680 | tf_op jit(solution)/shard_map/all_to_all | solution.py:304
  95.5 1.5 %step.8 = (f32[8,640]{1,0:T(8,128)S(1)}, f32[32,1,640]{2,1,0:T(1,128)S(1)}) custom-call(s32[16]{0:T(128)S(1)} %copy-done.6, f32[32,1,1280]{2,1,0:T(1,128)S(1)} %all_to_all.38.refs_1_, f32[8,640]{1,0:T(8,128)S(1)} %get-tuple-element.26.refs_2_, bf16[4,144,576]{2,1,0:T(8,128)(2,1)S(1)} %bitcast.12, bf16[4,144,576]{2,1,0:T(8,128)(2,1)S(1)} %collective-permute-done.3.b1.refs_4_, ...), custom_call_target="tpu_custom_call" | custom-call | tf_op jit(solution)/shard_map/step/pallas_call | solution.py:342
  97.0 11.0 %all_to_all.39.refs_1_ = f32[32,1,640]{2,1,0:T(1,128)S(1)} all-to-all(f32[32,1,640]{2,1,0:T(1,128)S(1)} %get-tuple-element.27), channel_id=1, replica_groups=mesh['clu'=32,'col'=4] {'clu'}, dimensions={0} | all-to-all | bytes 163840 | tf_op jit(solution)/shard_map/all_to_all | solution.py:304
  107.9 1.5 %step.9 = (f32[8,640]{1,0:T(8,128)S(1)}, f32[128,1,640]{2,1,0:T(1,128)S(1)}) custom-call(s32[16]{0:T(128)S(1)} %copy-done.6, f32[32,1,640]{2,1,0:T(1,128)S(1)} %all_to_all.39.refs_1_, f32[8,640]{1,0:T(8,128)S(1)} %get-tuple-element.28.refs_2_, bf16[4,144,576]{2,1,0:T(8,128)(2,1)S(1)} %bitcast.13, bf16[4,144,576]{2,1,0:T(8,128)(2,1)S(1)} %collective-permute-done.3.b1.refs_4_, ...), custom_call_target="tpu_custom_call" | custom-call | tf_op jit(solution)/shard_map/step/pallas_call | solution.py:342
  109.4 17.0 %all_to_all.40.recv_ref = f32[128,1,640]{2,1,0:T(1,128)S(1)} all-to-all(f32[128,1,640]{2,1,0:T(1,128)S(1)} %get-tuple-element.29), channel_id=1, replica_groups=mesh['clu'=32,'col'=4] {'clu','col'}, dimensions={0} | all-to-all | bytes 655360 | tf_op jit(solution)/shard_map/all_to_all | solution.py:362
  126.5 2.1 %last_step.1 = f32[1,144]{1,0:T(1,128)} custom-call(s32[16]{0:T(128)S(1)} %copy-done.6, f32[128,1,640]{2,1,0:T(1,128)S(1)} %all_to_all.40.recv_ref, f32[8,640]{1,0:T(8,128)S(1)} %get-tuple-element.30.state_ref, bf16[4,144,576]{2,1,0:T(8,128)(2,1)S(1)} %bitcast.14, bf16[4,144,576]{2,1,0:T(8,128)(2,1)S(1)} %collective-permute-done.3.b1.refs_4_, ...), custom_call_target="tpu_custom_call" | custom-call | tf_op jit(solution)/shard_map/last_step/pallas_call | solution.py:363
  (25 shorter events, 4.9 us)
Async XLA Ops:
  0.6 36.0 %copy-start = (bf16[1,4,576,144]{2,3,1,0:T(8,128)(2,1)S(1)}, bf16[1,4,576,144]{2,3,1,0:T(8,128)(2,1)}, u32[]{:S(2)}) copy-start(bf16[1,4,576,144]{2,3,1,0:T(8,128)(2,1)} %param.19) | copy-start | bytes 1990660
  0.6 19.4 %collective-permute-start.5 = (bf16[4,144,576]{2,1,0:T(8,128)(2,1)}, bf16[4,144,576]{2,1,0:T(8,128)(2,1)S(1)}, u32[]{:S(2)}, u32[]{:S(2)}) collective-permute-start(bf16[4,144,576]{2,1,0:T(8,128)(2,1)} %bitcast.6), channel_id=1, source_target_pairs={{0,3},{1,2},{2,1},{3,0},{4,7},{5,6},{6,5},{7,4},{8,11},{9,10},{10,... | collective-permute-start | bytes 1990664 | tf_op jit(solution)/shard_map/ppermute | solution.py:277
  4.0 17.2 %collective-permute-start.3 = (bf16[4,144,576]{2,1,0:T(8,128)(2,1)}, bf16[4,144,576]{2,1,0:T(8,128)(2,1)S(1)}, u32[]{:S(2)}, u32[]{:S(2)}) collective-permute-start(bf16[4,144,576]{2,1,0:T(8,128)(2,1)} %bitcast.7), channel_id=1, source_target_pairs={{0,1},{1,0},{2,3},{3,2},{4,5},{5,4},{6,7},{7,6},{8,9},{9,8},{10,11... | collective-permute-start | bytes 1990664 | tf_op jit(solution)/shard_map/ppermute | solution.py:277
  8.8 44.0 %copy-start.2 = (f32[3,3,1024]{2,1,0:T(4,128)S(1)}, f32[3,3,1024]{2,1,0:T(4,128)}, u32[]{:S(2)}) copy-start(f32[3,3,1024]{2,1,0:T(4,128)} %info_ref.5) | copy-start | bytes 110596
  8.8 44.0 %copy-start.3 = (s32[1024,1]{0,1:T(1,128)S(1)}, s32[1024,1]{0,1:T(1,128)}, u32[]{:S(2)}) copy-start(s32[1024,1]{0,1:T(1,128)} %param.11) | copy-start | bytes 12292
  8.8 43.9 %copy-start.4 = (s32[1024]{0:T(1024)S(1)}, s32[1024]{0:T(1024)}, u32[]{:S(2)}) copy-start(s32[1024]{0:T(1024)} %param.12) | copy-start | bytes 12292
  8.8 20.4 %all-to-all-start = ((f32[32,1,3584]{2,1,0:T(1,128)}), f32[32,1,3584]{2,1,0:T(1,128)S(1)}, u32[]{:S(2)}, u32[]{:S(2)}) async-start(f32[32,1,3584]{2,1,0:T(1,128)} %get-tuple-element.18), calls=%async_computation | async-start | bytes 917504 | tf_op jit(solution)/shard_map/all_to_all | solution.py:304
  20.8 15.9 %collective-permute-start.6 = (bf16[2,144,576]{2,1,0:T(8,128)(2,1)}, bf16[2,144,576]{2,1,0:T(8,128)(2,1)S(1)}, u32[]{:S(2)}, u32[]{:S(2)}) collective-permute-start(bf16[2,144,576]{2,1,0:T(8,128)(2,1)} %slice.9), channel_id=1, source_target_pairs={{0,1},{1,0},{2,3},{3,2},{4,5},{5,4},{6,7},{7,6},{8,9},{9,8},{10,11... | collective-permute-start | bytes 995336 | tf_op jit(solution)/shard_map/ppermute | solution.py:277
  22.0 14.6 %collective-permute-start.4 = (bf16[2,144,576]{2,1,0:T(8,128)(2,1)}, bf16[2,144,576]{2,1,0:T(8,128)(2,1)S(1)}, u32[]{:S(2)}, u32[]{:S(2)}) collective-permute-start(bf16[2,144,576]{2,1,0:T(8,128)(2,1)} %slice.8), channel_id=1, source_target_pairs={{0,3},{1,2},{2,1},{3,0},{4,7},{5,6},{6,5},{7,4},{8,11},{9,10},{10,... | collective-permute-start | bytes 995336 | tf_op jit(solution)/shard_map/ppermute | solution.py:277
  29.2 23.6 %copy-start.1 = (bf16[1024,1728]{0,1:T(8,128)(2,1)S(1)}, bf16[1024,1728]{0,1:T(8,128)(2,1)}, u32[]{:S(2)}) copy-start(bf16[1024,1728]{0,1:T(8,128)(2,1)} %param.13) | copy-start | bytes 10616836
  29.2 0.8 copy-start.5
  30.6 24.3 %copy-start.6 = (s32[16]{0:T(128)S(1)}, s32[16]{0:T(128)}, u32[]{:S(2)}) copy-start(s32[16]{0:T(128)} %get-tuple-element.17.ids_ref.refs_0_) | copy-start | bytes 196
  30.6 3.9 %collective-permute-start.2 = (f32[1,4736]{1,0:T(1,128)S(1)}, f32[1,4736]{1,0:T(1,128)S(1)}, u32[]{:S(2)}, u32[]{:S(2)}) collective-permute-start(f32[1,4736]{1,0:T(1,128)S(1)} %gather.1.v0), channel_id=1, source_target_pairs={{0,3},{1,2},{2,1},{3,0},{4,7},{5,6},{6,5},{7,4},{8,11},{9,10},{10,... | collective-permute-start | bytes 56840 | tf_op jit(solution)/shard_map/ppermute | solution.py:274
  31.6 4.1 %collective-permute-start.1 = (f32[1,4736]{1,0:T(1,128)S(1)}, f32[1,4736]{1,0:T(1,128)S(1)}, u32[]{:S(2)}, u32[]{:S(2)}) collective-permute-start(f32[1,4736]{1,0:T(1,128)S(1)} %gather.1.v0), channel_id=1, source_target_pairs={{0,2},{1,3},{2,0},{3,1},{4,6},{5,7},{6,4},{7,5},{8,10},{9,11},{10,... | collective-permute-start | bytes 56840 | tf_op jit(solution)/shard_map/ppermute | solution.py:274
  34.0 2.6 %collective-permute-start = (f32[1,4736]{1,0:T(1,128)S(1)}, f32[1,4736]{1,0:T(1,128)S(1)}, u32[]{:S(2)}, u32[]{:S(2)}) collective-permute-start(f32[1,4736]{1,0:T(1,128)S(1)} %gather.1.v0), channel_id=1, source_target_pairs={{0,1},{1,0},{2,3},{3,2},{4,5},{5,4},{6,7},{7,6},{8,9},{9,8},{10,11... | collective-permute-start | bytes 56840 | tf_op jit(solution)/shard_map/ppermute | solution.py:274

commit v5 on v4

--- a/solution.py
+++ b/solution.py
@@ -135,21 +135,27 @@
         out_ref[:, WIDE * 5 + SLOT * at : WIDE * 5 + SLOT * (at + 1)] = widen(share, SLOT)
 
 
-def couple(ids_ref, vectors, blocks, columns):
+def block_of(blocks, k, r):
+    if k == 2:
+        return blocks[2 + r // 2], r % 2
+    return blocks[k + k // 3], r
+
+
+def couple(ids_ref, vectors, blocks, columns, wanted, keep):
     columns[...] = jnp.concatenate(vectors + [jnp.zeros((4, WIDE), F32)], 0).T
     col = ids_ref[MY_COL]
-    acc = jnp.zeros((16, CAM), F32)
-    for k in range(COLS):
-        base = jnp.bitwise_xor(col, k) * SHARE
-        for m in range(SHARE // 16):
-            xs = columns[pl.ds(pl.multiple_of(base + 16 * m, 16), 16), :]
-            for r in range(ROUNDS):
-                if k == 2:
-                    block = blocks[2 + r // 2][r % 2, 16 * m : 16 * m + 16, :]
-                else:
-                    block = blocks[k + k // 3][r, 16 * m : 16 * m + 16, :]
-                acc = acc + block.astype(F32) * xs[:, r : r + 1]
-    return widen(jnp.sum(acc, 0, keepdims=True))
+    for r in range(ROUNDS):
+
+        @pl.when(wanted(r))
+        def _():
+            acc = jnp.zeros((16, CAM), F32)
+            for k in range(COLS):
+                base = jnp.bitwise_xor(col, k) * SHARE
+                ref, at = block_of(blocks, k, r)
+                for m in range(SHARE // 16):
+                    xs = columns[pl.ds(pl.multiple_of(base + 16 * m, 16), 16), r : r + 1]
+                    acc = acc + ref[at, 16 * m : 16 * m + 16, :].astype(F32) * xs
+            keep[r : r + 1, :] = widen(jnp.sum(acc, 0, keepdims=True))
 
 
 def first_step_kernel(
@@ -170,11 +176,14 @@
 
     rhs = vectors[:, :WIDE]
     step, diag = full(0), full(5)
-    near = []
-    for r in range(ROUNDS):
-        x = full(r + 1) * vectors[:, WIDE * (r + 1) : WIDE * (r + 2)]
-        near.append(jnp.where(ids_ref[PARTNER_COLOUR + r] == 0, x, 0.0))
-    coupled = couple(ids_ref, near, (b0, b1, b2, b3, b4), columns)
+    near = [full(r + 1) * vectors[:, WIDE * (r + 1) : WIDE * (r + 2)] for r in range(ROUNDS)]
+    keep = state_ref.at[8:16]
+    keep[...] = jnp.zeros((8, WIDE), F32)
+    couple(
+        ids_ref, near, (b0, b1, b2, b3, b4), columns,
+        lambda r: ids_ref[PARTNER_COLOUR + r] == 0, keep,
+    )
+    coupled = jnp.sum(keep[...], 0, keepdims=True)
     mine = ids_ref[MY_COLOUR]
     x = jnp.where(mine == 0, step * rhs, jnp.where(mine == 1, step * (rhs - coupled), 0.0))
     state_ref[0:1, :] = x
@@ -187,13 +196,18 @@
         out_ref[c] = x
 
 
-def step_kernel(number, has_send, has_recv, *refs):
+def step_kernel(number, has_recv, *refs):
     ids_ref, recv_ref, state_ref = refs[:3]
     blocks = refs[3:8]
-    send_ref = refs[8] if has_send else None
+    tracks = refs[8:-3]
     new_ref, out_ref, columns = refs[-3:]
+    fresh = (number - 1) % COLOURS
     near = [recv_ref[ids_ref[PARTNER + r], :, :WIDE] for r in range(ROUNDS)]
-    coupled = couple(ids_ref, near, blocks, columns)
+    keep = new_ref.at[8:16]
+    keep[...] = state_ref[8:16, :]
+    couple(
+        ids_ref, near, blocks, columns, lambda r: ids_ref[PARTNER_COLOUR + r] == fresh, keep
+    )
     x, rhs, step, diag, elim = (state_ref[i : i + 1, :] for i in range(5))
     mine = ids_ref[MY_COLOUR]
     if has_recv:
@@ -202,22 +216,27 @@
             total = total + recv_ref[c, :, WIDE:]
         elim = jnp.where(mine >= (2 if number > COLOURS else 0), total, elim)
     if number == COLOURS:
-        x, rhs, coupled = 0.25 * x, 0.25 * rhs, 0.25 * coupled
-    resid = rhs - coupled
+        x, rhs = 0.25 * x, 0.25 * rhs
+        keep[...] = 0.25 * keep[...]
+    resid = rhs - jnp.sum(keep[...], 0, keepdims=True)
     if number >= COLOURS:
         resid = resid - diag * x + elim
     x = jnp.where(mine == number % COLOURS, x + step * resid, x)
     for i, v in enumerate((x, rhs, step, diag, elim)):
         new_ref[i : i + 1, :] = v
     if number == 2 * COLOURS - 2:
-        x = jnp.where(mine == COLOURS - 1, x + step * (rhs - diag * x + elim), x)
+        resid = rhs - diag * x + elim
+        for r in range(ROUNDS):
+            done = ids_ref[PARTNER_COLOUR + r] != number % COLOURS
+            resid = resid - jnp.where(done, keep[r : r + 1, :], 0.0)
+        x = jnp.where(mine == COLOURS - 1, x + step * resid, x)
     for c in range(out_ref.shape[0]):
         out_ref[c, :, :WIDE] = x
-    if has_send:
-        out_ref[:, :, WIDE:] = send_ref[...]
-
-
-def last_step_kernel(ids_ref, recv_ref, state_ref, b0, b1, b2, b3, b4, out_ref, columns):
+    if tracks:
+        eliminate(recv_ref, out_ref, *tracks)
+
+
+def last_step_kernel(ids_ref, recv_ref, state_ref, b0, b1, b2, b3, b4, out_ref, columns, keep):
     def total(c):
         v = recv_ref[COLS * c]
         for k in range(1, COLS):
@@ -225,17 +244,22 @@
         return v
 
     near = [total(ids_ref[PARTNER + r]) for r in range(ROUNDS)]
-    coupled = couple(ids_ref, near, (b0, b1, b2, b3, b4), columns)
-    x = total(ids_ref[MY_CLU])
-    x = jnp.where(ids_ref[MY_COLOUR] == COLOURS - 1, x - state_ref[2:3, :] * coupled, x)
+    mine = ids_ref[MY_COLOUR]
+    last = COLOURS - 1
+    keep[...] = jnp.zeros((8, WIDE), F32)
+
+    def wanted(r):
+        return jnp.logical_and(mine == last, ids_ref[PARTNER_COLOUR + r] == last - 1)
+
+    couple(ids_ref, near, (b0, b1, b2, b3, b4), columns, wanted, keep)
+    x = total(ids_ref[MY_CLU]) - state_ref[2:3, :] * jnp.sum(keep[...], 0, keepdims=True)
     out_ref[...] = take_share(x, ids_ref[MY_COL])
 
 
-def elim_kernel(dest_ref, obs_ref, info_ref, recv_ref, jac_ref, out_ref):
+def eliminate(recv_ref, out_ref, dest_ref, obs_ref, info_ref, jac_ref):
     onehot = members(dest_ref)
     obs = obs_ref[...].astype(F32)
-    x = recv_ref[:, 0, :CAM]
-    high, low = two_parts(x)
+    high, low = two_parts(recv_ref[:, 0, :CAM])
     both = jnp.concatenate([high, low], 0)
     along = []
     for b in range(3):
@@ -254,7 +278,7 @@
             NT,
             preferred_element_type=F32,
         )
-    out_ref[:, 0, :] = widen(fold(total))
+    out_ref[:, 0, WIDE:] = widen(fold(total))
 
 
 def shape(*dims, dtype=F32):
@@ -318,43 +342,31 @@
         first_step_kernel,
         in_specs=[smem()] + [vmem()] * 9,
         out_specs=[vmem()] * 3,
-        out_shape=[shape(8, WIDE), shape(CLUSTERS, 1, WIDE), shape(1, SHARE)],
+        out_shape=[shape(16, WIDE), shape(CLUSTERS, 1, WIDE), shape(1, SHARE)],
         scratch_shapes=[columns],
         compiler_params=limit,
         name="first_step",
     )(ids, row, first, second, third, *blocks)
 
-    def eliminate(recv):
+    def update(number, recv, state, has_send=False, has_recv=False):
+        rows = CLUSTERS * COLS if number == 2 * COLOURS - 2 else CLUSTERS
+        extra = (dest, obs, point_info, jac) if has_send else ()
         return pl.pallas_call(
-            elim_kernel,
-            in_specs=[vmem()] * 5,
-            out_specs=vmem(),
-            out_shape=shape(CLUSTERS, 1, WIDE),
-            compiler_params=limit,
-            cost_estimate=pl.CostEstimate(
-                flops=12 * 64 * 1024 * 576, bytes_accessed=1 << 22, transcendentals=0
-            ),
-            name="elim",
-        )(dest, obs, point_info, recv, jac)
-
-    def update(number, recv, state, send=None, has_recv=False):
-        rows = CLUSTERS * COLS if number == 2 * COLOURS - 2 else CLUSTERS
-        return pl.pallas_call(
-            functools.partial(step_kernel, number, send is not None, has_recv),
-            in_specs=[smem()] + [vmem()] * (7 if send is None else 8),
+            functools.partial(step_kernel, number, has_recv),
+            in_specs=[smem()] + [vmem()] * (7 + len(extra)),
             out_specs=[vmem()] * 2,
-            out_shape=[shape(8, WIDE), shape(rows, 1, WIDE if send is None else 2 * WIDE)],
+            out_shape=[shape(16, WIDE), shape(rows, 1, 2 * WIDE if has_send else WIDE)],
             scratch_shapes=[columns],
             compiler_params=limit,
             name="step",
-        )(ids, recv, state, *blocks, *(() if send is None else (send,)))
-
-    recv = over_clu(payload)
-    state, payload = update(2, recv, state, send=eliminate(recv))
+        )(ids, recv, state, *blocks, *extra)
+
+    recv = over_clu(payload)
+    state, payload = update(2, recv, state, has_send=True)
     recv = over_clu(payload)
     state, payload = update(3, recv, state, has_recv=True)
     recv = over_clu(payload)
-    state, payload = update(4, recv, state, send=eliminate(recv))
+    state, payload = update(4, recv, state, has_send=True)
     recv = over_clu(payload)
     state, payload = update(5, recv, state, has_recv=True)
     recv = over_clu(payload)
@@ -365,7 +377,7 @@
         in_specs=[smem()] + [vmem()] * 7,
         out_specs=vmem(),
         out_shape=shape(1, SHARE),
-        scratch_shapes=[columns],
+        scratch_shapes=[columns, pltpu.VMEM((8, WIDE), F32)],
         compiler_params=limit,
         name="last_step",
     )(ids, recv, state, *blocks)

time: 129 us -> 126 us (0.977)
  Pallas kernels: 21.2 us -> 17.3 us
    pallas_call x7 -> x5, Pallas kernels: 11.6 us -> 8.9 us  [update(): pl.pallas_call(functools.partial(step_kernel, number, has_recv), in_specs...]
where the time goes in v5:
time: 126 us; the launch traced here: 125 us
  blocking collectives  76.8 us (61%)
  starting transfers between devices  18.8 us (15%)
  Pallas kernels  17.3 us (14%)
  waiting for transfers between devices  9.37 us (7%)
  local copies, waits for them, and re-layouts  2.4 us (2%)
    all_to_all x5, blocking collectives, over_clu(): return lax.all_to_all(v, 'clu', split_axis=0, concat_axis=0, tiled=True)  59.4 us
    all_to_all x1, blocking collectives, per_device(): lax.all_to_all(payload, ('clu', 'col'), split_axis=0, concat_axis=0, tile...  17.4 us
    all_to_all x1, starting transfers between devices, over_clu(): return lax.all_to_all(v, 'clu', split_axis=0, concat_axis=0, tiled=True)  9.4 us
    pallas_call x5, Pallas kernels, update(): pl.pallas_call(functools.partial(step_kernel, number, has_recv), in_specs...  8.9 us
    ppermute x4, starting transfers between devices, swap(): return lax.ppermute(v, 'col', [(i, i ^ k) for i in range(COLS)])  6.04 us
    all_to_all x1, waiting for transfers between devices, over_clu(): return lax.all_to_all(v, 'clu', split_axis=0, concat_axis=0, tiled=True)  4.86 us
    pallas_call x1, Pallas kernels, per_device(): pl.pallas_call(rhs_kernel, grid=(3,), in_specs=[smem(), smem(), whole(1,...  4.77 us
    ppermute x3, starting transfers between devices, over_col(): lax.ppermute(v, 'col', [(i, i ^ k) for i in range(COLS)])  3.38 us
  transfers between devices with their start and end apart: 8, of which 6 were waited for; matrix products, arithmetic and copies ran while one was open for 1% of the time, Pallas kernels for 4%

profile of v5, /device:TPU:1, one launch (start us, length us, event | category | flops | bytes accessed | tf_op | source)
XLA Modules:
  0.0 125.5 jit_solution(8787458381175444099)
XLA Ops:
  0.6 3.4 %collective-permute-start.5 = (bf16[4,144,576]{2,1,0:T(8,128)(2,1)}, bf16[4,144,576]{2,1,0:T(8,128)(2,1)S(1)}, u32[]{:S(2)}, u32[]{:S(2)}) collective-permute-start(bf16[4,144,576]{2,1,0:T(8,128)(2,1)} %bitcast.6), channel_id=1, source_target_pairs={{0,3},{1,2},{2,1},{3,0},{4,7},{5,6},{6,5},{7,4},{8,11},{9,10},{10,... | collective-permute-start | bytes 1990664 | tf_op jit(solution)/shard_map/ppermute | solution.py:301
  4.0 4.8 %rhs.1 = (f32[32,1,3584]{2,1,0:T(1,128)}, s32[16]{0:T(128)}) custom-call(s32[32]{0:T(128)} %cc_ref.1, s32[4,4,32]{2,1,0:T(4,128)} %rp_ref.1, s32[1,1024]{1,0:T(1,128)} %bitcast.18, s32[1,1024]{1,0:T(1,128)} %bitcast.21, f32[3,3,1024]{2,1,0:T(4,128)} %refs_10_.3, f32[3,1024]{1,0:T(4,128)} %grad_ref.1, bf16[1728,1024]{1,0:T(8,128)(2,1)} %bitcast.15, ...), custom_call_target="tpu_custom_call" | custom-call | tf_op jit(solution)/shard_map/rhs/pallas_call | solution.py:308
  8.9 9.4 %all-to-all-start = ((f32[32,1,3584]{2,1,0:T(1,128)}), f32[32,1,3584]{2,1,0:T(1,128)S(1)}, u32[]{:S(2)}, u32[]{:S(2)}) async-start(f32[32,1,3584]{2,1,0:T(1,128)} %get-tuple-element.18), calls=%async_computation | async-start | bytes 917504 | tf_op jit(solution)/shard_map/all_to_all | solution.py:328
  18.3 1.7 %collective-permute-done.5.b4.refs_7_ = bf16[4,144,576]{2,1,0:T(8,128)(2,1)S(1)} collective-permute-done((bf16[4,144,576]{2,1,0:T(8,128)(2,1)}, bf16[4,144,576]{2,1,0:T(8,128)(2,1)S(1)}, u32[]{:S(2)}, u32[]{:S(2)}) %collective-permute-start.5) | collective-permute-done | bytes 663584 | tf_op jit(solution)/shard_map/ppermute | solution.py:301
  20.0 0.8 slice.9
  22.0 2.3 %collective-permute-start.4 = (bf16[2,144,576]{2,1,0:T(8,128)(2,1)}, bf16[2,144,576]{2,1,0:T(8,128)(2,1)S(1)}, u32[]{:S(2)}, u32[]{:S(2)}) collective-permute-start(bf16[2,144,576]{2,1,0:T(8,128)(2,1)} %slice.8), channel_id=1, source_target_pairs={{0,3},{1,2},{2,1},{3,0},{4,7},{5,6},{6,5},{7,4},{8,11},{9,10},{10,... | collective-permute-start | bytes 995336 | tf_op jit(solution)/shard_map/ppermute | solution.py:301
  24.4 4.9 %all-to-all-done.recv_ref = f32[32,1,3584]{2,1,0:T(1,128)S(1)} async-done(((f32[32,1,3584]{2,1,0:T(1,128)}), f32[32,1,3584]{2,1,0:T(1,128)S(1)}, u32[]{:S(2)}, u32[]{:S(2)}) %all-to-all-start) | async-done | bytes 458784 | tf_op jit(solution)/shard_map/all_to_all | solution.py:328
  29.2 0.8 copy-done.5
  30.7 0.9 collective-permute-start.2
  31.6 2.5 %collective-permute-start.1 = (f32[1,4736]{1,0:T(1,128)S(1)}, f32[1,4736]{1,0:T(1,128)S(1)}, u32[]{:S(2)}, u32[]{:S(2)}) collective-permute-start(f32[1,4736]{1,0:T(1,128)S(1)} %gather.1.v0), channel_id=1, source_target_pairs={{0,2},{1,3},{2,0},{3,1},{4,6},{5,7},{6,4},{7,5},{8,10},{9,11},{10,... | collective-permute-start | bytes 56840 | tf_op jit(solution)/shard_map/ppermute | solution.py:298
  34.5 1.2 collective-permute-done.1.v2
  35.7 0.9 collective-permute-done.v1
  36.7 1.7 %first_step.1 = (f32[16,640]{1,0:T(8,128)S(1)}, f32[32,1,640]{2,1,0:T(1,128)S(1)}, f32[1,144]{1,0:T(1,128)}) custom-call(s32[16]{0:T(128)S(1)} %copy-done.5, f32[1,4736]{1,0:T(1,128)S(1)} %gather.1.v0, f32[1,4736]{1,0:T(1,128)S(1)} %collective-permute-done.v1, f32[1,4736]{1,0:T(1,128)S(1)} %collective-permute-done.1.v2, ...), custom_call_target="tpu_custom_call" | custom-call | tf_op jit(solution)/shard_map/first_step/pallas_call | solution.py:341
  38.3 14.0 %all_to_all.35.refs_1_ = f32[32,1,640]{2,1,0:T(1,128)S(1)} all-to-all(f32[32,1,640]{2,1,0:T(1,128)S(1)} %get-tuple-element.19), channel_id=1, replica_groups=mesh['clu'=32,'col'=4] {'clu'}, dimensions={0} | all-to-all | bytes 163840 | tf_op jit(solution)/shard_map/all_to_all | solution.py:328
  52.4 2.8 %step.5 = (f32[16,640]{1,0:T(8,128)S(1)}, f32[32,1,1280]{2,1,0:T(1,128)S(1)}) custom-call(s32[16]{0:T(128)S(1)} %copy-done.6, f32[32,1,640]{2,1,0:T(1,128)S(1)} %all_to_all.35.refs_1_, f32[16,640]{1,0:T(8,128)S(1)} %get-tuple-element.20.refs_2_, bf16[4,144,576]{2,1,0:T(8,128)(2,1)S(1)} %bitcast.9, ...), custom_call_target="tpu_custom_call" | custom-call | tf_op jit(solution)/shard_map/step/pallas_call | solution.py:354
  55.2 11.8 %all_to_all.36.refs_1_ = f32[32,1,1280]{2,1,0:T(1,128)S(1)} all-to-all(f32[32,1,1280]{2,1,0:T(1,128)S(1)} %get-tuple-element.21), channel_id=1, replica_groups=mesh['clu'=32,'col'=4] {'clu'}, dimensions={0} | all-to-all | bytes 327680 | tf_op jit(solution)/shard_map/all_to_all | solution.py:328
  67.1 1.2 step.6
  68.3 11.0 %all_to_all.37.refs_1_ = f32[32,1,640]{2,1,0:T(1,128)S(1)} all-to-all(f32[32,1,640]{2,1,0:T(1,128)S(1)} %get-tuple-element.23), channel_id=1, replica_groups=mesh['clu'=32,'col'=4] {'clu'}, dimensions={0} | all-to-all | bytes 163840 | tf_op jit(solution)/shard_map/all_to_all | solution.py:328
  79.3 3.1 %step.7 = (f32[16,640]{1,0:T(8,128)S(1)}, f32[32,1,1280]{2,1,0:T(1,128)S(1)}) custom-call(s32[16]{0:T(128)S(1)} %copy-done.6, f32[32,1,640]{2,1,0:T(1,128)S(1)} %all_to_all.37.refs_1_, f32[16,640]{1,0:T(8,128)S(1)} %get-tuple-element.24.refs_2_, bf16[4,144,576]{2,1,0:T(8,128)(2,1)S(1)} %bitcast.11, ...), custom_call_target="tpu_custom_call" | custom-call | tf_op jit(solution)/shard_map/step/pallas_call | solution.py:354
  82.3 11.6 %all_to_all.38.refs_1_ = f32[32,1,1280]{2,1,0:T(1,128)S(1)} all-to-all(f32[32,1,1280]{2,1,0:T(1,128)S(1)} %get-tuple-element.25), channel_id=1, replica_groups=mesh['clu'=32,'col'=4] {'clu'}, dimensions={0} | all-to-all | bytes 327680 | tf_op jit(solution)/shard_map/all_to_all | solution.py:328
  93.9 1.0 step.8
  94.9 11.0 %all_to_all.39.refs_1_ = f32[32,1,640]{2,1,0:T(1,128)S(1)} all-to-all(f32[32,1,640]{2,1,0:T(1,128)S(1)} %get-tuple-element.27), channel_id=1, replica_groups=mesh['clu'=32,'col'=4] {'clu'}, dimensions={0} | all-to-all | bytes 163840 | tf_op jit(solution)/shard_map/all_to_all | solution.py:328
  106.7 17.4 %all_to_all.40.recv_ref = f32[128,1,640]{2,1,0:T(1,128)S(1)} all-to-all(f32[128,1,640]{2,1,0:T(1,128)S(1)} %get-tuple-element.29), channel_id=1, replica_groups=mesh['clu'=32,'col'=4] {'clu','col'}, dimensions={0} | all-to-all | bytes 655360 | tf_op jit(solution)/shard_map/all_to_all | solution.py:374
  124.1 1.4 %last_step.1 = f32[1,144]{1,0:T(1,128)} custom-call(s32[16]{0:T(128)S(1)} %copy-done.6, f32[128,1,640]{2,1,0:T(1,128)S(1)} %all_to_all.40.recv_ref, f32[16,640]{1,0:T(8,128)S(1)} %get-tuple-element.30.state_ref, bf16[4,144,576]{2,1,0:T(8,128)(2,1)S(1)} %bitcast.14, bf16[4,144,576]{2,1,0:T(8,128)(2,1)S(1)} %collective-permute-done.3.b1.refs_4_, ...), custom_call_target="tpu_custom_call" | custom-call | tf_op jit(solution)/shard_map/last_step/pallas_call | solution.py:375
  (23 shorter events, 3.2 us)
Async XLA Ops:
  0.6 36.0 %copy-start = (bf16[1,4,576,144]{2,3,1,0:T(8,128)(2,1)S(1)}, bf16[1,4,576,144]{2,3,1,0:T(8,128)(2,1)}, u32[]{:S(2)}) copy-start(bf16[1,4,576,144]{2,3,1,0:T(8,128)(2,1)} %param.19) | copy-start | bytes 1990660
  0.6 19.4 %collective-permute-start.5 = (bf16[4,144,576]{2,1,0:T(8,128)(2,1)}, bf16[4,144,576]{2,1,0:T(8,128)(2,1)S(1)}, u32[]{:S(2)}, u32[]{:S(2)}) collective-permute-start(bf16[4,144,576]{2,1,0:T(8,128)(2,1)} %bitcast.6), channel_id=1, source_target_pairs={{0,3},{1,2},{2,1},{3,0},{4,7},{5,6},{6,5},{7,4},{8,11},{9,10},{10,... | collective-permute-start | bytes 1990664 | tf_op jit(solution)/shard_map/ppermute | solution.py:301
  4.0 17.2 %collective-permute-start.3 = (bf16[4,144,576]{2,1,0:T(8,128)(2,1)}, bf16[4,144,576]{2,1,0:T(8,128)(2,1)S(1)}, u32[]{:S(2)}, u32[]{:S(2)}) collective-permute-start(bf16[4,144,576]{2,1,0:T(8,128)(2,1)} %bitcast.7), channel_id=1, source_target_pairs={{0,1},{1,0},{2,3},{3,2},{4,5},{5,4},{6,7},{7,6},{8,9},{9,8},{10,11... | collective-permute-start | bytes 1990664 | tf_op jit(solution)/shard_map/ppermute | solution.py:301
  8.8 43.5 %copy-start.2 = (f32[3,3,1024]{2,1,0:T(4,128)S(1)}, f32[3,3,1024]{2,1,0:T(4,128)}, u32[]{:S(2)}) copy-start(f32[3,3,1024]{2,1,0:T(4,128)} %refs_10_.3) | copy-start | bytes 110596
  8.8 43.5 %copy-start.3 = (s32[1024,1]{0,1:T(1,128)S(1)}, s32[1024,1]{0,1:T(1,128)}, u32[]{:S(2)}) copy-start(s32[1024,1]{0,1:T(1,128)} %param.11) | copy-start | bytes 12292
  8.8 43.5 %copy-start.4 = (s32[1024]{0:T(1024)S(1)}, s32[1024]{0:T(1024)}, u32[]{:S(2)}) copy-start(s32[1024]{0:T(1024)} %param.12) | copy-start | bytes 12292
  8.8 43.5 %copy-start.6 = (s32[16]{0:T(128)S(1)}, s32[16]{0:T(128)}, u32[]{:S(2)}) copy-start(s32[16]{0:T(128)} %get-tuple-element.17.ids_ref.refs_0_) | copy-start | bytes 196
  8.9 20.4 %all-to-all-start = ((f32[32,1,3584]{2,1,0:T(1,128)}), f32[32,1,3584]{2,1,0:T(1,128)S(1)}, u32[]{:S(2)}, u32[]{:S(2)}) async-start(f32[32,1,3584]{2,1,0:T(1,128)} %get-tuple-element.18), calls=%async_computation | async-start | bytes 917504 | tf_op jit(solution)/shard_map/all_to_all | solution.py:328
  20.8 15.9 %collective-permute-start.6 = (bf16[2,144,576]{2,1,0:T(8,128)(2,1)}, bf16[2,144,576]{2,1,0:T(8,128)(2,1)S(1)}, u32[]{:S(2)}, u32[]{:S(2)}) collective-permute-start(bf16[2,144,576]{2,1,0:T(8,128)(2,1)} %slice.9), channel_id=1, source_target_pairs={{0,1},{1,0},{2,3},{3,2},{4,5},{5,4},{6,7},{7,6},{8,9},{9,8},{10,11... | collective-permute-start | bytes 995336 | tf_op jit(solution)/shard_map/ppermute | solution.py:301
  22.0 14.6 %collective-permute-start.4 = (bf16[2,144,576]{2,1,0:T(8,128)(2,1)}, bf16[2,144,576]{2,1,0:T(8,128)(2,1)S(1)}, u32[]{:S(2)}, u32[]{:S(2)}) collective-permute-start(bf16[2,144,576]{2,1,0:T(8,128)(2,1)} %slice.8), channel_id=1, source_target_pairs={{0,3},{1,2},{2,1},{3,0},{4,7},{5,6},{6,5},{7,4},{8,11},{9,10},{10,... | collective-permute-start | bytes 995336 | tf_op jit(solution)/shard_map/ppermute | solution.py:301
  29.2 23.1 %copy-start.1 = (bf16[1024,1728]{0,1:T(8,128)(2,1)S(1)}, bf16[1024,1728]{0,1:T(8,128)(2,1)}, u32[]{:S(2)}) copy-start(bf16[1024,1728]{0,1:T(8,128)(2,1)} %param.13) | copy-start | bytes 10616836
  29.2 0.8 copy-start.5
  30.7 3.9 %collective-permute-start.2 = (f32[1,4736]{1,0:T(1,128)S(1)}, f32[1,4736]{1,0:T(1,128)S(1)}, u32[]{:S(2)}, u32[]{:S(2)}) collective-permute-start(f32[1,4736]{1,0:T(1,128)S(1)} %gather.1.v0), channel_id=1, source_target_pairs={{0,3},{1,2},{2,1},{3,0},{4,7},{5,6},{6,5},{7,4},{8,11},{9,10},{10,... | collective-permute-start | bytes 56840 | tf_op jit(solution)/shard_map/ppermute | solution.py:298
  31.6 4.1 %collective-permute-start.1 = (f32[1,4736]{1,0:T(1,128)S(1)}, f32[1,4736]{1,0:T(1,128)S(1)}, u32[]{:S(2)}, u32[]{:S(2)}) collective-permute-start(f32[1,4736]{1,0:T(1,128)S(1)} %gather.1.v0), channel_id=1, source_target_pairs={{0,2},{1,3},{2,0},{3,1},{4,6},{5,7},{6,4},{7,5},{8,10},{9,11},{10,... | collective-permute-start | bytes 56840 | tf_op jit(solution)/shard_map/ppermute | solution.py:298
  34.0 2.6 %collective-permute-start = (f32[1,4736]{1,0:T(1,128)S(1)}, f32[1,4736]{1,0:T(1,128)S(1)}, u32[]{:S(2)}, u32[]{:S(2)}) collective-permute-start(f32[1,4736]{1,0:T(1,128)S(1)} %gather.1.v0), channel_id=1, source_target_pairs={{0,1},{1,0},{2,3},{3,2},{4,5},{5,4},{6,7},{7,6},{8,9},{9,8},{10,11... | collective-permute-start | bytes 56840 | tf_op jit(solution)/shard_map/ppermute | solution.py:298

commit v6 on v3

v6 whole, which is shorter than its diff:
```python
import functools

import jax
import jax.numpy as jnp
from jax import lax
from jax.experimental import pallas as pl
from jax.experimental.pallas import tpu as pltpu
from jax.sharding import PartitionSpec as P

CLUSTERS = 32
ROUNDS = 4
COLOURS = 4
COLS = 4
CAM = 576
SHARE = 144
WIDE = 640
SLOT = 256
PAIR = 384
TABLE = 2 * SHARE
TRK = 1024
NT = (((1,), (1,)), ((), ()))
NN = (((1,), (0,)), ((), ()))

MY_COLOUR, PARTNER, PARTNER_COLOUR = 0, 1, 5
LANES = 128

F32 = jnp.float32
BF16 = jnp.bfloat16


def smem():
    return pl.BlockSpec(memory_space=pltpu.SMEM)


def vmem():
    return pl.BlockSpec(memory_space=pltpu.VMEM)


def two_parts(v):
    high = v.astype(BF16)
    low = (v - high.astype(F32)).astype(BF16)
    return high, low


def widen(v, width=WIDE):
    return jnp.concatenate([v, jnp.zeros((v.shape[0], width - v.shape[1]), F32)], 1)


def place_share(share, col):
    total = jnp.zeros((1, WIDE), F32)
    for at in range(COLS):
        pieces = []
        if at:
            pieces.append(jnp.zeros((1, SHARE * at), F32))
        pieces.append(share)
        pieces.append(jnp.zeros((1, WIDE - SHARE * (at + 1)), F32))
        total = total + jnp.where(col == at, jnp.concatenate(pieces, 1), 0.0)
    return total


def take_share(vector, col):
    total = jnp.zeros((1, SHARE), F32)
    for at in range(COLS):
        total = total + jnp.where(col == at, vector[:, SHARE * at : SHARE * (at + 1)], 0.0)
    return total


def members(dest_ref):
    lanes = lax.broadcasted_iota(jnp.int32, (CLUSTERS, TRK), 0)
    return (lanes == dest_ref[...]).astype(F32)


def scatter_rows(onehot, row):
    high, low = two_parts(row)
    return jnp.concatenate(
        [onehot * high.astype(F32), onehot * low.astype(F32)], 0
    ).astype(BF16)


def fold(both):
    return both[:CLUSTERS] + both[CLUSTERS:]


def rhs_kernel(
    cc_ref, rp_ref, dest_ref, obs_ref, info_ref, grad_ref, jac_ref, cg_ref, step_ref, diag_ref,
    out_ref, total,
):
    a = pl.program_id(0)
    me = lax.axis_index("clu")
    col = lax.axis_index("col")
    obs = obs_ref[...].astype(F32)
    q = jnp.zeros((1, TRK), F32)
    for b in range(3):
        q = q + obs * info_ref[0, b : b + 1, :] * grad_ref[b : b + 1, :]
    part = fold(
        lax.dot_general(
            scatter_rows(members(dest_ref), q), jac_ref[...], NT, preferred_element_type=F32
        )
    )

    @pl.when(a == 0)
    def _():
        rows = lax.broadcasted_iota(jnp.int32, (CLUSTERS, WIDE), 0)
        total[...] = jnp.where(rows == me, place_share(cg_ref[...], col), 0.0)

    total[:, :CAM] = total[:, :CAM] - part

    @pl.when(a == 2)
    def _():
        share = widen(jnp.concatenate([step_ref[...], diag_ref[...]], 1), PAIR)
        lanes = lax.broadcasted_iota(jnp.int32, (1, PAIR), 1) - TABLE
        for c in range(CLUSTERS):
            colour = cc_ref[c]
            row = jnp.where(lanes == MY_COLOUR, colour.astype(F32), share)
            out_ref[c, :, 0:WIDE] = total[c : c + 1, :]
            for r in range(ROUNDS):
                p = rp_ref[colour, r, c]
                out_ref[c, :, WIDE * (r + 1) : WIDE * (r + 2)] = total[pl.ds(p, 1), :]
                row = jnp.where(lanes == PARTNER + r, p.astype(F32), row)
                row = jnp.where(lanes == PARTNER_COLOUR + r, cc_ref[p].astype(F32), row)
            out_ref[c, :, WIDE * 5 :] = row


def gather_kernel(recv_ref, ready_ref, out_ref, ids_ref):
    del ready_ref
    vectors = recv_ref[0, :, : WIDE * 5]
    for c in range(1, CLUSTERS):
        vectors = vectors + recv_ref[c, :, : WIDE * 5]
    out_ref[:, : WIDE * 5] = vectors
    table = recv_ref[0, :, WIDE * 5 + TABLE :].astype(jnp.int32)
    ids_ref[...] = jnp.concatenate(
        [table, jnp.zeros((1, LANES - table.shape[1]), jnp.int32)], 1
    )
    sources = [lax.axis_index("clu")] + [ids_ref[0, PARTNER + r] for r in range(ROUNDS)]
    shares = [recv_ref[c, :, WIDE * 5 : WIDE * 5 + SHARE] for c in sources]
    shares.append(recv_ref[sources[0], :, WIDE * 5 + SHARE : WIDE * 5 + 2 * SHARE])
    for at, share in enumerate(shares):
        out_ref[:, WIDE * 5 + SLOT * at : WIDE * 5 + SLOT * (at + 1)] = widen(share, SLOT)


def couple(vectors, blocks_ref):
    row = jnp.concatenate(vectors, 1)
    high = row.astype(BF16).astype(F32)
    middle = (row - high).astype(BF16).astype(F32)
    low = row - high - middle
    parts = jnp.concatenate([high, middle, low, jnp.zeros((13, ROUNDS * WIDE), F32)], 0)
    out = jnp.dot(
        parts.astype(BF16),
        blocks_ref[...].reshape(ROUNDS * WIDE, CAM),
        preferred_element_type=F32,
    )
    return widen(jnp.sum(out, 0, keepdims=True))


def lay_out(pieces, blocks_ref, sems):
    col, core = lax.axis_index("col"), lax.rem(lax.axis_index("clu"), 2)
    copies = []
    for i, (piece, away) in enumerate(zip(pieces, (0, 1 + 2 * core, 2, 3 - 2 * core))):
        at = pl.multiple_of(jnp.bitwise_xor(col, away) * SHARE, 16)
        copies.append(
            pltpu.make_async_copy(piece, blocks_ref.at[:, pl.ds(at, SHARE), :], sems.at[i])
        )
        copies[i].start()
    return copies


def first_step_kernel(
    ids_ref, v0, v1, v2, v3, b0, b1, b2, b3, state_ref, out_ref, rhs_ref, blocks_ref, sems
):
    copies = lay_out((b0, b1, b2, b3), blocks_ref, sems)
    blocks_ref[:, CAM:, :] = jnp.zeros((ROUNDS, WIDE - CAM, CAM), BF16)
    col = lax.axis_index("col")
    rows = [v[...] for v in (v0, v1, v2, v3)]
    vectors = (rows[0] + rows[1] + rows[2] + rows[3])[:, : WIDE * 5]
    shares = []
    for at in range(COLS):
        share = jnp.zeros((1, SLOT * 6), F32)
        for k in range(COLS):
            share = jnp.where(jnp.bitwise_xor(col, k) == at, rows[k][:, WIDE * 5 :], share)
        shares.append(share)

    def full(v):
        return widen(jnp.concatenate([s[:, SLOT * v : SLOT * v + SHARE] for s in shares], 1))

    rhs = vectors[:, :WIDE]
    step, diag = full(0), full(5)
    near = []
    for r in range(ROUNDS):
        x = full(r + 1) * vectors[:, WIDE * (r + 1) : WIDE * (r + 2)]
        near.append(jnp.where(ids_ref[0, PARTNER_COLOUR + r] == 0, x, 0.0))
    for copy in copies:
        copy.wait()
    coupled = couple(near, blocks_ref)
    mine = ids_ref[0, MY_COLOUR]
    x = jnp.where(mine == 0, step * rhs, jnp.where(mine == 1, step * (rhs - coupled), 0.0))
    state_ref[0:1, :] = x
    state_ref[1:2, :] = rhs
    state_ref[2:3, :] = step
    state_ref[3:4, :] = diag
    state_ref[4:8, :] = jnp.zeros((4, WIDE), F32)
    rhs_ref[...] = take_share(rhs, col)
    for c in range(CLUSTERS):
        out_ref[c] = x


def step_kernel(number, has_recv, *refs):
    ids_ref, recv_ref, state_ref, blocks_ref = refs[:4]
    tracks = refs[4:-2]
    new_ref, out_ref = refs[-2:]
    near = [recv_ref[ids_ref[0, PARTNER + r], :, :WIDE] for r in range(ROUNDS)]
    coupled = couple(near, blocks_ref)
    x, rhs, step, diag, elim = (state_ref[i : i + 1, :] for i in range(5))
    mine = ids_ref[0, MY_COLOUR]
    if has_recv:
        total = recv_ref[0, :, WIDE:]
        for c in range(1, CLUSTERS):
            total = total + recv_ref[c, :, WIDE:]
        elim = jnp.where(mine >= (2 if number > COLOURS else 0), total, elim)
    if number == COLOURS:
        x, rhs, coupled = 0.25 * x, 0.25 * rhs, 0.25 * coupled
    resid = rhs - coupled
    if number >= COLOURS:
        resid = resid - diag * x + elim
    x = jnp.where(mine == number % COLOURS, x + step * resid, x)
    for i, v in enumerate((x, rhs, step, diag, elim)):
        new_ref[i : i + 1, :] = v
    if number == 2 * COLOURS - 2:
        x = jnp.where(mine == COLOURS - 1, x + step * (rhs - diag * x + elim), x)
    for c in range(out_ref.shape[0]):
        out_ref[c, :, :WIDE] = x
    if tracks:
        eliminate(recv_ref, out_ref, *tracks)


def last_step_kernel(ids_ref, recv_ref, state_ref, blocks_ref, out_ref):
    def total(c):
        v = recv_ref[COLS * c]
        for k in range(1, COLS):
            v = v + recv_ref[COLS * c + k]
        return v

    coupled = couple([total(ids_ref[0, PARTNER + r]) for r in range(ROUNDS)], blocks_ref)
    x = total(lax.axis_index("clu"))
    x = jnp.where(ids_ref[0, MY_COLOUR] == COLOURS - 1, x - state_ref[2:3, :] * coupled, x)
    out_ref[...] = take_share(x, lax.axis_index("col"))


def eliminate(recv_ref, out_ref, dest_ref, obs_ref, info_ref, jac_ref):
    onehot = members(dest_ref)
    obs = obs_ref[...].astype(F32)
    high, low = two_parts(recv_ref[:, 0, :CAM])
    both = jnp.concatenate([high, low], 0)
    along = []
    for b in range(3):
        every = lax.dot_general(
            both, jac_ref[CAM * b : CAM * (b + 1), :], NN, preferred_element_type=F32
        )
        along.append(jnp.sum(fold(every) * onehot, 0, keepdims=True))
    total = jnp.zeros((2 * CLUSTERS, CAM), F32)
    for a in range(3):
        u = jnp.zeros((1, TRK), F32)
        for b in range(3):
            u = u + obs * info_ref[a, b : b + 1, :] * along[b]
        total = total + lax.dot_general(
            scatter_rows(onehot, u),
            jac_ref[CAM * a : CAM * (a + 1), :],
            NT,
            preferred_element_type=F32,
        )
    out_ref[:, 0, WIDE:] = widen(fold(total))


def shape(*dims, dtype=F32):
    return jax.ShapeDtypeStruct(dims, dtype)


def per_device(
    track_dest, obs_count, track_jac, point_info, point_grad, camera_grad, camera_diag,
    step_scale, covis_blocks, cluster_colour, round_partner,
):
    dest = jnp.transpose(track_dest)
    obs = obs_count[None, :]
    jac = jnp.transpose(track_jac)
    own = jnp.transpose(covis_blocks[0], (0, 2, 1))

    def over_col(v):
        return [v] + [lax.ppermute(v, "col", [(i, i ^ k) for i in range(COLS)]) for k in (1, 3, 2)]

    def swap(v, even, odd):
        pairs = []
        for c in range(CLUSTERS):
            for i in range(COLS):
                pairs.append((COLS * c + i, COLS * c + (i ^ (odd if c % 2 else even))))
        return lax.ppermute(v, ("clu", "col"), pairs)

    near, other = swap(own, 1, 3), swap(own, 3, 1)
    limit = pltpu.CompilerParams(vmem_limit_bytes=24 << 20)
    large = pltpu.CompilerParams(vmem_limit_bytes=56 << 20)

    whole = lambda *block: pl.BlockSpec(block, lambda a: (0,) * len(block))
    payload = pl.pallas_call(
        rhs_kernel,
        grid=(3,),
        in_specs=[
            smem(), smem(), whole(1, TRK), whole(1, TRK),
            pl.BlockSpec((1, 3, TRK), lambda a: (a, 0, 0)), whole(3, TRK),
            pl.BlockSpec((CAM, TRK), lambda a: (a, 0)), whole(1, SHARE), whole(1, SHARE),
            whole(1, SHARE),
        ],
        out_specs=whole(CLUSTERS, 1, 5 * WIDE + PAIR),
        out_shape=shape(CLUSTERS, 1, 5 * WIDE + PAIR),
        scratch_shapes=[pltpu.VMEM((CLUSTERS, WIDE), F32)],
        compiler_params=large,
        name="rhs",
    )(
        cluster_colour, round_partner, dest, obs, point_info, point_grad, jac,
        camera_grad, step_scale, camera_diag,
    )

    pieces = [own, near, swap(near, 3, 1), other]

    def over_clu(v):
        return lax.all_to_all(v, "clu", split_axis=0, concat_axis=0, tiled=True)

    recv = over_clu(payload)
    row, ids = pl.pallas_call(
        gather_kernel,
        in_specs=[vmem(), pl.BlockSpec(memory_space=pl.ANY)],
        out_specs=[vmem()] * 2,
        out_shape=[shape(1, 5 * WIDE + 6 * SLOT), shape(1, LANES, dtype=jnp.int32)],
        compiler_params=limit,
        cost_estimate=pl.CostEstimate(
            flops=6 * 10**9, bytes_accessed=1 << 19, transcendentals=0
        ),
        name="gather",
    )(recv, other)
    row, first, third, second = over_col(row)
    state, payload, reduced_rhs, blocks = pl.pallas_call(
        first_step_kernel,
        in_specs=[vmem()] * 5 + [pl.BlockSpec(memory_space=pl.ANY)] * 4,
        out_specs=[vmem()] * 4,
        out_shape=[
            shape(8, WIDE), shape(CLUSTERS, 1, WIDE), shape(1, SHARE),
            shape(ROUNDS, WIDE, CAM, dtype=BF16),
        ],
        scratch_shapes=[pltpu.SemaphoreType.DMA((COLS,))],
        compiler_params=limit,
        name="first_step",
    )(ids, row, first, second, third, *pieces)

    def update(number, recv, state, has_send=False, has_recv=False):
        rows = CLUSTERS * COLS if number == 2 * COLOURS - 2 else CLUSTERS
        extra = (dest, obs, point_info, jac) if has_send else ()
        return pl.pallas_call(
            functools.partial(step_kernel, number, has_recv),
            in_specs=[vmem()] * (4 + len(extra)),
            out_specs=[vmem()] * 2,
            out_shape=[shape(8, WIDE), shape(rows, 1, 2 * WIDE if has_send else WIDE)],
            compiler_params=limit,
            name="step",
        )(ids, recv, state, blocks, *extra)

    recv = over_clu(payload)
    state, payload = update(2, recv, state, has_send=True)
    recv = over_clu(payload)
    state, payload = update(3, recv, state, has_recv=True)
    recv = over_clu(payload)
    state, payload = update(4, recv, state, has_send=True)
    recv = over_clu(payload)
    state, payload = update(5, recv, state, has_recv=True)
    recv = over_clu(payload)
    state, payload = update(6, recv, state)
    recv = lax.all_to_all(payload, ("clu", "col"), split_axis=0, concat_axis=0, tiled=True)
    solution = pl.pallas_call(
        last_step_kernel,
        in_specs=[vmem()] * 4,
        out_specs=vmem(),
        out_shape=shape(1, SHARE),
        compiler_params=limit,
        name="last_step",
    )(ids, recv, state, blocks)
    return solution, reduced_rhs


def solution(mesh):
    in_specs = (
        P(("clu", "col"), None),
        P(("clu", "col")),
        P(("clu", "col"), None),
        P(None, None, ("clu", "col")),
        P(None, ("clu", "col")),
        P("clu", "col"),
        P("clu", "col"),
        P("clu", "col"),
        P("clu", None, None, "col"),
        P(),
        P(),
    )
    out_specs = (P("clu", "col"), P("clu", "col"))
    return jax.shard_map(
        per_device, mesh=mesh, in_specs=in_specs, out_specs=out_specs, check_vma=False
    )
```

time: 136 us -> 122 us (0.90)
  blocking collectives: 101 us -> 76.9 us
  starting transfers between devices: 7.35 us -> 17.4 us
  waiting for transfers between devices: 4.02 us -> 11.9 us
  Pallas kernels: 21.3 us -> 15.1 us
    all_to_all x6 -> x5, blocking collectives: 83.9 us -> 59.5 us  [over_clu(): return lax.all_to_all(v, 'clu', split_axis=0, concat_axis=0, tiled=True)]
    all_to_all x0 -> x1, waiting for transfers between devices: none -> 10.1 us  [over_clu(): return lax.all_to_all(v, 'clu', split_axis=0, concat_axis=0, tiled=True)]
    all_to_all x0 -> x1, starting transfers between devices: none -> 9.86 us  [over_clu(): return lax.all_to_all(v, 'clu', split_axis=0, concat_axis=0, tiled=True)]
    pallas_call x10 -> x8, Pallas kernels: 16.3 us -> 10.3 us  [the longest x5 7.16 us: update(): pl.pallas_call(functools.partial(step_kernel, number, has_recv), in_specs...]
    ppermute x0 -> x3, starting transfers between devices: none -> 4.16 us  [swap(): return lax.ppermute(v, ('clu', 'col'), pairs)]
    ppermute x6 -> x3, starting transfers between devices: 7.35 us -> 3.35 us  [over_col(): lax.ppermute(v, 'col', [(i, i ^ k) for i in range(COLS)])]
    ppermute x6 -> x3, waiting for transfers between devices: 4.02 us -> 1.76 us  [over_col(): lax.ppermute(v, 'col', [(i, i ^ k) for i in range(COLS)])]
  transfers between devices with their start and end apart: 6 -> 7, of which waited for: 3 -> 3; matrix products, arithmetic and copies ran while one was open for 0% -> 0% of each run, Pallas kernels for 4% -> 4%
where the time goes in v6:
time: 122 us
  blocking collectives  76.9 us (63%)
  starting transfers between devices  17.4 us (14%)
  Pallas kernels  15.1 us (12%)
  waiting for transfers between devices  11.9 us (10%)
    all_to_all x5, blocking collectives, over_clu(): return lax.all_to_all(v, 'clu', split_axis=0, concat_axis=0, tiled=True)  59.5 us
    all_to_all x1, blocking collectives, per_device(): lax.all_to_all(payload, ('clu', 'col'), split_axis=0, concat_axis=0, tile...  17.3 us
    all_to_all x1, waiting for transfers between devices, over_clu(): return lax.all_to_all(v, 'clu', split_axis=0, concat_axis=0, tiled=True)  10.1 us
    all_to_all x1, starting transfers between devices, over_clu(): return lax.all_to_all(v, 'clu', split_axis=0, concat_axis=0, tiled=True)  9.86 us
    pallas_call x5, Pallas kernels, update(): pl.pallas_call(functools.partial(step_kernel, number, has_recv), in_specs...  7.16 us
    pallas_call x1, Pallas kernels, per_device(): pl.pallas_call(rhs_kernel, grid=(3,), in_specs=[smem(), smem(), whole(1,...  4.84 us
    ppermute x3, starting transfers between devices, swap(): return lax.ppermute(v, ('clu', 'col'), pairs)  4.16 us
    ppermute x3, starting transfers between devices, over_col(): lax.ppermute(v, 'col', [(i, i ^ k) for i in range(COLS)])  3.35 us
  transfers between devices with their start and end apart: 7, of which 3 were waited for; matrix products, arithmetic and copies ran while one was open for 0% of the time, Pallas kernels for 4%

profile of v6, /device:TPU:1, one launch (start us, length us, event | category | flops | bytes accessed | tf_op | source)
XLA Modules:
  0.0 122.0 jit_solution(7366939364533591439)
XLA Ops:
  0.6 3.4 %collective-permute-start.4 = (bf16[4,144,576]{2,1,0:T(8,128)(2,1)}, bf16[4,144,576]{2,1,0:T(8,128)(2,1)S(1)}, u32[]{:S(2)}, u32[]{:S(2)}) collective-permute-start(bf16[4,144,576]{2,1,0:T(8,128)(2,1)} %bitcast.9), channel_id=1, source_target_pairs={{0,1},{1,0},{2,3},{3,2},{4,7},{5,6},{6,5},{7,4},{8,9},{9,8},{10,11... | collective-permute-start | bytes 1990664 | tf_op jit(solution)/shard_map/ppermute | solution.py:294
  4.0 4.8 %rhs.1 = f32[32,1,3584]{2,1,0:T(1,128)} custom-call(s32[32]{0:T(128)} %cc_ref.1, s32[4,4,32]{2,1,0:T(4,128)} %rp_ref.1, s32[1,1024]{1,0:T(1,128)} %bitcast.12, s32[1,1024]{1,0:T(1,128)} %bitcast.15, f32[3,3,1024]{2,1,0:T(4,128)} %refs_6_.3, f32[3,1024]{1,0:T(4,128)} %grad_ref.1, bf16[1728,1024]{1,0:T(8,128)(2,1)} %bitcast.6, f32[1,144]{1,0:T(1,128)} %cg_ref.1, ...), custom_call_target="tpu_custom_call" | custom-call | tf_op jit(solution)/shard_map/rhs/pallas_call | solution.py:301
  8.9 9.9 %all-to-all-start = ((f32[32,1,3584]{2,1,0:T(1,128)}), f32[32,1,3584]{2,1,0:T(1,128)S(1)}, u32[]{:S(2)}, u32[]{:S(2)}) async-start(f32[32,1,3584]{2,1,0:T(1,128)} %rhs.1), calls=%async_computation | async-start | bytes 917504 | tf_op jit(solution)/shard_map/all_to_all | solution.py:323
  18.8 0.8 collective-permute-start.5
  19.6 10.1 %all-to-all-done.recv_ref = f32[32,1,3584]{2,1,0:T(1,128)S(1)} async-done(((f32[32,1,3584]{2,1,0:T(1,128)}), f32[32,1,3584]{2,1,0:T(1,128)S(1)}, u32[]{:S(2)}, u32[]{:S(2)}) %all-to-all-start) | async-done | bytes 458784 | tf_op jit(solution)/shard_map/all_to_all | solution.py:323
  29.7 0.2 gather.1
  29.9 0.9 collective-permute-start.3
  30.8 1.3 %collective-permute-start.2 = (f32[1,4736]{1,0:T(1,128)S(1)}, f32[1,4736]{1,0:T(1,128)S(1)}, u32[]{:S(2)}, u32[]{:S(2)}) collective-permute-start(f32[1,4736]{1,0:T(1,128)S(1)} %get-tuple-element.19.v0), channel_id=1, source_target_pairs={{0,2},{1,3},{2,0},{3,1},{4,6},{5,7},{6,4},{7,5},{8,10},{9,11},{10,... | collective-permute-start | bytes 56840 | tf_op jit(solution)/shard_map/ppermute | solution.py:287
  32.1 1.1 collective-permute-start.1
  33.3 0.6 collective-permute-done.3.v3
  33.8 1.2 collective-permute-done.2.v2
  35.0 1.7 %first_step.1 = (f32[8,640]{1,0:T(8,128)S(1)}, f32[32,1,640]{2,1,0:T(1,128)S(1)}, f32[1,144]{1,0:T(1,128)}, bf16[4,640,576]{2,1,0:T(8,128)(2,1)S(1)}) custom-call(s32[1,128]{1,0:T(1,128)S(1)} %get-tuple-element.18.ids_ref.refs_0_, f32[1,4736]{1,0:T(1,128)S(1)} %get-tuple-element.19.v0, f32[1,4736]{1,0:T(1,128)S(1)} %collective-permute-done.1.v1, ...), custom_call_target="tpu_custom_call" | custom-call | tf_op jit(solution)/shard_map/first_step/pallas_call | solution.py:338
  36.7 14.5 %all_to_all.35.refs_1_ = f32[32,1,640]{2,1,0:T(1,128)S(1)} all-to-all(f32[32,1,640]{2,1,0:T(1,128)S(1)} %get-tuple-element.20), channel_id=1, replica_groups=mesh['clu'=32,'col'=4] {'clu'}, dimensions={0} | all-to-all | bytes 163840 | tf_op jit(solution)/shard_map/all_to_all | solution.py:323
  51.3 2.6 %step.5 = (f32[8,640]{1,0:T(8,128)S(1)}, f32[32,1,1280]{2,1,0:T(1,128)S(1)}) custom-call(s32[1,128]{1,0:T(1,128)S(1)} %get-tuple-element.18.ids_ref.refs_0_, f32[32,1,640]{2,1,0:T(1,128)S(1)} %all_to_all.35.refs_1_, f32[8,640]{1,0:T(8,128)S(1)} %get-tuple-element.21.refs_2_, bf16[4,640,576]{2,1,0:T(8,128)(2,1)S(1)} %get-tuple-element.22.refs_3_.blocks_ref, ...), custom_call_target="tpu_custom_call" | custom-call | tf_op jit(solution)/shard_map/step/pallas_call | solution.py:354
  53.8 11.5 %all_to_all.36.refs_1_ = f32[32,1,1280]{2,1,0:T(1,128)S(1)} all-to-all(f32[32,1,1280]{2,1,0:T(1,128)S(1)} %get-tuple-element.23), channel_id=1, replica_groups=mesh['clu'=32,'col'=4] {'clu'}, dimensions={0} | all-to-all | bytes 327680 | tf_op jit(solution)/shard_map/all_to_all | solution.py:323
  65.4 0.7 step.6
  66.0 11.0 %all_to_all.37.refs_1_ = f32[32,1,640]{2,1,0:T(1,128)S(1)} all-to-all(f32[32,1,640]{2,1,0:T(1,128)S(1)} %get-tuple-element.25), channel_id=1, replica_groups=mesh['clu'=32,'col'=4] {'clu'}, dimensions={0} | all-to-all | bytes 163840 | tf_op jit(solution)/shard_map/all_to_all | solution.py:323
  77.0 2.6 %step.7 = (f32[8,640]{1,0:T(8,128)S(1)}, f32[32,1,1280]{2,1,0:T(1,128)S(1)}) custom-call(s32[1,128]{1,0:T(1,128)S(1)} %get-tuple-element.18.ids_ref.refs_0_, f32[32,1,640]{2,1,0:T(1,128)S(1)} %all_to_all.37.refs_1_, f32[8,640]{1,0:T(8,128)S(1)} %get-tuple-element.26.refs_2_, bf16[4,640,576]{2,1,0:T(8,128)(2,1)S(1)} %get-tuple-element.22.refs_3_.blocks_ref, ...), custom_call_target="tpu_custom_call" | custom-call | tf_op jit(solution)/shard_map/step/pallas_call | solution.py:354
  79.6 11.5 %all_to_all.38.refs_1_ = f32[32,1,1280]{2,1,0:T(1,128)S(1)} all-to-all(f32[32,1,1280]{2,1,0:T(1,128)S(1)} %get-tuple-element.27), channel_id=1, replica_groups=mesh['clu'=32,'col'=4] {'clu'}, dimensions={0} | all-to-all | bytes 327680 | tf_op jit(solution)/shard_map/all_to_all | solution.py:323
  91.1 0.7 step.8
  91.8 11.0 %all_to_all.39.refs_1_ = f32[32,1,640]{2,1,0:T(1,128)S(1)} all-to-all(f32[32,1,640]{2,1,0:T(1,128)S(1)} %get-tuple-element.29), channel_id=1, replica_groups=mesh['clu'=32,'col'=4] {'clu'}, dimensions={0} | all-to-all | bytes 163840 | tf_op jit(solution)/shard_map/all_to_all | solution.py:323
  102.8 0.7 step.9
  103.5 17.3 %all_to_all.40.recv_ref = f32[128,1,640]{2,1,0:T(1,128)S(1)} all-to-all(f32[128,1,640]{2,1,0:T(1,128)S(1)} %get-tuple-element.31), channel_id=1, replica_groups=mesh['clu'=32,'col'=4] {'clu','col'}, dimensions={0} | all-to-all | bytes 655360 | tf_op jit(solution)/shard_map/all_to_all | solution.py:373
  120.8 1.3 %last_step.1 = f32[1,144]{1,0:T(1,128)} custom-call(s32[1,128]{1,0:T(1,128)S(1)} %get-tuple-element.18.ids_ref.refs_0_, f32[128,1,640]{2,1,0:T(1,128)S(1)} %all_to_all.40.recv_ref, f32[8,640]{1,0:T(8,128)S(1)} %get-tuple-element.32.state_ref, bf16[4,640,576]{2,1,0:T(8,128)(2,1)S(1)} %get-tuple-element.22.refs_3_.blocks_ref), custom_call_target="tpu_custom_call" | custom-call | tf_op jit(solution)/shard_map/last_step/pallas_call | solution.py:374
  (15 shorter events, 0.1 us)
Async XLA Ops:
  0.6 18.2 %collective-permute-start.4 = (bf16[4,144,576]{2,1,0:T(8,128)(2,1)}, bf16[4,144,576]{2,1,0:T(8,128)(2,1)S(1)}, u32[]{:S(2)}, u32[]{:S(2)}) collective-permute-start(bf16[4,144,576]{2,1,0:T(8,128)(2,1)} %bitcast.9), channel_id=1, source_target_pairs={{0,1},{1,0},{2,3},{3,2},{4,7},{5,6},{6,5},{7,4},{8,9},{9,8},{10,11... | collective-permute-start | bytes 1990664 | tf_op jit(solution)/shard_map/ppermute | solution.py:294
  4.0 25.7 %collective-permute-start = (bf16[4,144,576]{2,1,0:T(8,128)(2,1)}, bf16[4,144,576]{2,1,0:T(8,128)(2,1)S(1)}, u32[]{:S(2)}, u32[]{:S(2)}) collective-permute-start(bf16[4,144,576]{2,1,0:T(8,128)(2,1)} %bitcast.10), channel_id=1, source_target_pairs={{0,3},{1,2},{2,1},{3,0},{4,5},{5,4},{6,7},{7,6},{8,11},{9,10},{10,... | collective-permute-start | bytes 1990664 | tf_op jit(solution)/shard_map/ppermute | solution.py:294
  8.9 20.8 %all-to-all-start = ((f32[32,1,3584]{2,1,0:T(1,128)}), f32[32,1,3584]{2,1,0:T(1,128)S(1)}, u32[]{:S(2)}, u32[]{:S(2)}) async-start(f32[32,1,3584]{2,1,0:T(1,128)} %rhs.1), calls=%async_computation | async-start | bytes 917504 | tf_op jit(solution)/shard_map/all_to_all | solution.py:323
  18.7 16.3 %copy-start.1 = (bf16[1,4,576,144]{2,3,1,0:T(8,128)(2,1)S(1)}, bf16[1,4,576,144]{2,3,1,0:T(8,128)(2,1)}, u32[]{:S(2)}) copy-start(bf16[1,4,576,144]{2,3,1,0:T(8,128)(2,1)} %param.19) | copy-start | bytes 1990660
  18.7 32.5 %copy-start.2 = (f32[3,3,1024]{2,1,0:T(4,128)S(1)}, f32[3,3,1024]{2,1,0:T(4,128)}, u32[]{:S(2)}) copy-start(f32[3,3,1024]{2,1,0:T(4,128)} %refs_6_.3) | copy-start | bytes 110596
  18.8 32.5 %copy-start.3 = (s32[1024,1]{0,1:T(1,128)S(1)}, s32[1024,1]{0,1:T(1,128)}, u32[]{:S(2)}) copy-start(s32[1024,1]{0,1:T(1,128)} %param.11) | copy-start | bytes 12292
  18.8 32.5 %copy-start.4 = (s32[1024]{0:T(1024)S(1)}, s32[1024]{0:T(1024)}, u32[]{:S(2)}) copy-start(s32[1024]{0:T(1024)} %param.12) | copy-start | bytes 12292
  18.8 16.2 %collective-permute-start.5 = (bf16[4,144,576]{2,1,0:T(8,128)(2,1)S(1)}, bf16[4,144,576]{2,1,0:T(8,128)(2,1)S(1)}, u32[]{:S(2)}, u32[]{:S(2)}) collective-permute-start(bf16[4,144,576]{2,1,0:T(8,128)(2,1)S(1)} %collective-permute-done.4.b1), channel_id=1, source_target_pairs={{0,3},{1,2},{2,1},{3,0},{4,5},{5,4},{6,7},{7,6},{8,11},{9,10},{10,... | collective-permute-start | bytes 1990664 | tf_op jit(solution)/shard_map/ppermute | solution.py:294
  29.7 21.5 %copy-start = (bf16[1024,1728]{0,1:T(8,128)(2,1)S(1)}, bf16[1024,1728]{0,1:T(8,128)(2,1)}, u32[]{:S(2)}) copy-start(bf16[1024,1728]{0,1:T(8,128)(2,1)} %param.13) | copy-start | bytes 10616836
  29.9 3.9 %collective-permute-start.3 = (f32[1,4736]{1,0:T(1,128)S(1)}, f32[1,4736]{1,0:T(1,128)S(1)}, u32[]{:S(2)}, u32[]{:S(2)}) collective-permute-start(f32[1,4736]{1,0:T(1,128)S(1)} %get-tuple-element.19.v0), channel_id=1, source_target_pairs={{0,3},{1,2},{2,1},{3,0},{4,7},{5,6},{6,5},{7,4},{8,11},{9,10},{10,... | collective-permute-start | bytes 56840 | tf_op jit(solution)/shard_map/ppermute | solution.py:287
  30.8 4.1 %collective-permute-start.2 = (f32[1,4736]{1,0:T(1,128)S(1)}, f32[1,4736]{1,0:T(1,128)S(1)}, u32[]{:S(2)}, u32[]{:S(2)}) collective-permute-start(f32[1,4736]{1,0:T(1,128)S(1)} %get-tuple-element.19.v0), channel_id=1, source_target_pairs={{0,2},{1,3},{2,0},{3,1},{4,6},{5,7},{6,4},{7,5},{8,10},{9,11},{10,... | collective-permute-start | bytes 56840 | tf_op jit(solution)/shard_map/ppermute | solution.py:287
  32.1 2.9 %collective-permute-start.1 = (f32[1,4736]{1,0:T(1,128)S(1)}, f32[1,4736]{1,0:T(1,128)S(1)}, u32[]{:S(2)}, u32[]{:S(2)}) collective-permute-start(f32[1,4736]{1,0:T(1,128)S(1)} %get-tuple-element.19.v0), channel_id=1, source_target_pairs={{0,1},{1,0},{2,3},{3,2},{4,5},{5,4},{6,7},{7,6},{8,9},{9,8},{10,11... | collective-permute-start | bytes 56840 | tf_op jit(solution)/shard_map/ppermute | solution.py:287

commit v7 on v6

--- a/solution.py
+++ b/solution.py
@@ -82,43 +82,60 @@
 
 
 def rhs_kernel(
-    cc_ref, rp_ref, dest_ref, obs_ref, info_ref, grad_ref, jac_ref, cg_ref, step_ref, diag_ref,
-    out_ref, total,
+    cc_hbm, rp_hbm, dest_hbm, obs_hbm, info_hbm, grad_hbm, cg_hbm, step_hbm, diag_hbm, jac_hbm,
+    own_hbm, out_ref, again_hbm,
+    cc_ref, rp_ref, dest_ref, obs_ref, info_ref, grad_ref, cg_ref, step_ref, diag_ref, jac_ref,
+    total, block_ref, sems,
 ):
-    a = pl.program_id(0)
+    sources = [dest_hbm, obs_hbm, info_hbm, grad_hbm, cg_hbm, step_hbm, diag_hbm, cc_hbm, rp_hbm]
+    targets = [dest_ref, obs_ref, info_ref, grad_ref, cg_ref, step_ref, diag_ref, cc_ref, rp_ref]
+    for a in range(3):
+        sources.append(jac_hbm.at[CAM * a : CAM * (a + 1), :])
+        targets.append(jac_ref.at[a])
+    sources.append(own_hbm)
+    targets.append(block_ref)
+    copies = [
+        pltpu.make_async_copy(source, target, sems.at[i])
+        for i, (source, target) in enumerate(zip(sources, targets))
+    ]
+    for copy in copies:
+        copy.start()
     me = lax.axis_index("clu")
     col = lax.axis_index("col")
+    for copy in copies[:7]:
+        copy.wait()
+    onehot = members(dest_ref)
     obs = obs_ref[...].astype(F32)
-    q = jnp.zeros((1, TRK), F32)
-    for b in range(3):
-        q = q + obs * info_ref[0, b : b + 1, :] * grad_ref[b : b + 1, :]
-    part = fold(
-        lax.dot_general(
-            scatter_rows(members(dest_ref), q), jac_ref[...], NT, preferred_element_type=F32
-        )
-    )
-
-    @pl.when(a == 0)
-    def _():
-        rows = lax.broadcasted_iota(jnp.int32, (CLUSTERS, WIDE), 0)
-        total[...] = jnp.where(rows == me, place_share(cg_ref[...], col), 0.0)
-
-    total[:, :CAM] = total[:, :CAM] - part
-
-    @pl.when(a == 2)
-    def _():
-        share = widen(jnp.concatenate([step_ref[...], diag_ref[...]], 1), PAIR)
-        lanes = lax.broadcasted_iota(jnp.int32, (1, PAIR), 1) - TABLE
-        for c in range(CLUSTERS):
-            colour = cc_ref[c]
-            row = jnp.where(lanes == MY_COLOUR, colour.astype(F32), share)
-            out_ref[c, :, 0:WIDE] = total[c : c + 1, :]
-            for r in range(ROUNDS):
-                p = rp_ref[colour, r, c]
-                out_ref[c, :, WIDE * (r + 1) : WIDE * (r + 2)] = total[pl.ds(p, 1), :]
-                row = jnp.where(lanes == PARTNER + r, p.astype(F32), row)
-                row = jnp.where(lanes == PARTNER_COLOUR + r, cc_ref[p].astype(F32), row)
-            out_ref[c, :, WIDE * 5 :] = row
+    part = jnp.zeros((2 * CLUSTERS, CAM), F32)
+    for a in range(3):
+        q = jnp.zeros((1, TRK), F32)
+        for b in range(3):
+            q = q + obs * info_ref[a, b : b + 1, :] * grad_ref[b : b + 1, :]
+        spread = scatter_rows(onehot, q)
+        copies[9 + a].wait()
+        part = part + lax.dot_general(spread, jac_ref[a], NT, preferred_element_type=F32)
+    rows = lax.broadcasted_iota(jnp.int32, (CLUSTERS, WIDE), 0)
+    total[...] = jnp.where(rows == me, place_share(cg_ref[...], col), 0.0) - widen(fold(part))
+    copies[7].wait()
+    copies[8].wait()
+    copies[12].wait()
+    back = pltpu.make_async_copy(block_ref, again_hbm, sems.at[13])
+    back.start()
+    share = widen(jnp.concatenate([step_ref[...], diag_ref[...]], 1), PAIR)
+    ends = PAIR - LANES
+    lanes = lax.broadcasted_iota(jnp.int32, (1, LANES), 1) + (ends - TABLE)
+    for c in range(CLUSTERS):
+        colour = cc_ref[c]
+        row = jnp.where(lanes == MY_COLOUR, colour.astype(F32), share[:, ends:])
+        out_ref[c, :, 0:WIDE] = total[c : c + 1, :]
+        for r in range(ROUNDS):
+            p = rp_ref[colour, r, c]
+            out_ref[c, :, WIDE * (r + 1) : WIDE * (r + 2)] = total[pl.ds(p, 1), :]
+            row = jnp.where(lanes == PARTNER + r, p.astype(F32), row)
+            row = jnp.where(lanes == PARTNER_COLOUR + r, cc_ref[p].astype(F32), row)
+        out_ref[c, :, WIDE * 5 : WIDE * 5 + ends] = share[:, :ends]
+        out_ref[c, :, WIDE * 5 + ends :] = row
+    back.wait()
 
 
 def gather_kernel(recv_ref, ready_ref, out_ref, ids_ref):
@@ -293,30 +310,39 @@
                 pairs.append((COLS * c + i, COLS * c + (i ^ (odd if c % 2 else even))))
         return lax.ppermute(v, ("clu", "col"), pairs)
 
-    near, other = swap(own, 1, 3), swap(own, 3, 1)
+    near = swap(own, 1, 3)
     limit = pltpu.CompilerParams(vmem_limit_bytes=24 << 20)
     large = pltpu.CompilerParams(vmem_limit_bytes=56 << 20)
 
-    whole = lambda *block: pl.BlockSpec(block, lambda a: (0,) * len(block))
-    payload = pl.pallas_call(
+    payload, again = pl.pallas_call(
         rhs_kernel,
-        grid=(3,),
-        in_specs=[
-            smem(), smem(), whole(1, TRK), whole(1, TRK),
-            pl.BlockSpec((1, 3, TRK), lambda a: (a, 0, 0)), whole(3, TRK),
-            pl.BlockSpec((CAM, TRK), lambda a: (a, 0)), whole(1, SHARE), whole(1, SHARE),
-            whole(1, SHARE),
+        in_specs=[pl.BlockSpec(memory_space=pl.ANY)] * 11,
+        out_specs=[vmem(), pl.BlockSpec(memory_space=pl.ANY)],
+        out_shape=[
+            shape(CLUSTERS, 1, 5 * WIDE + PAIR), shape(ROUNDS, SHARE, CAM, dtype=BF16),
         ],
-        out_specs=whole(CLUSTERS, 1, 5 * WIDE + PAIR),
-        out_shape=shape(CLUSTERS, 1, 5 * WIDE + PAIR),
-        scratch_shapes=[pltpu.VMEM((CLUSTERS, WIDE), F32)],
+        scratch_shapes=[
+            pltpu.SMEM((CLUSTERS,), jnp.int32),
+            pltpu.SMEM((COLOURS, ROUNDS, CLUSTERS), jnp.int32),
+            pltpu.VMEM((1, TRK), jnp.int32),
+            pltpu.VMEM((1, TRK), jnp.int32),
+            pltpu.VMEM((3, 3, TRK), F32),
+            pltpu.VMEM((3, TRK), F32),
+            pltpu.VMEM((1, SHARE), F32),
+            pltpu.VMEM((1, SHARE), F32),
+            pltpu.VMEM((1, SHARE), F32),
+            pltpu.VMEM((3, CAM, TRK), BF16),
+            pltpu.VMEM((CLUSTERS, WIDE), F32),
+            pltpu.VMEM((ROUNDS, SHARE, CAM), BF16),
+            pltpu.SemaphoreType.DMA((14,)),
+        ],
         compiler_params=large,
         name="rhs",
     )(
-        cluster_colour, round_partner, dest, obs, point_info, point_grad, jac,
-        camera_grad, step_scale, camera_diag,
+        cluster_colour, round_partner, dest, obs, point_info, point_grad,
+        camera_grad, step_scale, camera_diag, jac, own,
     )
-
+    other = swap(again, 3, 1)
     pieces = [own, near, swap(near, 3, 1), other]
 
     def over_clu(v):

time: 122 us -> 119 us (0.975)
  blocking collectives: 76.9 us -> 73.8 us
    all_to_all x5, blocking collectives: 59.5 us -> 57.4 us  [over_clu(): return lax.all_to_all(v, 'clu', split_axis=0, concat_axis=0, tiled=True)]
where the time goes in v7:
time: 119 us
  blocking collectives  73.8 us (62%)
  starting transfers between devices  17.1 us (14%)
  Pallas kernels  15.1 us (13%)
  waiting for transfers between devices  12.3 us (10%)
    all_to_all x5, blocking collectives, over_clu(): return lax.all_to_all(v, 'clu', split_axis=0, concat_axis=0, tiled=True)  57.4 us
    all_to_all x1, blocking collectives, per_device(): lax.all_to_all(payload, ('clu', 'col'), split_axis=0, concat_axis=0, tile...  16.3 us
    all_to_all x1, waiting for transfers between devices, over_clu(): return lax.all_to_all(v, 'clu', split_axis=0, concat_axis=0, tiled=True)  10.5 us
    all_to_all x1, starting transfers between devices, over_clu(): return lax.all_to_all(v, 'clu', split_axis=0, concat_axis=0, tiled=True)  9.87 us
    pallas_call x5, Pallas kernels, update(): pl.pallas_call(functools.partial(step_kernel, number, has_recv), in_specs...  7.15 us
    pallas_call x1, Pallas kernels, per_device(): pl.pallas_call(rhs_kernel, in_specs=[pl.BlockSpec(memory_space=pl.ANY)] *...  4.78 us
    ppermute x3, starting transfers between devices, swap(): return lax.ppermute(v, ('clu', 'col'), pairs)  3.86 us
    ppermute x3, starting transfers between devices, over_col(): lax.ppermute(v, 'col', [(i, i ^ k) for i in range(COLS)])  3.35 us
  transfers between devices with their start and end apart: 7, of which 3 were waited for; matrix products, arithmetic and copies ran while one was open for 0% of the time, Pallas kernels for 4%

profile of v7, /device:TPU:1, one launch (start us, length us, event | category | flops | bytes accessed | tf_op | source)
XLA Modules:
  0.0 119.0 jit_solution(12612208009732108562)
XLA Ops:
  0.6 3.4 %collective-permute-start.4 = (bf16[4,144,576]{2,1,0:T(8,128)(2,1)}, bf16[4,144,576]{2,1,0:T(8,128)(2,1)S(1)}, u32[]{:S(2)}, u32[]{:S(2)}) collective-permute-start(bf16[4,144,576]{2,1,0:T(8,128)(2,1)} %bitcast.9), channel_id=1, source_target_pairs={{0,1},{1,0},{2,3},{3,2},{4,7},{5,6},{6,5},{7,4},{8,9},{9,8},{10,11... | collective-permute-start | bytes 1990664 | tf_op jit(solution)/shard_map/ppermute | solution.py:311
  4.0 4.8 %rhs.1 = (f32[32,1,3584]{2,1,0:T(1,128)}, bf16[4,144,576]{2,1,0:T(8,128)(2,1)}) custom-call(s32[32]{0:T(128)} %cc_hbm.1, s32[4,4,32]{2,1,0:T(4,128)} %rp_hbm.1, s32[1,1024]{1,0:T(1,128)} %bitcast.12, s32[1,1024]{1,0:T(1,128)} %bitcast.15, f32[3,3,1024]{2,1,0:T(4,128)} %refs_6_.3, f32[3,1024]{1,0:T(4,128)} %grad_hbm.1, f32[1,144]{1,0:T(1,128)} %cg_hbm.1, ...), custom_call_target="tpu_custom_call" | custom-call | tf_op jit(solution)/shard_map/rhs/pallas_call | solution.py:317
  8.9 9.9 %all-to-all-start = ((f32[32,1,3584]{2,1,0:T(1,128)}), f32[32,1,3584]{2,1,0:T(1,128)S(1)}, u32[]{:S(2)}, u32[]{:S(2)}) async-start(f32[32,1,3584]{2,1,0:T(1,128)} %get-tuple-element.20), calls=%async_computation | async-start | bytes 917504 | tf_op jit(solution)/shard_map/all_to_all | solution.py:349
  18.8 0.4 collective-permute-start.5
  19.2 10.5 %all-to-all-done.recv_ref = f32[32,1,3584]{2,1,0:T(1,128)S(1)} async-done(((f32[32,1,3584]{2,1,0:T(1,128)}), f32[32,1,3584]{2,1,0:T(1,128)S(1)}, u32[]{:S(2)}, u32[]{:S(2)}) %all-to-all-start) | async-done | bytes 458784 | tf_op jit(solution)/shard_map/all_to_all | solution.py:349
  29.7 0.2 gather.1
  29.9 0.9 collective-permute-start.3
  30.9 1.3 %collective-permute-start.2 = (f32[1,4736]{1,0:T(1,128)S(1)}, f32[1,4736]{1,0:T(1,128)S(1)}, u32[]{:S(2)}, u32[]{:S(2)}) collective-permute-start(f32[1,4736]{1,0:T(1,128)S(1)} %get-tuple-element.23.v0), channel_id=1, source_target_pairs={{0,2},{1,3},{2,0},{3,1},{4,6},{5,7},{6,4},{7,5},{8,10},{9,11},{10,... | collective-permute-start | bytes 56840 | tf_op jit(solution)/shard_map/ppermute | solution.py:304
  32.1 1.2 collective-permute-start.1
  33.3 0.6 collective-permute-done.3.v3
  33.9 1.2 collective-permute-done.2.v2
  35.1 1.7 %first_step.1 = (f32[8,640]{1,0:T(8,128)S(1)}, f32[32,1,640]{2,1,0:T(1,128)S(1)}, f32[1,144]{1,0:T(1,128)}, bf16[4,640,576]{2,1,0:T(8,128)(2,1)S(1)}) custom-call(s32[1,128]{1,0:T(1,128)S(1)} %get-tuple-element.22.ids_ref.refs_0_, f32[1,4736]{1,0:T(1,128)S(1)} %get-tuple-element.23.v0, f32[1,4736]{1,0:T(1,128)S(1)} %collective-permute-done.1.v1, ...), custom_call_target="tpu_custom_call" | custom-call | tf_op jit(solution)/shard_map/first_step/pallas_call | solution.py:364
  36.7 12.4 %all_to_all.35.refs_1_ = f32[32,1,640]{2,1,0:T(1,128)S(1)} all-to-all(f32[32,1,640]{2,1,0:T(1,128)S(1)} %get-tuple-element.24), channel_id=1, replica_groups=mesh['clu'=32,'col'=4] {'clu'}, dimensions={0} | all-to-all | bytes 163840 | tf_op jit(solution)/shard_map/all_to_all | solution.py:349
  49.2 2.6 %step.5 = (f32[8,640]{1,0:T(8,128)S(1)}, f32[32,1,1280]{2,1,0:T(1,128)S(1)}) custom-call(s32[1,128]{1,0:T(1,128)S(1)} %get-tuple-element.22.ids_ref.refs_0_, f32[32,1,640]{2,1,0:T(1,128)S(1)} %all_to_all.35.refs_1_, f32[8,640]{1,0:T(8,128)S(1)} %get-tuple-element.25.refs_2_, bf16[4,640,576]{2,1,0:T(8,128)(2,1)S(1)} %get-tuple-element.26.refs_3_.blocks_ref, ...), custom_call_target="tpu_custom_call" | custom-call | tf_op jit(solution)/shard_map/step/pallas_call | solution.py:380
  51.8 11.5 %all_to_all.36.refs_1_ = f32[32,1,1280]{2,1,0:T(1,128)S(1)} all-to-all(f32[32,1,1280]{2,1,0:T(1,128)S(1)} %get-tuple-element.27), channel_id=1, replica_groups=mesh['clu'=32,'col'=4] {'clu'}, dimensions={0} | all-to-all | bytes 327680 | tf_op jit(solution)/shard_map/all_to_all | solution.py:349
  63.3 0.7 step.6
  63.9 11.0 %all_to_all.37.refs_1_ = f32[32,1,640]{2,1,0:T(1,128)S(1)} all-to-all(f32[32,1,640]{2,1,0:T(1,128)S(1)} %get-tuple-element.29), channel_id=1, replica_groups=mesh['clu'=32,'col'=4] {'clu'}, dimensions={0} | all-to-all | bytes 163840 | tf_op jit(solution)/shard_map/all_to_all | solution.py:349
  74.9 2.6 %step.7 = (f32[8,640]{1,0:T(8,128)S(1)}, f32[32,1,1280]{2,1,0:T(1,128)S(1)}) custom-call(s32[1,128]{1,0:T(1,128)S(1)} %get-tuple-element.22.ids_ref.refs_0_, f32[32,1,640]{2,1,0:T(1,128)S(1)} %all_to_all.37.refs_1_, f32[8,640]{1,0:T(8,128)S(1)} %get-tuple-element.30.refs_2_, bf16[4,640,576]{2,1,0:T(8,128)(2,1)S(1)} %get-tuple-element.26.refs_3_.blocks_ref, ...), custom_call_target="tpu_custom_call" | custom-call | tf_op jit(solution)/shard_map/step/pallas_call | solution.py:380
  77.5 11.5 %all_to_all.38.refs_1_ = f32[32,1,1280]{2,1,0:T(1,128)S(1)} all-to-all(f32[32,1,1280]{2,1,0:T(1,128)S(1)} %get-tuple-element.31), channel_id=1, replica_groups=mesh['clu'=32,'col'=4] {'clu'}, dimensions={0} | all-to-all | bytes 327680 | tf_op jit(solution)/shard_map/all_to_all | solution.py:349
  89.0 0.7 step.8
  89.7 11.0 %all_to_all.39.refs_1_ = f32[32,1,640]{2,1,0:T(1,128)S(1)} all-to-all(f32[32,1,640]{2,1,0:T(1,128)S(1)} %get-tuple-element.33), channel_id=1, replica_groups=mesh['clu'=32,'col'=4] {'clu'}, dimensions={0} | all-to-all | bytes 163840 | tf_op jit(solution)/shard_map/all_to_all | solution.py:349
  100.7 0.7 step.9
  101.4 16.3 %all_to_all.40.recv_ref = f32[128,1,640]{2,1,0:T(1,128)S(1)} all-to-all(f32[128,1,640]{2,1,0:T(1,128)S(1)} %get-tuple-element.35), channel_id=1, replica_groups=mesh['clu'=32,'col'=4] {'clu','col'}, dimensions={0} | all-to-all | bytes 655360 | tf_op jit(solution)/shard_map/all_to_all | solution.py:399
  117.7 1.3 %last_step.1 = f32[1,144]{1,0:T(1,128)} custom-call(s32[1,128]{1,0:T(1,128)S(1)} %get-tuple-element.22.ids_ref.refs_0_, f32[128,1,640]{2,1,0:T(1,128)S(1)} %all_to_all.40.recv_ref, f32[8,640]{1,0:T(8,128)S(1)} %get-tuple-element.36.state_ref, bf16[4,640,576]{2,1,0:T(8,128)(2,1)S(1)} %get-tuple-element.26.refs_3_.blocks_ref), custom_call_target="tpu_custom_call" | custom-call | tf_op jit(solution)/shard_map/last_step/pallas_call | solution.py:400
  (15 shorter events, 0.2 us)
Async XLA Ops:
  0.6 18.2 %collective-permute-start.4 = (bf16[4,144,576]{2,1,0:T(8,128)(2,1)}, bf16[4,144,576]{2,1,0:T(8,128)(2,1)S(1)}, u32[]{:S(2)}, u32[]{:S(2)}) collective-permute-start(bf16[4,144,576]{2,1,0:T(8,128)(2,1)} %bitcast.9), channel_id=1, source_target_pairs={{0,1},{1,0},{2,3},{3,2},{4,7},{5,6},{6,5},{7,4},{8,9},{9,8},{10,11... | collective-permute-start | bytes 1990664 | tf_op jit(solution)/shard_map/ppermute | solution.py:311
  8.8 20.9 %collective-permute-start = (bf16[4,144,576]{2,1,0:T(8,128)(2,1)}, bf16[4,144,576]{2,1,0:T(8,128)(2,1)S(1)}, u32[]{:S(2)}, u32[]{:S(2)}) collective-permute-start(bf16[4,144,576]{2,1,0:T(8,128)(2,1)} %get-tuple-element.21), channel_id=1, source_target_pairs={{0,3},{1,2},{2,1},{3,0},{4,5},{5,4},{6,7},{7,6},{8,11},{9,10},{10,... | collective-permute-start | bytes 1990664 | tf_op jit(solution)/shard_map/ppermute | solution.py:311
  8.9 20.8 %all-to-all-start = ((f32[32,1,3584]{2,1,0:T(1,128)}), f32[32,1,3584]{2,1,0:T(1,128)S(1)}, u32[]{:S(2)}, u32[]{:S(2)}) async-start(f32[32,1,3584]{2,1,0:T(1,128)} %get-tuple-element.20), calls=%async_computation | async-start | bytes 917504 | tf_op jit(solution)/shard_map/all_to_all | solution.py:349
  18.8 16.3 %copy-start.1 = (bf16[1,4,576,144]{2,3,1,0:T(8,128)(2,1)S(1)}, bf16[1,4,576,144]{2,3,1,0:T(8,128)(2,1)}, u32[]{:S(2)}) copy-start(bf16[1,4,576,144]{2,3,1,0:T(8,128)(2,1)} %param.19) | copy-start | bytes 1990660
  18.8 30.4 %copy-start.2 = (f32[3,3,1024]{2,1,0:T(4,128)S(1)}, f32[3,3,1024]{2,1,0:T(4,128)}, u32[]{:S(2)}) copy-start(f32[3,3,1024]{2,1,0:T(4,128)} %refs_6_.3) | copy-start | bytes 110596
  18.8 30.4 %copy-start.3 = (s32[1024,1]{0,1:T(1,128)S(1)}, s32[1024,1]{0,1:T(1,128)}, u32[]{:S(2)}) copy-start(s32[1024,1]{0,1:T(1,128)} %param.11) | copy-start | bytes 12292
  18.8 30.3 %copy-start.4 = (s32[1024]{0:T(1024)S(1)}, s32[1024]{0:T(1024)}, u32[]{:S(2)}) copy-start(s32[1024]{0:T(1024)} %param.12) | copy-start | bytes 12292
  18.8 16.2 %collective-permute-start.5 = (bf16[4,144,576]{2,1,0:T(8,128)(2,1)S(1)}, bf16[4,144,576]{2,1,0:T(8,128)(2,1)S(1)}, u32[]{:S(2)}, u32[]{:S(2)}) collective-permute-start(bf16[4,144,576]{2,1,0:T(8,128)(2,1)S(1)} %collective-permute-done.4.b1), channel_id=1, source_target_pairs={{0,3},{1,2},{2,1},{3,0},{4,5},{5,4},{6,7},{7,6},{8,11},{9,10},{10,... | collective-permute-start | bytes 1990664 | tf_op jit(solution)/shard_map/ppermute | solution.py:311
  29.7 19.4 %copy-start = (bf16[1024,1728]{0,1:T(8,128)(2,1)S(1)}, bf16[1024,1728]{0,1:T(8,128)(2,1)}, u32[]{:S(2)}) copy-start(bf16[1024,1728]{0,1:T(8,128)(2,1)} %param.13) | copy-start | bytes 10616836
  29.9 3.9 %collective-permute-start.3 = (f32[1,4736]{1,0:T(1,128)S(1)}, f32[1,4736]{1,0:T(1,128)S(1)}, u32[]{:S(2)}, u32[]{:S(2)}) collective-permute-start(f32[1,4736]{1,0:T(1,128)S(1)} %get-tuple-element.23.v0), channel_id=1, source_target_pairs={{0,3},{1,2},{2,1},{3,0},{4,7},{5,6},{6,5},{7,4},{8,11},{9,10},{10,... | collective-permute-start | bytes 56840 | tf_op jit(solution)/shard_map/ppermute | solution.py:304
  30.9 4.1 %collective-permute-start.2 = (f32[1,4736]{1,0:T(1,128)S(1)}, f32[1,4736]{1,0:T(1,128)S(1)}, u32[]{:S(2)}, u32[]{:S(2)}) collective-permute-start(f32[1,4736]{1,0:T(1,128)S(1)} %get-tuple-element.23.v0), channel_id=1, source_target_pairs={{0,2},{1,3},{2,0},{3,1},{4,6},{5,7},{6,4},{7,5},{8,10},{9,11},{10,... | collective-permute-start | bytes 56840 | tf_op jit(solution)/shard_map/ppermute | solution.py:304
  32.1 2.9 %collective-permute-start.1 = (f32[1,4736]{1,0:T(1,128)S(1)}, f32[1,4736]{1,0:T(1,128)S(1)}, u32[]{:S(2)}, u32[]{:S(2)}) collective-permute-start(f32[1,4736]{1,0:T(1,128)S(1)} %get-tuple-element.23.v0), channel_id=1, source_target_pairs={{0,1},{1,0},{2,3},{3,2},{4,5},{5,4},{6,7},{7,6},{8,9},{9,8},{10,11... | collective-permute-start | bytes 56840 | tf_op jit(solution)/shard_map/ppermute | solution.py:304

commit v8 on v7

--- a/solution.py
+++ b/solution.py
@@ -15,8 +15,9 @@
 SHARE = 144
 WIDE = 640
 SLOT = 256
-PAIR = 384
+SPARE = WIDE - CAM
 TABLE = 2 * SHARE
+GROUP = 8
 TRK = 1024
 NT = (((1,), (1,)), ((), ()))
 NN = (((1,), (0,)), ((), ()))
@@ -83,9 +84,9 @@
 
 def rhs_kernel(
     cc_hbm, rp_hbm, dest_hbm, obs_hbm, info_hbm, grad_hbm, cg_hbm, step_hbm, diag_hbm, jac_hbm,
-    own_hbm, out_ref, again_hbm,
+    own_hbm, out_hbm, again_hbm,
     cc_ref, rp_ref, dest_ref, obs_ref, info_ref, grad_ref, cg_ref, step_ref, diag_ref, jac_ref,
-    total, block_ref, sems,
+    total, block_ref, out_ref, sems,
 ):
     sources = [dest_hbm, obs_hbm, info_hbm, grad_hbm, cg_hbm, step_hbm, diag_hbm, cc_hbm, rp_hbm]
     targets = [dest_ref, obs_ref, info_ref, grad_ref, cg_ref, step_ref, diag_ref, cc_ref, rp_ref]
@@ -121,36 +122,59 @@
     copies[12].wait()
     back = pltpu.make_async_copy(block_ref, again_hbm, sems.at[13])
     back.start()
-    share = widen(jnp.concatenate([step_ref[...], diag_ref[...]], 1), PAIR)
-    ends = PAIR - LANES
-    lanes = lax.broadcasted_iota(jnp.int32, (1, LANES), 1) + (ends - TABLE)
+    spare = jnp.concatenate(
+        [step_ref[...], diag_ref[...], jnp.zeros((1, 5 * SPARE - 2 * SHARE), F32)], 1
+    )
+    empty = jnp.zeros((1, CAM), F32)
+    tails = [
+        jnp.concatenate([empty, spare[:, SPARE * v : SPARE * (v + 1)]], 1) for v in range(5)
+    ]
+    lanes = lax.broadcasted_iota(jnp.int32, (1, WIDE), 1) - (CAM + TABLE % SPARE)
+    outs = []
     for c in range(CLUSTERS):
         colour = cc_ref[c]
-        row = jnp.where(lanes == MY_COLOUR, colour.astype(F32), share[:, ends:])
-        out_ref[c, :, 0:WIDE] = total[c : c + 1, :]
-        for r in range(ROUNDS):
-            p = rp_ref[colour, r, c]
-            out_ref[c, :, WIDE * (r + 1) : WIDE * (r + 2)] = total[pl.ds(p, 1), :]
-            row = jnp.where(lanes == PARTNER + r, p.astype(F32), row)
-            row = jnp.where(lanes == PARTNER_COLOUR + r, cc_ref[p].astype(F32), row)
-        out_ref[c, :, WIDE * 5 : WIDE * 5 + ends] = share[:, :ends]
-        out_ref[c, :, WIDE * 5 + ends :] = row
+        sources = [c] + [rp_ref[colour, r, c] for r in range(ROUNDS)]
+        last = jnp.where(lanes == MY_COLOUR, colour.astype(F32), tails[4])
+        for r, p in enumerate(sources[1:]):
+            last = jnp.where(lanes == PARTNER + r, p.astype(F32), last)
+            last = jnp.where(lanes == PARTNER_COLOUR + r, cc_ref[p].astype(F32), last)
+        for v, p in enumerate(sources):
+            tail = last if v == 4 else tails[v]
+            out_ref[c, :, WIDE * v : WIDE * (v + 1)] = total[pl.ds(p, 1), :] + tail
+        if c % GROUP == GROUP - 1:
+            rows = pl.ds(c + 1 - GROUP, GROUP)
+            outs.append(
+                pltpu.make_async_copy(
+                    out_ref.at[rows], out_hbm.at[rows], sems.at[14 + c // GROUP]
+                )
+            )
+            outs[-1].start()
+    for copy in outs:
+        copy.wait()
     back.wait()
 
 
 def gather_kernel(recv_ref, ready_ref, out_ref, ids_ref):
     del ready_ref
-    vectors = recv_ref[0, :, : WIDE * 5]
+    vectors = recv_ref[0]
     for c in range(1, CLUSTERS):
-        vectors = vectors + recv_ref[c, :, : WIDE * 5]
+        vectors = vectors + recv_ref[c]
     out_ref[:, : WIDE * 5] = vectors
-    table = recv_ref[0, :, WIDE * 5 + TABLE :].astype(jnp.int32)
+
+    def spare(c):
+        return jnp.concatenate(
+            [recv_ref[c, :, WIDE * (v + 1) - SPARE : WIDE * (v + 1)] for v in range(5)], 1
+        )
+
+    me = lax.axis_index("clu")
+    mine = spare(me)
+    table = mine[:, TABLE:].astype(jnp.int32)
     ids_ref[...] = jnp.concatenate(
         [table, jnp.zeros((1, LANES - table.shape[1]), jnp.int32)], 1
     )
-    sources = [lax.axis_index("clu")] + [ids_ref[0, PARTNER + r] for r in range(ROUNDS)]
-    shares = [recv_ref[c, :, WIDE * 5 : WIDE * 5 + SHARE] for c in sources]
-    shares.append(recv_ref[sources[0], :, WIDE * 5 + SHARE : WIDE * 5 + 2 * SHARE])
+    shares = [mine[:, :SHARE]]
+    shares += [spare(ids_ref[0, PARTNER + r])[:, :SHARE] for r in range(ROUNDS)]
+    shares.append(mine[:, SHARE:TABLE])
     for at, share in enumerate(shares):
         out_ref[:, WIDE * 5 + SLOT * at : WIDE * 5 + SLOT * (at + 1)] = widen(share, SLOT)
 
@@ -169,7 +193,8 @@
     return widen(jnp.sum(out, 0, keepdims=True))
 
 
-def lay_out(pieces, blocks_ref, sems):
+def lay_out_kernel(*refs):
+    pieces, blocks_ref, sems = refs[:COLS], refs[COLS], refs[COLS + 1]
     col, core = lax.axis_index("col"), lax.rem(lax.axis_index("clu"), 2)
     copies = []
     for i, (piece, away) in enumerate(zip(pieces, (0, 1 + 2 * core, 2, 3 - 2 * core))):
@@ -178,14 +203,14 @@
             pltpu.make_async_copy(piece, blocks_ref.at[:, pl.ds(at, SHARE), :], sems.at[i])
         )
         copies[i].start()
-    return copies
+    blocks_ref[:, CAM:, :] = jnp.zeros((ROUNDS, WIDE - CAM, CAM), BF16)
+    for copy in copies:
+        copy.wait()
 
 
 def first_step_kernel(
-    ids_ref, v0, v1, v2, v3, b0, b1, b2, b3, state_ref, out_ref, rhs_ref, blocks_ref, sems
+    ids_ref, v0, v1, v2, v3, blocks_ref, state_ref, out_ref, rhs_ref
 ):
-    copies = lay_out((b0, b1, b2, b3), blocks_ref, sems)
-    blocks_ref[:, CAM:, :] = jnp.zeros((ROUNDS, WIDE - CAM, CAM), BF16)
     col = lax.axis_index("col")
     rows = [v[...] for v in (v0, v1, v2, v3)]
     vectors = (rows[0] + rows[1] + rows[2] + rows[3])[:, : WIDE * 5]
@@ -205,8 +230,6 @@
     for r in range(ROUNDS):
         x = full(r + 1) * vectors[:, WIDE * (r + 1) : WIDE * (r + 2)]
         near.append(jnp.where(ids_ref[0, PARTNER_COLOUR + r] == 0, x, 0.0))
-    for copy in copies:
-        copy.wait()
     coupled = couple(near, blocks_ref)
     mine = ids_ref[0, MY_COLOUR]
     x = jnp.where(mine == 0, step * rhs, jnp.where(mine == 1, step * (rhs - coupled), 0.0))
@@ -317,9 +340,9 @@
     payload, again = pl.pallas_call(
         rhs_kernel,
         in_specs=[pl.BlockSpec(memory_space=pl.ANY)] * 11,
-        out_specs=[vmem(), pl.BlockSpec(memory_space=pl.ANY)],
+        out_specs=[pl.BlockSpec(memory_space=pl.ANY)] * 2,
         out_shape=[
-            shape(CLUSTERS, 1, 5 * WIDE + PAIR), shape(ROUNDS, SHARE, CAM, dtype=BF16),
+            shape(CLUSTERS, 1, 5 * WIDE), shape(ROUNDS, SHARE, CAM, dtype=BF16),
         ],
         scratch_shapes=[
             pltpu.SMEM((CLUSTERS,), jnp.int32),
@@ -334,7 +357,8 @@
             pltpu.VMEM((3, CAM, TRK), BF16),
             pltpu.VMEM((CLUSTERS, WIDE), F32),
             pltpu.VMEM((ROUNDS, SHARE, CAM), BF16),
-            pltpu.SemaphoreType.DMA((14,)),
+            pltpu.VMEM((CLUSTERS, 1, 5 * WIDE), F32),
+            pltpu.SemaphoreType.DMA((14 + CLUSTERS // GROUP,)),
         ],
         compiler_params=large,
         name="rhs",
@@ -361,18 +385,23 @@
         name="gather",
     )(recv, other)
     row, first, third, second = over_col(row)
-    state, payload, reduced_rhs, blocks = pl.pallas_call(
-        first_step_kernel,
-        in_specs=[vmem()] * 5 + [pl.BlockSpec(memory_space=pl.ANY)] * 4,
-        out_specs=[vmem()] * 4,
-        out_shape=[
-            shape(8, WIDE), shape(CLUSTERS, 1, WIDE), shape(1, SHARE),
-            shape(ROUNDS, WIDE, CAM, dtype=BF16),
-        ],
+    blocks = pl.pallas_call(
+        lay_out_kernel,
+        in_specs=[pl.BlockSpec(memory_space=pl.ANY)] * COLS,
+        out_specs=vmem(),
+        out_shape=shape(ROUNDS, WIDE, CAM, dtype=BF16),
         scratch_shapes=[pltpu.SemaphoreType.DMA((COLS,))],
         compiler_params=limit,
+        name="lay_out",
+    )(*pieces)
+    state, payload, reduced_rhs = pl.pallas_call(
+        first_step_kernel,
+        in_specs=[vmem()] * 6,
+        out_specs=[vmem()] * 3,
+        out_shape=[shape(8, WIDE), shape(CLUSTERS, 1, WIDE), shape(1, SHARE)],
+        compiler_params=limit,
         name="first_step",
-    )(ids, row, first, second, third, *pieces)
+    )(ids, row, first, second, third, blocks)
 
     def update(number, recv, state, has_send=False, has_recv=False):
         rows = CLUSTERS * COLS if number == 2 * COLOURS - 2 else CLUSTERS

time: 119 us -> 120 us (level)
  no operation moved by 1% of the time
where the time goes in v8:
time: 120 us; the launch traced here: 119 us
  blocking collectives  74.5 us (62%)
  starting transfers between devices  17.7 us (15%)
  Pallas kernels  14.7 us (12%)
  waiting for transfers between devices  11.6 us (10%)
    all_to_all x5, blocking collectives, over_clu(): return lax.all_to_all(v, 'clu', split_axis=0, concat_axis=0, tiled=True)  57.5 us
    all_to_all x1, blocking collectives, per_device(): lax.all_to_all(payload, ('clu', 'col'), split_axis=0, concat_axis=0, tile...  17.1 us
    all_to_all x1, waiting for transfers between devices, over_clu(): return lax.all_to_all(v, 'clu', split_axis=0, concat_axis=0, tiled=True)  10.1 us
    all_to_all x1, starting transfers between devices, over_clu(): return lax.all_to_all(v, 'clu', split_axis=0, concat_axis=0, tiled=True)  9.87 us
    pallas_call x5, Pallas kernels, update(): pl.pallas_call(functools.partial(step_kernel, number, has_recv), in_specs...  7.15 us
    pallas_call x1, Pallas kernels, per_device(): pl.pallas_call(rhs_kernel, in_specs=[pl.BlockSpec(memory_space=pl.ANY)] *...  4.27 us
    ppermute x3, starting transfers between devices, over_col(): lax.ppermute(v, 'col', [(i, i ^ k) for i in range(COLS)])  3.94 us
    ppermute x3, starting transfers between devices, swap(): return lax.ppermute(v, ('clu', 'col'), pairs)  3.86 us
  transfers between devices with their start and end apart: 7, of which 3 were waited for; matrix products, arithmetic and copies ran while one was open for 0% of the time, Pallas kernels for 4%

profile of v8, /device:TPU:1, one launch (start us, length us, event | category | flops | bytes accessed | tf_op | source)
XLA Modules:
  0.0 119.2 jit_solution(16405065461918255930)
XLA Ops:
  0.6 3.4 %collective-permute-start.4 = (bf16[4,144,576]{2,1,0:T(8,128)(2,1)}, bf16[4,144,576]{2,1,0:T(8,128)(2,1)S(1)}, u32[]{:S(2)}, u32[]{:S(2)}) collective-permute-start(bf16[4,144,576]{2,1,0:T(8,128)(2,1)} %bitcast.9), channel_id=1, source_target_pairs={{0,1},{1,0},{2,3},{3,2},{4,7},{5,6},{6,5},{7,4},{8,9},{9,8},{10,11... | collective-permute-start | bytes 1990664 | tf_op jit(solution)/shard_map/ppermute | solution.py:334
  4.0 4.3 %rhs.1 = (f32[32,1,3200]{2,1,0:T(1,128)}, bf16[4,144,576]{2,1,0:T(8,128)(2,1)}) custom-call(s32[32]{0:T(128)} %cc_hbm.1, s32[4,4,32]{2,1,0:T(4,128)} %rp_hbm.1, s32[1,1024]{1,0:T(1,128)} %bitcast.12, s32[1,1024]{1,0:T(1,128)} %bitcast.15, f32[3,3,1024]{2,1,0:T(4,128)} %refs_6_.3, f32[3,1024]{1,0:T(4,128)} %grad_hbm.1, f32[1,144]{1,0:T(1,128)} %cg_hbm.1, ...), custom_call_target="tpu_custom_call" | custom-call | tf_op jit(solution)/shard_map/rhs/pallas_call | solution.py:340
  8.4 9.9 %all-to-all-start = ((f32[32,1,3200]{2,1,0:T(1,128)}), f32[32,1,3200]{2,1,0:T(1,128)S(1)}, u32[]{:S(2)}, u32[]{:S(2)}) async-start(f32[32,1,3200]{2,1,0:T(1,128)} %get-tuple-element.19), calls=%async_computation | async-start | bytes 819200 | tf_op jit(solution)/shard_map/all_to_all | solution.py:373
  18.3 0.4 collective-permute-start.5
  18.7 10.1 %all-to-all-done.recv_ref = f32[32,1,3200]{2,1,0:T(1,128)S(1)} async-done(((f32[32,1,3200]{2,1,0:T(1,128)}), f32[32,1,3200]{2,1,0:T(1,128)S(1)}, u32[]{:S(2)}, u32[]{:S(2)}) %all-to-all-start) | async-done | bytes 409632 | tf_op jit(solution)/shard_map/all_to_all | solution.py:373
  28.7 0.3 gather.1
  29.1 0.4 collective-permute-start.1
  29.5 1.7 %collective-permute-start.2 = (f32[1,4736]{1,0:T(1,128)S(1)}, f32[1,4736]{1,0:T(1,128)S(1)}, u32[]{:S(2)}, u32[]{:S(2)}) collective-permute-start(f32[1,4736]{1,0:T(1,128)S(1)} %get-tuple-element.22.v0), channel_id=1, source_target_pairs={{0,2},{1,3},{2,0},{3,1},{4,6},{5,7},{6,4},{7,5},{8,10},{9,11},{10,... | collective-permute-start | bytes 56840 | tf_op jit(solution)/shard_map/ppermute | solution.py:327
  31.3 1.8 %collective-permute-start.3 = (f32[1,4736]{1,0:T(1,128)S(1)}, f32[1,4736]{1,0:T(1,128)S(1)}, u32[]{:S(2)}, u32[]{:S(2)}) collective-permute-start(f32[1,4736]{1,0:T(1,128)S(1)} %get-tuple-element.22.v0), channel_id=1, source_target_pairs={{0,3},{1,2},{2,1},{3,0},{4,7},{5,6},{6,5},{7,4},{8,11},{9,10},{10,... | collective-permute-start | bytes 56840 | tf_op jit(solution)/shard_map/ppermute | solution.py:327
  33.1 0.5 lay_out.1.blocks_ref.refs_3_
  33.6 1.4 %collective-permute-done.3.v3 = f32[1,4736]{1,0:T(1,128)S(1)} collective-permute-done((f32[1,4736]{1,0:T(1,128)S(1)}, f32[1,4736]{1,0:T(1,128)S(1)}, u32[]{:S(2)}, u32[]{:S(2)}) %collective-permute-start.3) | collective-permute-done | bytes 18976 | tf_op jit(solution)/shard_map/ppermute | solution.py:327
  35.1 1.1 first_step.1
  36.2 12.5 %all_to_all.35.refs_1_ = f32[32,1,640]{2,1,0:T(1,128)S(1)} all-to-all(f32[32,1,640]{2,1,0:T(1,128)S(1)} %get-tuple-element.23), channel_id=1, replica_groups=mesh['clu'=32,'col'=4] {'clu'}, dimensions={0} | all-to-all | bytes 163840 | tf_op jit(solution)/shard_map/all_to_all | solution.py:373
  48.7 2.6 %step.5 = (f32[8,640]{1,0:T(8,128)S(1)}, f32[32,1,1280]{2,1,0:T(1,128)S(1)}) custom-call(s32[1,128]{1,0:T(1,128)S(1)} %get-tuple-element.21.ids_ref.refs_0_, f32[32,1,640]{2,1,0:T(1,128)S(1)} %all_to_all.35.refs_1_, f32[8,640]{1,0:T(8,128)S(1)} %get-tuple-element.24.refs_2_, bf16[4,640,576]{2,1,0:T(8,128)(2,1)S(1)} %lay_out.1.blocks_ref.refs_3_, ...), custom_call_target="tpu_custom_call" | custom-call | tf_op jit(solution)/shard_map/step/pallas_call | solution.py:409
  51.3 11.5 %all_to_all.36.refs_1_ = f32[32,1,1280]{2,1,0:T(1,128)S(1)} all-to-all(f32[32,1,1280]{2,1,0:T(1,128)S(1)} %get-tuple-element.25), channel_id=1, replica_groups=mesh['clu'=32,'col'=4] {'clu'}, dimensions={0} | all-to-all | bytes 327680 | tf_op jit(solution)/shard_map/all_to_all | solution.py:373
  62.8 0.7 step.6
  63.5 11.0 %all_to_all.37.refs_1_ = f32[32,1,640]{2,1,0:T(1,128)S(1)} all-to-all(f32[32,1,640]{2,1,0:T(1,128)S(1)} %get-tuple-element.27), channel_id=1, replica_groups=mesh['clu'=32,'col'=4] {'clu'}, dimensions={0} | all-to-all | bytes 163840 | tf_op jit(solution)/shard_map/all_to_all | solution.py:373
  74.5 2.6 %step.7 = (f32[8,640]{1,0:T(8,128)S(1)}, f32[32,1,1280]{2,1,0:T(1,128)S(1)}) custom-call(s32[1,128]{1,0:T(1,128)S(1)} %get-tuple-element.21.ids_ref.refs_0_, f32[32,1,640]{2,1,0:T(1,128)S(1)} %all_to_all.37.refs_1_, f32[8,640]{1,0:T(8,128)S(1)} %get-tuple-element.28.refs_2_, bf16[4,640,576]{2,1,0:T(8,128)(2,1)S(1)} %lay_out.1.blocks_ref.refs_3_, ...), custom_call_target="tpu_custom_call" | custom-call | tf_op jit(solution)/shard_map/step/pallas_call | solution.py:409
  77.0 11.5 %all_to_all.38.refs_1_ = f32[32,1,1280]{2,1,0:T(1,128)S(1)} all-to-all(f32[32,1,1280]{2,1,0:T(1,128)S(1)} %get-tuple-element.29), channel_id=1, replica_groups=mesh['clu'=32,'col'=4] {'clu'}, dimensions={0} | all-to-all | bytes 327680 | tf_op jit(solution)/shard_map/all_to_all | solution.py:373
  88.6 0.7 step.8
  89.2 11.0 %all_to_all.39.refs_1_ = f32[32,1,640]{2,1,0:T(1,128)S(1)} all-to-all(f32[32,1,640]{2,1,0:T(1,128)S(1)} %get-tuple-element.31), channel_id=1, replica_groups=mesh['clu'=32,'col'=4] {'clu'}, dimensions={0} | all-to-all | bytes 163840 | tf_op jit(solution)/shard_map/all_to_all | solution.py:373
  100.2 0.7 step.9
  100.9 17.1 %all_to_all.40.recv_ref = f32[128,1,640]{2,1,0:T(1,128)S(1)} all-to-all(f32[128,1,640]{2,1,0:T(1,128)S(1)} %get-tuple-element.33), channel_id=1, replica_groups=mesh['clu'=32,'col'=4] {'clu','col'}, dimensions={0} | all-to-all | bytes 655360 | tf_op jit(solution)/shard_map/all_to_all | solution.py:428
  118.0 1.3 %last_step.1 = f32[1,144]{1,0:T(1,128)} custom-call(s32[1,128]{1,0:T(1,128)S(1)} %get-tuple-element.21.ids_ref.refs_0_, f32[128,1,640]{2,1,0:T(1,128)S(1)} %all_to_all.40.recv_ref, f32[8,640]{1,0:T(8,128)S(1)} %get-tuple-element.34.state_ref, bf16[4,640,576]{2,1,0:T(8,128)(2,1)S(1)} %lay_out.1.blocks_ref.refs_3_), custom_call_target="tpu_custom_call" | custom-call | tf_op jit(solution)/shard_map/last_step/pallas_call | solution.py:429
  (16 shorter events, 0.2 us)
Async XLA Ops:
  0.6 17.7 %collective-permute-start.4 = (bf16[4,144,576]{2,1,0:T(8,128)(2,1)}, bf16[4,144,576]{2,1,0:T(8,128)(2,1)S(1)}, u32[]{:S(2)}, u32[]{:S(2)}) collective-permute-start(bf16[4,144,576]{2,1,0:T(8,128)(2,1)} %bitcast.9), channel_id=1, source_target_pairs={{0,1},{1,0},{2,3},{3,2},{4,7},{5,6},{6,5},{7,4},{8,9},{9,8},{10,11... | collective-permute-start | bytes 1990664 | tf_op jit(solution)/shard_map/ppermute | solution.py:334
  8.3 20.4 %collective-permute-start = (bf16[4,144,576]{2,1,0:T(8,128)(2,1)}, bf16[4,144,576]{2,1,0:T(8,128)(2,1)S(1)}, u32[]{:S(2)}, u32[]{:S(2)}) collective-permute-start(bf16[4,144,576]{2,1,0:T(8,128)(2,1)} %get-tuple-element.20), channel_id=1, source_target_pairs={{0,3},{1,2},{2,1},{3,0},{4,5},{5,4},{6,7},{7,6},{8,11},{9,10},{10,... | collective-permute-start | bytes 1990664 | tf_op jit(solution)/shard_map/ppermute | solution.py:334
  8.4 20.3 %all-to-all-start = ((f32[32,1,3200]{2,1,0:T(1,128)}), f32[32,1,3200]{2,1,0:T(1,128)S(1)}, u32[]{:S(2)}, u32[]{:S(2)}) async-start(f32[32,1,3200]{2,1,0:T(1,128)} %get-tuple-element.19), calls=%async_computation | async-start | bytes 819200 | tf_op jit(solution)/shard_map/all_to_all | solution.py:373
  18.3 14.8 %copy-start.1 = (bf16[1,4,576,144]{2,3,1,0:T(8,128)(2,1)S(1)}, bf16[1,4,576,144]{2,3,1,0:T(8,128)(2,1)}, u32[]{:S(2)}) copy-start(bf16[1,4,576,144]{2,3,1,0:T(8,128)(2,1)} %param.19) | copy-start | bytes 1990660
  18.3 14.8 %collective-permute-start.5 = (bf16[4,144,576]{2,1,0:T(8,128)(2,1)S(1)}, bf16[4,144,576]{2,1,0:T(8,128)(2,1)S(1)}, u32[]{:S(2)}, u32[]{:S(2)}) collective-permute-start(bf16[4,144,576]{2,1,0:T(8,128)(2,1)S(1)} %collective-permute-done.4.refs_1_), channel_id=1, source_target_pairs={{0,3},{1,2},{2,1},{3,0},{4,5},{5,4},{6,7},{7,6},{8,11},{9,10},{10,... | collective-permute-start | bytes 1990664 | tf_op jit(solution)/shard_map/ppermute | solution.py:334
  29.1 19.6 %copy-start = (bf16[1024,1728]{0,1:T(8,128)(2,1)S(1)}, bf16[1024,1728]{0,1:T(8,128)(2,1)}, u32[]{:S(2)}) copy-start(bf16[1024,1728]{0,1:T(8,128)(2,1)} %param.13) | copy-start | bytes 10616836
  29.1 19.6 %copy-start.2 = (f32[3,3,1024]{2,1,0:T(4,128)S(1)}, f32[3,3,1024]{2,1,0:T(4,128)}, u32[]{:S(2)}) copy-start(f32[3,3,1024]{2,1,0:T(4,128)} %refs_6_.3) | copy-start | bytes 110596
  29.1 19.6 %copy-start.3 = (s32[1024,1]{0,1:T(1,128)S(1)}, s32[1024,1]{0,1:T(1,128)}, u32[]{:S(2)}) copy-start(s32[1024,1]{0,1:T(1,128)} %param.11) | copy-start | bytes 12292
  29.1 19.6 %copy-start.4 = (s32[1024]{0:T(1024)S(1)}, s32[1024]{0:T(1024)}, u32[]{:S(2)}) copy-start(s32[1024]{0:T(1024)} %param.12) | copy-start | bytes 12292
  29.1 4.4 %collective-permute-start.1 = (f32[1,4736]{1,0:T(1,128)S(1)}, f32[1,4736]{1,0:T(1,128)S(1)}, u32[]{:S(2)}, u32[]{:S(2)}) collective-permute-start(f32[1,4736]{1,0:T(1,128)S(1)} %get-tuple-element.22.v0), channel_id=1, source_target_pairs={{0,1},{1,0},{2,3},{3,2},{4,5},{5,4},{6,7},{7,6},{8,9},{9,8},{10,11... | collective-permute-start | bytes 56840 | tf_op jit(solution)/shard_map/ppermute | solution.py:327
  29.5 4.1 %collective-permute-start.2 = (f32[1,4736]{1,0:T(1,128)S(1)}, f32[1,4736]{1,0:T(1,128)S(1)}, u32[]{:S(2)}, u32[]{:S(2)}) collective-permute-start(f32[1,4736]{1,0:T(1,128)S(1)} %get-tuple-element.22.v0), channel_id=1, source_target_pairs={{0,2},{1,3},{2,0},{3,1},{4,6},{5,7},{6,4},{7,5},{8,10},{9,11},{10,... | collective-permute-start | bytes 56840 | tf_op jit(solution)/shard_map/ppermute | solution.py:327
  31.3 3.8 %collective-permute-start.3 = (f32[1,4736]{1,0:T(1,128)S(1)}, f32[1,4736]{1,0:T(1,128)S(1)}, u32[]{:S(2)}, u32[]{:S(2)}) collective-permute-start(f32[1,4736]{1,0:T(1,128)S(1)} %get-tuple-element.22.v0), channel_id=1, source_target_pairs={{0,3},{1,2},{2,1},{3,0},{4,7},{5,6},{6,5},{7,4},{8,11},{9,10},{10,... | collective-permute-start | bytes 56840 | tf_op jit(solution)/shard_map/ppermute | solution.py:327

commit v9 on v8

--- a/solution.py
+++ b/solution.py
@@ -179,18 +179,19 @@
         out_ref[:, WIDE * 5 + SLOT * at : WIDE * 5 + SLOT * (at + 1)] = widen(share, SLOT)
 
 
-def couple(vectors, blocks_ref):
+def three_parts(vectors):
     row = jnp.concatenate(vectors, 1)
     high = row.astype(BF16).astype(F32)
     middle = (row - high).astype(BF16).astype(F32)
     low = row - high - middle
-    parts = jnp.concatenate([high, middle, low, jnp.zeros((13, ROUNDS * WIDE), F32)], 0)
-    out = jnp.dot(
-        parts.astype(BF16),
-        blocks_ref[...].reshape(ROUNDS * WIDE, CAM),
-        preferred_element_type=F32,
-    )
-    return widen(jnp.sum(out, 0, keepdims=True))
+    parts = [high, middle, low, jnp.zeros((13, ROUNDS * WIDE), F32)]
+    return jnp.concatenate(parts, 0).astype(BF16)
+
+
+def couple(vectors, blocks_ref, begin=0, end=CAM):
+    blocks = blocks_ref[:, :, begin:end].reshape(ROUNDS * WIDE, end - begin)
+    out = jnp.dot(three_parts(vectors), blocks, preferred_element_type=F32)
+    return jnp.sum(out, 0, keepdims=True)
 
 
 def lay_out_kernel(*refs):
@@ -230,7 +231,7 @@
     for r in range(ROUNDS):
         x = full(r + 1) * vectors[:, WIDE * (r + 1) : WIDE * (r + 2)]
         near.append(jnp.where(ids_ref[0, PARTNER_COLOUR + r] == 0, x, 0.0))
-    coupled = couple(near, blocks_ref)
+    coupled = widen(couple(near, blocks_ref))
     mine = ids_ref[0, MY_COLOUR]
     x = jnp.where(mine == 0, step * rhs, jnp.where(mine == 1, step * (rhs - coupled), 0.0))
     state_ref[0:1, :] = x
@@ -248,7 +249,7 @@
     tracks = refs[4:-2]
     new_ref, out_ref = refs[-2:]
     near = [recv_ref[ids_ref[0, PARTNER + r], :, :WIDE] for r in range(ROUNDS)]
-    coupled = couple(near, blocks_ref)
+    coupled = widen(couple(near, blocks_ref))
     x, rhs, step, diag, elim = (state_ref[i : i + 1, :] for i in range(5))
     mine = ids_ref[0, MY_COLOUR]
     if has_recv:
@@ -279,10 +280,20 @@
             v = v + recv_ref[COLS * c + k]
         return v
 
-    coupled = couple([total(ids_ref[0, PARTNER + r]) for r in range(ROUNDS)], blocks_ref)
+    near = [total(ids_ref[0, PARTNER + r]) for r in range(ROUNDS)]
     x = total(lax.axis_index("clu"))
-    x = jnp.where(ids_ref[0, MY_COLOUR] == COLOURS - 1, x - state_ref[2:3, :] * coupled, x)
-    out_ref[...] = take_share(x, lax.axis_index("col"))
+    col = lax.axis_index("col")
+    for at in range(COLS):
+
+        @pl.when(col == at)
+        def _():
+            begin = SHARE * at // LANES * LANES
+            end = min(begin + 2 * LANES, CAM)
+            coupled = couple(near, blocks_ref, begin, end)
+            share = slice(SHARE * at - begin, SHARE * (at + 1) - begin)
+            new = x[:, begin:end] - state_ref[2:3, begin:end] * coupled
+            new = jnp.where(ids_ref[0, MY_COLOUR] == COLOURS - 1, new, x[:, begin:end])
+            out_ref[...] = new[:, share]
 
 
 def eliminate(recv_ref, out_ref, dest_ref, obs_ref, info_ref, jac_ref):

time: 120 us -> 119 us (level)
  no operation moved by 1% of the time
where the time goes in v9:
time: 119 us
  blocking collectives  74.5 us (63%)
  starting transfers between devices  17.7 us (15%)
  Pallas kernels  14.4 us (12%)
  waiting for transfers between devices  11.6 us (10%)
    all_to_all x5, blocking collectives, over_clu(): return lax.all_to_all(v, 'clu', split_axis=0, concat_axis=0, tiled=True)  57.5 us
    all_to_all x1, blocking collectives, per_device(): lax.all_to_all(payload, ('clu', 'col'), split_axis=0, concat_axis=0, tile...  17.1 us
    all_to_all x1, waiting for transfers between devices, over_clu(): return lax.all_to_all(v, 'clu', split_axis=0, concat_axis=0, tiled=True)  10.1 us
    all_to_all x1, starting transfers between devices, over_clu(): return lax.all_to_all(v, 'clu', split_axis=0, concat_axis=0, tiled=True)  9.87 us
    pallas_call x5, Pallas kernels, update(): pl.pallas_call(functools.partial(step_kernel, number, has_recv), in_specs...  7.14 us
    pallas_call x1, Pallas kernels, per_device(): pl.pallas_call(rhs_kernel, in_specs=[pl.BlockSpec(memory_space=pl.ANY)] *...  4.27 us
    ppermute x3, starting transfers between devices, over_col(): lax.ppermute(v, 'col', [(i, i ^ k) for i in range(COLS)])  3.94 us
    ppermute x3, starting transfers between devices, swap(): return lax.ppermute(v, ('clu', 'col'), pairs)  3.86 us
  transfers between devices with their start and end apart: 7, of which 3 were waited for; matrix products, arithmetic and copies ran while one was open for 0% of the time, Pallas kernels for 4%

profile of v9, /device:TPU:1, one launch (start us, length us, event | category | flops | bytes accessed | tf_op | source)
XLA Modules:
  0.0 118.9 jit_solution(8987265211562858271)
XLA Ops:
  0.6 3.4 %collective-permute-start.4 = (bf16[4,144,576]{2,1,0:T(8,128)(2,1)}, bf16[4,144,576]{2,1,0:T(8,128)(2,1)S(1)}, u32[]{:S(2)}, u32[]{:S(2)}) collective-permute-start(bf16[4,144,576]{2,1,0:T(8,128)(2,1)} %bitcast.9), channel_id=1, source_target_pairs={{0,1},{1,0},{2,3},{3,2},{4,7},{5,6},{6,5},{7,4},{8,9},{9,8},{10,11... | collective-permute-start | bytes 1990664 | tf_op jit(solution)/shard_map/ppermute | solution.py:345
  4.0 4.3 %rhs.1 = (f32[32,1,3200]{2,1,0:T(1,128)}, bf16[4,144,576]{2,1,0:T(8,128)(2,1)}) custom-call(s32[32]{0:T(128)} %cc_hbm.1, s32[4,4,32]{2,1,0:T(4,128)} %rp_hbm.1, s32[1,1024]{1,0:T(1,128)} %bitcast.12, s32[1,1024]{1,0:T(1,128)} %bitcast.15, f32[3,3,1024]{2,1,0:T(4,128)} %refs_6_.3, f32[3,1024]{1,0:T(4,128)} %grad_hbm.1, f32[1,144]{1,0:T(1,128)} %cg_hbm.1, ...), custom_call_target="tpu_custom_call" | custom-call | tf_op jit(solution)/shard_map/rhs/pallas_call | solution.py:351
  8.4 9.9 %all-to-all-start = ((f32[32,1,3200]{2,1,0:T(1,128)}), f32[32,1,3200]{2,1,0:T(1,128)S(1)}, u32[]{:S(2)}, u32[]{:S(2)}) async-start(f32[32,1,3200]{2,1,0:T(1,128)} %get-tuple-element.19), calls=%async_computation | async-start | bytes 819200 | tf_op jit(solution)/shard_map/all_to_all | solution.py:384
  18.3 0.4 collective-permute-start.5
  18.7 10.1 %all-to-all-done.recv_ref = f32[32,1,3200]{2,1,0:T(1,128)S(1)} async-done(((f32[32,1,3200]{2,1,0:T(1,128)}), f32[32,1,3200]{2,1,0:T(1,128)S(1)}, u32[]{:S(2)}, u32[]{:S(2)}) %all-to-all-start) | async-done | bytes 409632 | tf_op jit(solution)/shard_map/all_to_all | solution.py:384
  28.7 0.3 gather.1
  29.1 0.4 collective-permute-start.1
  29.5 1.7 %collective-permute-start.2 = (f32[1,4736]{1,0:T(1,128)S(1)}, f32[1,4736]{1,0:T(1,128)S(1)}, u32[]{:S(2)}, u32[]{:S(2)}) collective-permute-start(f32[1,4736]{1,0:T(1,128)S(1)} %get-tuple-element.22.v0), channel_id=1, source_target_pairs={{0,2},{1,3},{2,0},{3,1},{4,6},{5,7},{6,4},{7,5},{8,10},{9,11},{10,... | collective-permute-start | bytes 56840 | tf_op jit(solution)/shard_map/ppermute | solution.py:338
  31.3 1.8 %collective-permute-start.3 = (f32[1,4736]{1,0:T(1,128)S(1)}, f32[1,4736]{1,0:T(1,128)S(1)}, u32[]{:S(2)}, u32[]{:S(2)}) collective-permute-start(f32[1,4736]{1,0:T(1,128)S(1)} %get-tuple-element.22.v0), channel_id=1, source_target_pairs={{0,3},{1,2},{2,1},{3,0},{4,7},{5,6},{6,5},{7,4},{8,11},{9,10},{10,... | collective-permute-start | bytes 56840 | tf_op jit(solution)/shard_map/ppermute | solution.py:338
  33.1 0.5 lay_out.1.blocks_ref.refs_3_
  33.6 1.4 %collective-permute-done.3.v3 = f32[1,4736]{1,0:T(1,128)S(1)} collective-permute-done((f32[1,4736]{1,0:T(1,128)S(1)}, f32[1,4736]{1,0:T(1,128)S(1)}, u32[]{:S(2)}, u32[]{:S(2)}) %collective-permute-start.3) | collective-permute-done | bytes 18976 | tf_op jit(solution)/shard_map/ppermute | solution.py:338
  35.1 1.1 first_step.1
  36.2 12.5 %all_to_all.35.refs_1_ = f32[32,1,640]{2,1,0:T(1,128)S(1)} all-to-all(f32[32,1,640]{2,1,0:T(1,128)S(1)} %get-tuple-element.23), channel_id=1, replica_groups=mesh['clu'=32,'col'=4] {'clu'}, dimensions={0} | all-to-all | bytes 163840 | tf_op jit(solution)/shard_map/all_to_all | solution.py:384
  48.7 2.6 %step.5 = (f32[8,640]{1,0:T(8,128)S(1)}, f32[32,1,1280]{2,1,0:T(1,128)S(1)}) custom-call(s32[1,128]{1,0:T(1,128)S(1)} %get-tuple-element.21.ids_ref.refs_0_, f32[32,1,640]{2,1,0:T(1,128)S(1)} %all_to_all.35.refs_1_, f32[8,640]{1,0:T(8,128)S(1)} %get-tuple-element.24.refs_2_, bf16[4,640,576]{2,1,0:T(8,128)(2,1)S(1)} %lay_out.1.blocks_ref.refs_3_, ...), custom_call_target="tpu_custom_call" | custom-call | tf_op jit(solution)/shard_map/step/pallas_call | solution.py:420
  51.3 11.5 %all_to_all.36.refs_1_ = f32[32,1,1280]{2,1,0:T(1,128)S(1)} all-to-all(f32[32,1,1280]{2,1,0:T(1,128)S(1)} %get-tuple-element.25), channel_id=1, replica_groups=mesh['clu'=32,'col'=4] {'clu'}, dimensions={0} | all-to-all | bytes 327680 | tf_op jit(solution)/shard_map/all_to_all | solution.py:384
  62.8 0.7 step.6
  63.5 11.0 %all_to_all.37.refs_1_ = f32[32,1,640]{2,1,0:T(1,128)S(1)} all-to-all(f32[32,1,640]{2,1,0:T(1,128)S(1)} %get-tuple-element.27), channel_id=1, replica_groups=mesh['clu'=32,'col'=4] {'clu'}, dimensions={0} | all-to-all | bytes 163840 | tf_op jit(solution)/shard_map/all_to_all | solution.py:384
  74.5 2.6 %step.7 = (f32[8,640]{1,0:T(8,128)S(1)}, f32[32,1,1280]{2,1,0:T(1,128)S(1)}) custom-call(s32[1,128]{1,0:T(1,128)S(1)} %get-tuple-element.21.ids_ref.refs_0_, f32[32,1,640]{2,1,0:T(1,128)S(1)} %all_to_all.37.refs_1_, f32[8,640]{1,0:T(8,128)S(1)} %get-tuple-element.28.refs_2_, bf16[4,640,576]{2,1,0:T(8,128)(2,1)S(1)} %lay_out.1.blocks_ref.refs_3_, ...), custom_call_target="tpu_custom_call" | custom-call | tf_op jit(solution)/shard_map/step/pallas_call | solution.py:420
  77.0 11.5 %all_to_all.38.refs_1_ = f32[32,1,1280]{2,1,0:T(1,128)S(1)} all-to-all(f32[32,1,1280]{2,1,0:T(1,128)S(1)} %get-tuple-element.29), channel_id=1, replica_groups=mesh['clu'=32,'col'=4] {'clu'}, dimensions={0} | all-to-all | bytes 327680 | tf_op jit(solution)/shard_map/all_to_all | solution.py:384
  88.6 0.7 step.8
  89.2 11.0 %all_to_all.39.refs_1_ = f32[32,1,640]{2,1,0:T(1,128)S(1)} all-to-all(f32[32,1,640]{2,1,0:T(1,128)S(1)} %get-tuple-element.31), channel_id=1, replica_groups=mesh['clu'=32,'col'=4] {'clu'}, dimensions={0} | all-to-all | bytes 163840 | tf_op jit(solution)/shard_map/all_to_all | solution.py:384
  100.2 0.7 step.9
  100.9 17.1 %all_to_all.40.recv_ref = f32[128,1,640]{2,1,0:T(1,128)S(1)} all-to-all(f32[128,1,640]{2,1,0:T(1,128)S(1)} %get-tuple-element.33), channel_id=1, replica_groups=mesh['clu'=32,'col'=4] {'clu','col'}, dimensions={0} | all-to-all | bytes 655360 | tf_op jit(solution)/shard_map/all_to_all | solution.py:439
  118.0 1.0 last_step.1
  (16 shorter events, 0.2 us)
Async XLA Ops:
  0.6 17.7 %collective-permute-start.4 = (bf16[4,144,576]{2,1,0:T(8,128)(2,1)}, bf16[4,144,576]{2,1,0:T(8,128)(2,1)S(1)}, u32[]{:S(2)}, u32[]{:S(2)}) collective-permute-start(bf16[4,144,576]{2,1,0:T(8,128)(2,1)} %bitcast.9), channel_id=1, source_target_pairs={{0,1},{1,0},{2,3},{3,2},{4,7},{5,6},{6,5},{7,4},{8,9},{9,8},{10,11... | collective-permute-start | bytes 1990664 | tf_op jit(solution)/shard_map/ppermute | solution.py:345
  8.3 20.4 %collective-permute-start = (bf16[4,144,576]{2,1,0:T(8,128)(2,1)}, bf16[4,144,576]{2,1,0:T(8,128)(2,1)S(1)}, u32[]{:S(2)}, u32[]{:S(2)}) collective-permute-start(bf16[4,144,576]{2,1,0:T(8,128)(2,1)} %get-tuple-element.20), channel_id=1, source_target_pairs={{0,3},{1,2},{2,1},{3,0},{4,5},{5,4},{6,7},{7,6},{8,11},{9,10},{10,... | collective-permute-start | bytes 1990664 | tf_op jit(solution)/shard_map/ppermute | solution.py:345
  8.4 20.3 %all-to-all-start = ((f32[32,1,3200]{2,1,0:T(1,128)}), f32[32,1,3200]{2,1,0:T(1,128)S(1)}, u32[]{:S(2)}, u32[]{:S(2)}) async-start(f32[32,1,3200]{2,1,0:T(1,128)} %get-tuple-element.19), calls=%async_computation | async-start | bytes 819200 | tf_op jit(solution)/shard_map/all_to_all | solution.py:384
  18.3 14.8 %copy-start.1 = (bf16[1,4,576,144]{2,3,1,0:T(8,128)(2,1)S(1)}, bf16[1,4,576,144]{2,3,1,0:T(8,128)(2,1)}, u32[]{:S(2)}) copy-start(bf16[1,4,576,144]{2,3,1,0:T(8,128)(2,1)} %param.19) | copy-start | bytes 1990660
  18.3 14.8 %collective-permute-start.5 = (bf16[4,144,576]{2,1,0:T(8,128)(2,1)S(1)}, bf16[4,144,576]{2,1,0:T(8,128)(2,1)S(1)}, u32[]{:S(2)}, u32[]{:S(2)}) collective-permute-start(bf16[4,144,576]{2,1,0:T(8,128)(2,1)S(1)} %collective-permute-done.4.refs_1_), channel_id=1, source_target_pairs={{0,3},{1,2},{2,1},{3,0},{4,5},{5,4},{6,7},{7,6},{8,11},{9,10},{10,... | collective-permute-start | bytes 1990664 | tf_op jit(solution)/shard_map/ppermute | solution.py:345
  29.1 19.6 %copy-start = (bf16[1024,1728]{0,1:T(8,128)(2,1)S(1)}, bf16[1024,1728]{0,1:T(8,128)(2,1)}, u32[]{:S(2)}) copy-start(bf16[1024,1728]{0,1:T(8,128)(2,1)} %param.13) | copy-start | bytes 10616836
  29.1 19.6 %copy-start.2 = (f32[3,3,1024]{2,1,0:T(4,128)S(1)}, f32[3,3,1024]{2,1,0:T(4,128)}, u32[]{:S(2)}) copy-start(f32[3,3,1024]{2,1,0:T(4,128)} %refs_6_.3) | copy-start | bytes 110596
  29.1 19.6 %copy-start.3 = (s32[1024,1]{0,1:T(1,128)S(1)}, s32[1024,1]{0,1:T(1,128)}, u32[]{:S(2)}) copy-start(s32[1024,1]{0,1:T(1,128)} %param.11) | copy-start | bytes 12292
  29.1 19.6 %copy-start.4 = (s32[1024]{0:T(1024)S(1)}, s32[1024]{0:T(1024)}, u32[]{:S(2)}) copy-start(s32[1024]{0:T(1024)} %param.12) | copy-start | bytes 12292
  29.1 4.4 %collective-permute-start.1 = (f32[1,4736]{1,0:T(1,128)S(1)}, f32[1,4736]{1,0:T(1,128)S(1)}, u32[]{:S(2)}, u32[]{:S(2)}) collective-permute-start(f32[1,4736]{1,0:T(1,128)S(1)} %get-tuple-element.22.v0), channel_id=1, source_target_pairs={{0,1},{1,0},{2,3},{3,2},{4,5},{5,4},{6,7},{7,6},{8,9},{9,8},{10,11... | collective-permute-start | bytes 56840 | tf_op jit(solution)/shard_map/ppermute | solution.py:338
  29.5 4.1 %collective-permute-start.2 = (f32[1,4736]{1,0:T(1,128)S(1)}, f32[1,4736]{1,0:T(1,128)S(1)}, u32[]{:S(2)}, u32[]{:S(2)}) collective-permute-start(f32[1,4736]{1,0:T(1,128)S(1)} %get-tuple-element.22.v0), channel_id=1, source_target_pairs={{0,2},{1,3},{2,0},{3,1},{4,6},{5,7},{6,4},{7,5},{8,10},{9,11},{10,... | collective-permute-start | bytes 56840 | tf_op jit(solution)/shard_map/ppermute | solution.py:338
  31.3 3.8 %collective-permute-start.3 = (f32[1,4736]{1,0:T(1,128)S(1)}, f32[1,4736]{1,0:T(1,128)S(1)}, u32[]{:S(2)}, u32[]{:S(2)}) collective-permute-start(f32[1,4736]{1,0:T(1,128)S(1)} %get-tuple-element.22.v0), channel_id=1, source_target_pairs={{0,3},{1,2},{2,1},{3,0},{4,7},{5,6},{6,5},{7,4},{8,11},{9,10},{10,... | collective-permute-start | bytes 56840 | tf_op jit(solution)/shard_map/ppermute | solution.py:338

commit v10 on v9

--- a/solution.py
+++ b/solution.py
@@ -301,23 +301,31 @@
     obs = obs_ref[...].astype(F32)
     high, low = two_parts(recv_ref[:, 0, :CAM])
     both = jnp.concatenate([high, low], 0)
-    along = []
-    for b in range(3):
-        every = lax.dot_general(
-            both, jac_ref[CAM * b : CAM * (b + 1), :], NN, preferred_element_type=F32
-        )
-        along.append(jnp.sum(fold(every) * onehot, 0, keepdims=True))
+
+    def along(lanes):
+        sums = []
+        for b in range(3):
+            rows = jac_ref[CAM * b : CAM * (b + 1), lanes]
+            every = lax.dot_general(both, rows, NN, preferred_element_type=F32)
+            sums.append(jnp.sum(fold(every) * onehot[:, lanes], 0, keepdims=True))
+        return sums
+
+    halves = [slice(0, TRK // 2), slice(TRK // 2, TRK)]
+    sums = along(halves[0])
     total = jnp.zeros((2 * CLUSTERS, CAM), F32)
-    for a in range(3):
-        u = jnp.zeros((1, TRK), F32)
-        for b in range(3):
-            u = u + obs * info_ref[a, b : b + 1, :] * along[b]
-        total = total + lax.dot_general(
-            scatter_rows(onehot, u),
-            jac_ref[CAM * a : CAM * (a + 1), :],
-            NT,
-            preferred_element_type=F32,
-        )
+    for i, lanes in enumerate(halves):
+        later = along(halves[1]) if i == 0 else None
+        for a in range(3):
+            u = jnp.zeros((1, TRK // 2), F32)
+            for b in range(3):
+                u = u + obs[:, lanes] * info_ref[a, b : b + 1, lanes] * sums[b]
+            total = total + lax.dot_general(
+                scatter_rows(onehot[:, lanes], u),
+                jac_ref[CAM * a : CAM * (a + 1), lanes],
+                NT,
+                preferred_element_type=F32,
+            )
+        sums = later
     out_ref[:, 0, WIDE:] = widen(fold(total))
 
 

time: 119 us -> 119 us (level)
  no operation moved by 1% of the time
where the time goes in v10:
time: 119 us
  blocking collectives  74.5 us (63%)
  starting transfers between devices  17.7 us (15%)
  Pallas kernels  14 us (12%)
  waiting for transfers between devices  11.6 us (10%)
    all_to_all x5, blocking collectives, over_clu(): return lax.all_to_all(v, 'clu', split_axis=0, concat_axis=0, tiled=True)  57.5 us
    all_to_all x1, blocking collectives, per_device(): lax.all_to_all(payload, ('clu', 'col'), split_axis=0, concat_axis=0, tile...  17 us
    all_to_all x1, waiting for transfers between devices, over_clu(): return lax.all_to_all(v, 'clu', split_axis=0, concat_axis=0, tiled=True)  10.1 us
    all_to_all x1, starting transfers between devices, over_clu(): return lax.all_to_all(v, 'clu', split_axis=0, concat_axis=0, tiled=True)  9.87 us
    pallas_call x5, Pallas kernels, update(): pl.pallas_call(functools.partial(step_kernel, number, has_recv), in_specs...  6.77 us
    pallas_call x1, Pallas kernels, per_device(): pl.pallas_call(rhs_kernel, in_specs=[pl.BlockSpec(memory_space=pl.ANY)] *...  4.27 us
    ppermute x3, starting transfers between devices, over_col(): lax.ppermute(v, 'col', [(i, i ^ k) for i in range(COLS)])  3.94 us
    ppermute x3, starting transfers between devices, swap(): return lax.ppermute(v, ('clu', 'col'), pairs)  3.86 us
  transfers between devices with their start and end apart: 7, of which 3 were waited for; matrix products, arithmetic and copies ran while one was open for 0% of the time, Pallas kernels for 4%

profile of v10, /device:TPU:1, one launch (start us, length us, event | category | flops | bytes accessed | tf_op | source)
XLA Modules:
  0.0 118.6 jit_solution(10657832114924800616)
XLA Ops:
  0.6 3.4 %collective-permute-start.4 = (bf16[4,144,576]{2,1,0:T(8,128)(2,1)}, bf16[4,144,576]{2,1,0:T(8,128)(2,1)S(1)}, u32[]{:S(2)}, u32[]{:S(2)}) collective-permute-start(bf16[4,144,576]{2,1,0:T(8,128)(2,1)} %bitcast.9), channel_id=1, source_target_pairs={{0,1},{1,0},{2,3},{3,2},{4,7},{5,6},{6,5},{7,4},{8,9},{9,8},{10,11... | collective-permute-start | bytes 1990664 | tf_op jit(solution)/shard_map/ppermute | solution.py:353
  4.0 4.3 %rhs.1 = (f32[32,1,3200]{2,1,0:T(1,128)}, bf16[4,144,576]{2,1,0:T(8,128)(2,1)}) custom-call(s32[32]{0:T(128)} %cc_hbm.1, s32[4,4,32]{2,1,0:T(4,128)} %rp_hbm.1, s32[1,1024]{1,0:T(1,128)} %bitcast.12, s32[1,1024]{1,0:T(1,128)} %bitcast.15, f32[3,3,1024]{2,1,0:T(4,128)} %refs_6_.3, f32[3,1024]{1,0:T(4,128)} %grad_hbm.1, f32[1,144]{1,0:T(1,128)} %cg_hbm.1, ...), custom_call_target="tpu_custom_call" | custom-call | tf_op jit(solution)/shard_map/rhs/pallas_call | solution.py:359
  8.4 9.9 %all-to-all-start = ((f32[32,1,3200]{2,1,0:T(1,128)}), f32[32,1,3200]{2,1,0:T(1,128)S(1)}, u32[]{:S(2)}, u32[]{:S(2)}) async-start(f32[32,1,3200]{2,1,0:T(1,128)} %get-tuple-element.19), calls=%async_computation | async-start | bytes 819200 | tf_op jit(solution)/shard_map/all_to_all | solution.py:392
  18.3 0.4 collective-permute-start.5
  18.7 10.1 %all-to-all-done.recv_ref = f32[32,1,3200]{2,1,0:T(1,128)S(1)} async-done(((f32[32,1,3200]{2,1,0:T(1,128)}), f32[32,1,3200]{2,1,0:T(1,128)S(1)}, u32[]{:S(2)}, u32[]{:S(2)}) %all-to-all-start) | async-done | bytes 409632 | tf_op jit(solution)/shard_map/all_to_all | solution.py:392
  28.7 0.3 gather.1
  29.1 0.4 collective-permute-start.1
  29.5 1.7 %collective-permute-start.2 = (f32[1,4736]{1,0:T(1,128)S(1)}, f32[1,4736]{1,0:T(1,128)S(1)}, u32[]{:S(2)}, u32[]{:S(2)}) collective-permute-start(f32[1,4736]{1,0:T(1,128)S(1)} %get-tuple-element.22.v0), channel_id=1, source_target_pairs={{0,2},{1,3},{2,0},{3,1},{4,6},{5,7},{6,4},{7,5},{8,10},{9,11},{10,... | collective-permute-start | bytes 56840 | tf_op jit(solution)/shard_map/ppermute | solution.py:346
  31.3 1.8 %collective-permute-start.3 = (f32[1,4736]{1,0:T(1,128)S(1)}, f32[1,4736]{1,0:T(1,128)S(1)}, u32[]{:S(2)}, u32[]{:S(2)}) collective-permute-start(f32[1,4736]{1,0:T(1,128)S(1)} %get-tuple-element.22.v0), channel_id=1, source_target_pairs={{0,3},{1,2},{2,1},{3,0},{4,7},{5,6},{6,5},{7,4},{8,11},{9,10},{10,... | collective-permute-start | bytes 56840 | tf_op jit(solution)/shard_map/ppermute | solution.py:346
  33.1 0.5 lay_out.1.blocks_ref.refs_3_
  33.6 1.4 %collective-permute-done.3.v3 = f32[1,4736]{1,0:T(1,128)S(1)} collective-permute-done((f32[1,4736]{1,0:T(1,128)S(1)}, f32[1,4736]{1,0:T(1,128)S(1)}, u32[]{:S(2)}, u32[]{:S(2)}) %collective-permute-start.3) | collective-permute-done | bytes 18976 | tf_op jit(solution)/shard_map/ppermute | solution.py:346
  35.1 1.1 first_step.1
  36.2 12.5 %all_to_all.35.refs_1_ = f32[32,1,640]{2,1,0:T(1,128)S(1)} all-to-all(f32[32,1,640]{2,1,0:T(1,128)S(1)} %get-tuple-element.23), channel_id=1, replica_groups=mesh['clu'=32,'col'=4] {'clu'}, dimensions={0} | all-to-all | bytes 163840 | tf_op jit(solution)/shard_map/all_to_all | solution.py:392
  48.7 2.4 %step.5 = (f32[8,640]{1,0:T(8,128)S(1)}, f32[32,1,1280]{2,1,0:T(1,128)S(1)}) custom-call(s32[1,128]{1,0:T(1,128)S(1)} %get-tuple-element.21.ids_ref.refs_0_, f32[32,1,640]{2,1,0:T(1,128)S(1)} %all_to_all.35.refs_1_, f32[8,640]{1,0:T(8,128)S(1)} %get-tuple-element.24.refs_2_, bf16[4,640,576]{2,1,0:T(8,128)(2,1)S(1)} %lay_out.1.blocks_ref.refs_3_, ...), custom_call_target="tpu_custom_call" | custom-call | tf_op jit(solution)/shard_map/step/pallas_call | solution.py:428
  51.1 11.5 %all_to_all.36.refs_1_ = f32[32,1,1280]{2,1,0:T(1,128)S(1)} all-to-all(f32[32,1,1280]{2,1,0:T(1,128)S(1)} %get-tuple-element.25), channel_id=1, replica_groups=mesh['clu'=32,'col'=4] {'clu'}, dimensions={0} | all-to-all | bytes 327680 | tf_op jit(solution)/shard_map/all_to_all | solution.py:392
  62.6 0.7 step.6
  63.3 11.0 %all_to_all.37.refs_1_ = f32[32,1,640]{2,1,0:T(1,128)S(1)} all-to-all(f32[32,1,640]{2,1,0:T(1,128)S(1)} %get-tuple-element.27), channel_id=1, replica_groups=mesh['clu'=32,'col'=4] {'clu'}, dimensions={0} | all-to-all | bytes 163840 | tf_op jit(solution)/shard_map/all_to_all | solution.py:392
  74.3 2.4 %step.7 = (f32[8,640]{1,0:T(8,128)S(1)}, f32[32,1,1280]{2,1,0:T(1,128)S(1)}) custom-call(s32[1,128]{1,0:T(1,128)S(1)} %get-tuple-element.21.ids_ref.refs_0_, f32[32,1,640]{2,1,0:T(1,128)S(1)} %all_to_all.37.refs_1_, f32[8,640]{1,0:T(8,128)S(1)} %get-tuple-element.28.refs_2_, bf16[4,640,576]{2,1,0:T(8,128)(2,1)S(1)} %lay_out.1.blocks_ref.refs_3_, ...), custom_call_target="tpu_custom_call" | custom-call | tf_op jit(solution)/shard_map/step/pallas_call | solution.py:428
  76.7 11.5 %all_to_all.38.refs_1_ = f32[32,1,1280]{2,1,0:T(1,128)S(1)} all-to-all(f32[32,1,1280]{2,1,0:T(1,128)S(1)} %get-tuple-element.29), channel_id=1, replica_groups=mesh['clu'=32,'col'=4] {'clu'}, dimensions={0} | all-to-all | bytes 327680 | tf_op jit(solution)/shard_map/all_to_all | solution.py:392
  88.2 0.7 step.8
  88.9 11.0 %all_to_all.39.refs_1_ = f32[32,1,640]{2,1,0:T(1,128)S(1)} all-to-all(f32[32,1,640]{2,1,0:T(1,128)S(1)} %get-tuple-element.31), channel_id=1, replica_groups=mesh['clu'=32,'col'=4] {'clu'}, dimensions={0} | all-to-all | bytes 163840 | tf_op jit(solution)/shard_map/all_to_all | solution.py:392
  99.9 0.7 step.9
  100.5 17.0 %all_to_all.40.recv_ref = f32[128,1,640]{2,1,0:T(1,128)S(1)} all-to-all(f32[128,1,640]{2,1,0:T(1,128)S(1)} %get-tuple-element.33), channel_id=1, replica_groups=mesh['clu'=32,'col'=4] {'clu','col'}, dimensions={0} | all-to-all | bytes 655360 | tf_op jit(solution)/shard_map/all_to_all | solution.py:447
  117.6 1.0 last_step.1
  (16 shorter events, 0.2 us)
Async XLA Ops:
  0.6 17.7 %collective-permute-start.4 = (bf16[4,144,576]{2,1,0:T(8,128)(2,1)}, bf16[4,144,576]{2,1,0:T(8,128)(2,1)S(1)}, u32[]{:S(2)}, u32[]{:S(2)}) collective-permute-start(bf16[4,144,576]{2,1,0:T(8,128)(2,1)} %bitcast.9), channel_id=1, source_target_pairs={{0,1},{1,0},{2,3},{3,2},{4,7},{5,6},{6,5},{7,4},{8,9},{9,8},{10,11... | collective-permute-start | bytes 1990664 | tf_op jit(solution)/shard_map/ppermute | solution.py:353
  8.3 20.4 %collective-permute-start = (bf16[4,144,576]{2,1,0:T(8,128)(2,1)}, bf16[4,144,576]{2,1,0:T(8,128)(2,1)S(1)}, u32[]{:S(2)}, u32[]{:S(2)}) collective-permute-start(bf16[4,144,576]{2,1,0:T(8,128)(2,1)} %get-tuple-element.20), channel_id=1, source_target_pairs={{0,3},{1,2},{2,1},{3,0},{4,5},{5,4},{6,7},{7,6},{8,11},{9,10},{10,... | collective-permute-start | bytes 1990664 | tf_op jit(solution)/shard_map/ppermute | solution.py:353
  8.4 20.3 %all-to-all-start = ((f32[32,1,3200]{2,1,0:T(1,128)}), f32[32,1,3200]{2,1,0:T(1,128)S(1)}, u32[]{:S(2)}, u32[]{:S(2)}) async-start(f32[32,1,3200]{2,1,0:T(1,128)} %get-tuple-element.19), calls=%async_computation | async-start | bytes 819200 | tf_op jit(solution)/shard_map/all_to_all | solution.py:392
  18.3 14.8 %copy-start.1 = (bf16[1,4,576,144]{2,3,1,0:T(8,128)(2,1)S(1)}, bf16[1,4,576,144]{2,3,1,0:T(8,128)(2,1)}, u32[]{:S(2)}) copy-start(bf16[1,4,576,144]{2,3,1,0:T(8,128)(2,1)} %param.19) | copy-start | bytes 1990660
  18.3 14.8 %collective-permute-start.5 = (bf16[4,144,576]{2,1,0:T(8,128)(2,1)S(1)}, bf16[4,144,576]{2,1,0:T(8,128)(2,1)S(1)}, u32[]{:S(2)}, u32[]{:S(2)}) collective-permute-start(bf16[4,144,576]{2,1,0:T(8,128)(2,1)S(1)} %collective-permute-done.4.refs_1_), channel_id=1, source_target_pairs={{0,3},{1,2},{2,1},{3,0},{4,5},{5,4},{6,7},{7,6},{8,11},{9,10},{10,... | collective-permute-start | bytes 1990664 | tf_op jit(solution)/shard_map/ppermute | solution.py:353
  29.1 19.6 %copy-start = (bf16[1024,1728]{0,1:T(8,128)(2,1)S(1)}, bf16[1024,1728]{0,1:T(8,128)(2,1)}, u32[]{:S(2)}) copy-start(bf16[1024,1728]{0,1:T(8,128)(2,1)} %param.13) | copy-start | bytes 10616836
  29.1 19.6 %copy-start.2 = (f32[3,3,1024]{2,1,0:T(4,128)S(1)}, f32[3,3,1024]{2,1,0:T(4,128)}, u32[]{:S(2)}) copy-start(f32[3,3,1024]{2,1,0:T(4,128)} %refs_6_.3) | copy-start | bytes 110596
  29.1 19.6 %copy-start.3 = (s32[1024,1]{0,1:T(1,128)S(1)}, s32[1024,1]{0,1:T(1,128)}, u32[]{:S(2)}) copy-start(s32[1024,1]{0,1:T(1,128)} %param.11) | copy-start | bytes 12292
  29.1 19.6 %copy-start.4 = (s32[1024]{0:T(1024)S(1)}, s32[1024]{0:T(1024)}, u32[]{:S(2)}) copy-start(s32[1024]{0:T(1024)} %param.12) | copy-start | bytes 12292
  29.1 4.4 %collective-permute-start.1 = (f32[1,4736]{1,0:T(1,128)S(1)}, f32[1,4736]{1,0:T(1,128)S(1)}, u32[]{:S(2)}, u32[]{:S(2)}) collective-permute-start(f32[1,4736]{1,0:T(1,128)S(1)} %get-tuple-element.22.v0), channel_id=1, source_target_pairs={{0,1},{1,0},{2,3},{3,2},{4,5},{5,4},{6,7},{7,6},{8,9},{9,8},{10,11... | collective-permute-start | bytes 56840 | tf_op jit(solution)/shard_map/ppermute | solution.py:346
  29.5 4.1 %collective-permute-start.2 = (f32[1,4736]{1,0:T(1,128)S(1)}, f32[1,4736]{1,0:T(1,128)S(1)}, u32[]{:S(2)}, u32[]{:S(2)}) collective-permute-start(f32[1,4736]{1,0:T(1,128)S(1)} %get-tuple-element.22.v0), channel_id=1, source_target_pairs={{0,2},{1,3},{2,0},{3,1},{4,6},{5,7},{6,4},{7,5},{8,10},{9,11},{10,... | collective-permute-start | bytes 56840 | tf_op jit(solution)/shard_map/ppermute | solution.py:346
  31.3 3.8 %collective-permute-start.3 = (f32[1,4736]{1,0:T(1,128)S(1)}, f32[1,4736]{1,0:T(1,128)S(1)}, u32[]{:S(2)}, u32[]{:S(2)}) collective-permute-start(f32[1,4736]{1,0:T(1,128)S(1)} %get-tuple-element.22.v0), channel_id=1, source_target_pairs={{0,3},{1,2},{2,1},{3,0},{4,7},{5,6},{6,5},{7,4},{8,11},{9,10},{10,... | collective-permute-start | bytes 56840 | tf_op jit(solution)/shard_map/ppermute | solution.py:346

commit v11 on v10

--- a/solution.py
+++ b/solution.py
@@ -248,6 +248,8 @@
     ids_ref, recv_ref, state_ref, blocks_ref = refs[:4]
     tracks = refs[4:-2]
     new_ref, out_ref = refs[-2:]
+    if tracks:
+        eliminate(recv_ref, out_ref, *tracks)
     near = [recv_ref[ids_ref[0, PARTNER + r], :, :WIDE] for r in range(ROUNDS)]
     coupled = widen(couple(near, blocks_ref))
     x, rhs, step, diag, elim = (state_ref[i : i + 1, :] for i in range(5))
@@ -269,8 +271,6 @@
         x = jnp.where(mine == COLOURS - 1, x + step * (rhs - diag * x + elim), x)
     for c in range(out_ref.shape[0]):
         out_ref[c, :, :WIDE] = x
-    if tracks:
-        eliminate(recv_ref, out_ref, *tracks)
 
 
 def last_step_kernel(ids_ref, recv_ref, state_ref, blocks_ref, out_ref):

time: 119 us -> 119 us (level)
  no operation moved by 1% of the time
where the time goes in v11:
time: 119 us; the launch traced here: 118 us
  blocking collectives  74.5 us (63%)
  starting transfers between devices  17.7 us (15%)
  Pallas kernels  13.8 us (12%)
  waiting for transfers between devices  11.6 us (10%)
    all_to_all x5, blocking collectives, over_clu(): return lax.all_to_all(v, 'clu', split_axis=0, concat_axis=0, tiled=True)  57.5 us
    all_to_all x1, blocking collectives, per_device(): lax.all_to_all(payload, ('clu', 'col'), split_axis=0, concat_axis=0, tile...  17 us
    all_to_all x1, waiting for transfers between devices, over_clu(): return lax.all_to_all(v, 'clu', split_axis=0, concat_axis=0, tiled=True)  10.1 us
    all_to_all x1, starting transfers between devices, over_clu(): return lax.all_to_all(v, 'clu', split_axis=0, concat_axis=0, tiled=True)  9.87 us
    pallas_call x5, Pallas kernels, update(): pl.pallas_call(functools.partial(step_kernel, number, has_recv), in_specs...  6.63 us
    pallas_call x1, Pallas kernels, per_device(): pl.pallas_call(rhs_kernel, in_specs=[pl.BlockSpec(memory_space=pl.ANY)] *...  4.27 us
    ppermute x3, starting transfers between devices, over_col(): lax.ppermute(v, 'col', [(i, i ^ k) for i in range(COLS)])  3.94 us
    ppermute x3, starting transfers between devices, swap(): return lax.ppermute(v, ('clu', 'col'), pairs)  3.86 us
  transfers between devices with their start and end apart: 7, of which 3 were waited for; matrix products, arithmetic and copies ran while one was open for 0% of the time, Pallas kernels for 4%

profile of v11, /device:TPU:1, one launch (start us, length us, event | category | flops | bytes accessed | tf_op | source)
XLA Modules:
  0.0 118.4 jit_solution(7264590977055175297)
XLA Ops:
  0.6 3.4 %collective-permute-start.4 = (bf16[4,144,576]{2,1,0:T(8,128)(2,1)}, bf16[4,144,576]{2,1,0:T(8,128)(2,1)S(1)}, u32[]{:S(2)}, u32[]{:S(2)}) collective-permute-start(bf16[4,144,576]{2,1,0:T(8,128)(2,1)} %bitcast.9), channel_id=1, source_target_pairs={{0,1},{1,0},{2,3},{3,2},{4,7},{5,6},{6,5},{7,4},{8,9},{9,8},{10,11... | collective-permute-start | bytes 1990664 | tf_op jit(solution)/shard_map/ppermute | solution.py:353
  4.0 4.3 %rhs.1 = (f32[32,1,3200]{2,1,0:T(1,128)}, bf16[4,144,576]{2,1,0:T(8,128)(2,1)}) custom-call(s32[32]{0:T(128)} %cc_hbm.1, s32[4,4,32]{2,1,0:T(4,128)} %rp_hbm.1, s32[1,1024]{1,0:T(1,128)} %bitcast.12, s32[1,1024]{1,0:T(1,128)} %bitcast.15, f32[3,3,1024]{2,1,0:T(4,128)} %refs_6_.3, f32[3,1024]{1,0:T(4,128)} %grad_hbm.1, f32[1,144]{1,0:T(1,128)} %cg_hbm.1, ...), custom_call_target="tpu_custom_call" | custom-call | tf_op jit(solution)/shard_map/rhs/pallas_call | solution.py:359
  8.4 9.9 %all-to-all-start = ((f32[32,1,3200]{2,1,0:T(1,128)}), f32[32,1,3200]{2,1,0:T(1,128)S(1)}, u32[]{:S(2)}, u32[]{:S(2)}) async-start(f32[32,1,3200]{2,1,0:T(1,128)} %get-tuple-element.19), calls=%async_computation | async-start | bytes 819200 | tf_op jit(solution)/shard_map/all_to_all | solution.py:392
  18.3 0.4 collective-permute-start.5
  18.7 10.1 %all-to-all-done.recv_ref = f32[32,1,3200]{2,1,0:T(1,128)S(1)} async-done(((f32[32,1,3200]{2,1,0:T(1,128)}), f32[32,1,3200]{2,1,0:T(1,128)S(1)}, u32[]{:S(2)}, u32[]{:S(2)}) %all-to-all-start) | async-done | bytes 409632 | tf_op jit(solution)/shard_map/all_to_all | solution.py:392
  28.7 0.3 gather.1
  29.1 0.4 collective-permute-start.1
  29.5 1.7 %collective-permute-start.2 = (f32[1,4736]{1,0:T(1,128)S(1)}, f32[1,4736]{1,0:T(1,128)S(1)}, u32[]{:S(2)}, u32[]{:S(2)}) collective-permute-start(f32[1,4736]{1,0:T(1,128)S(1)} %get-tuple-element.22.v0), channel_id=1, source_target_pairs={{0,2},{1,3},{2,0},{3,1},{4,6},{5,7},{6,4},{7,5},{8,10},{9,11},{10,... | collective-permute-start | bytes 56840 | tf_op jit(solution)/shard_map/ppermute | solution.py:346
  31.3 1.8 %collective-permute-start.3 = (f32[1,4736]{1,0:T(1,128)S(1)}, f32[1,4736]{1,0:T(1,128)S(1)}, u32[]{:S(2)}, u32[]{:S(2)}) collective-permute-start(f32[1,4736]{1,0:T(1,128)S(1)} %get-tuple-element.22.v0), channel_id=1, source_target_pairs={{0,3},{1,2},{2,1},{3,0},{4,7},{5,6},{6,5},{7,4},{8,11},{9,10},{10,... | collective-permute-start | bytes 56840 | tf_op jit(solution)/shard_map/ppermute | solution.py:346
  33.1 0.5 lay_out.1.blocks_ref.refs_3_
  33.6 1.4 %collective-permute-done.3.v3 = f32[1,4736]{1,0:T(1,128)S(1)} collective-permute-done((f32[1,4736]{1,0:T(1,128)S(1)}, f32[1,4736]{1,0:T(1,128)S(1)}, u32[]{:S(2)}, u32[]{:S(2)}) %collective-permute-start.3) | collective-permute-done | bytes 18976 | tf_op jit(solution)/shard_map/ppermute | solution.py:346
  35.1 1.1 first_step.1
  36.2 12.5 %all_to_all.35.refs_1_ = f32[32,1,640]{2,1,0:T(1,128)S(1)} all-to-all(f32[32,1,640]{2,1,0:T(1,128)S(1)} %get-tuple-element.23), channel_id=1, replica_groups=mesh['clu'=32,'col'=4] {'clu'}, dimensions={0} | all-to-all | bytes 163840 | tf_op jit(solution)/shard_map/all_to_all | solution.py:392
  48.7 2.3 %step.5 = (f32[8,640]{1,0:T(8,128)S(1)}, f32[32,1,1280]{2,1,0:T(1,128)S(1)}) custom-call(s32[1,128]{1,0:T(1,128)S(1)} %get-tuple-element.21.ids_ref.refs_0_, f32[32,1,640]{2,1,0:T(1,128)S(1)} %all_to_all.35.refs_1_, f32[8,640]{1,0:T(8,128)S(1)} %get-tuple-element.24.refs_2_, bf16[4,640,576]{2,1,0:T(8,128)(2,1)S(1)} %lay_out.1.blocks_ref.refs_3_, ...), custom_call_target="tpu_custom_call" | custom-call | tf_op jit(solution)/shard_map/step/pallas_call | solution.py:428
  51.0 11.5 %all_to_all.36.refs_1_ = f32[32,1,1280]{2,1,0:T(1,128)S(1)} all-to-all(f32[32,1,1280]{2,1,0:T(1,128)S(1)} %get-tuple-element.25), channel_id=1, replica_groups=mesh['clu'=32,'col'=4] {'clu'}, dimensions={0} | all-to-all | bytes 327680 | tf_op jit(solution)/shard_map/all_to_all | solution.py:392
  62.6 0.7 step.6
  63.2 11.0 %all_to_all.37.refs_1_ = f32[32,1,640]{2,1,0:T(1,128)S(1)} all-to-all(f32[32,1,640]{2,1,0:T(1,128)S(1)} %get-tuple-element.27), channel_id=1, replica_groups=mesh['clu'=32,'col'=4] {'clu'}, dimensions={0} | all-to-all | bytes 163840 | tf_op jit(solution)/shard_map/all_to_all | solution.py:392
  74.2 2.3 %step.7 = (f32[8,640]{1,0:T(8,128)S(1)}, f32[32,1,1280]{2,1,0:T(1,128)S(1)}) custom-call(s32[1,128]{1,0:T(1,128)S(1)} %get-tuple-element.21.ids_ref.refs_0_, f32[32,1,640]{2,1,0:T(1,128)S(1)} %all_to_all.37.refs_1_, f32[8,640]{1,0:T(8,128)S(1)} %get-tuple-element.28.refs_2_, bf16[4,640,576]{2,1,0:T(8,128)(2,1)S(1)} %lay_out.1.blocks_ref.refs_3_, ...), custom_call_target="tpu_custom_call" | custom-call | tf_op jit(solution)/shard_map/step/pallas_call | solution.py:428
  76.5 11.5 %all_to_all.38.refs_1_ = f32[32,1,1280]{2,1,0:T(1,128)S(1)} all-to-all(f32[32,1,1280]{2,1,0:T(1,128)S(1)} %get-tuple-element.29), channel_id=1, replica_groups=mesh['clu'=32,'col'=4] {'clu'}, dimensions={0} | all-to-all | bytes 327680 | tf_op jit(solution)/shard_map/all_to_all | solution.py:392
  88.1 0.7 step.8
  88.7 11.0 %all_to_all.39.refs_1_ = f32[32,1,640]{2,1,0:T(1,128)S(1)} all-to-all(f32[32,1,640]{2,1,0:T(1,128)S(1)} %get-tuple-element.31), channel_id=1, replica_groups=mesh['clu'=32,'col'=4] {'clu'}, dimensions={0} | all-to-all | bytes 163840 | tf_op jit(solution)/shard_map/all_to_all | solution.py:392
  99.7 0.7 step.9
  100.4 17.0 %all_to_all.40.recv_ref = f32[128,1,640]{2,1,0:T(1,128)S(1)} all-to-all(f32[128,1,640]{2,1,0:T(1,128)S(1)} %get-tuple-element.33), channel_id=1, replica_groups=mesh['clu'=32,'col'=4] {'clu','col'}, dimensions={0} | all-to-all | bytes 655360 | tf_op jit(solution)/shard_map/all_to_all | solution.py:447
  117.4 1.0 last_step.1
  (16 shorter events, 0.2 us)
Async XLA Ops:
  0.6 17.7 %collective-permute-start.4 = (bf16[4,144,576]{2,1,0:T(8,128)(2,1)}, bf16[4,144,576]{2,1,0:T(8,128)(2,1)S(1)}, u32[]{:S(2)}, u32[]{:S(2)}) collective-permute-start(bf16[4,144,576]{2,1,0:T(8,128)(2,1)} %bitcast.9), channel_id=1, source_target_pairs={{0,1},{1,0},{2,3},{3,2},{4,7},{5,6},{6,5},{7,4},{8,9},{9,8},{10,11... | collective-permute-start | bytes 1990664 | tf_op jit(solution)/shard_map/ppermute | solution.py:353
  8.3 20.4 %collective-permute-start = (bf16[4,144,576]{2,1,0:T(8,128)(2,1)}, bf16[4,144,576]{2,1,0:T(8,128)(2,1)S(1)}, u32[]{:S(2)}, u32[]{:S(2)}) collective-permute-start(bf16[4,144,576]{2,1,0:T(8,128)(2,1)} %get-tuple-element.20), channel_id=1, source_target_pairs={{0,3},{1,2},{2,1},{3,0},{4,5},{5,4},{6,7},{7,6},{8,11},{9,10},{10,... | collective-permute-start | bytes 1990664 | tf_op jit(solution)/shard_map/ppermute | solution.py:353
  8.4 20.3 %all-to-all-start = ((f32[32,1,3200]{2,1,0:T(1,128)}), f32[32,1,3200]{2,1,0:T(1,128)S(1)}, u32[]{:S(2)}, u32[]{:S(2)}) async-start(f32[32,1,3200]{2,1,0:T(1,128)} %get-tuple-element.19), calls=%async_computation | async-start | bytes 819200 | tf_op jit(solution)/shard_map/all_to_all | solution.py:392
  18.3 14.8 %copy-start.1 = (bf16[1,4,576,144]{2,3,1,0:T(8,128)(2,1)S(1)}, bf16[1,4,576,144]{2,3,1,0:T(8,128)(2,1)}, u32[]{:S(2)}) copy-start(bf16[1,4,576,144]{2,3,1,0:T(8,128)(2,1)} %param.19) | copy-start | bytes 1990660
  18.3 14.8 %collective-permute-start.5 = (bf16[4,144,576]{2,1,0:T(8,128)(2,1)S(1)}, bf16[4,144,576]{2,1,0:T(8,128)(2,1)S(1)}, u32[]{:S(2)}, u32[]{:S(2)}) collective-permute-start(bf16[4,144,576]{2,1,0:T(8,128)(2,1)S(1)} %collective-permute-done.4.refs_1_), channel_id=1, source_target_pairs={{0,3},{1,2},{2,1},{3,0},{4,5},{5,4},{6,7},{7,6},{8,11},{9,10},{10,... | collective-permute-start | bytes 1990664 | tf_op jit(solution)/shard_map/ppermute | solution.py:353
  29.1 19.6 %copy-start = (bf16[1024,1728]{0,1:T(8,128)(2,1)S(1)}, bf16[1024,1728]{0,1:T(8,128)(2,1)}, u32[]{:S(2)}) copy-start(bf16[1024,1728]{0,1:T(8,128)(2,1)} %param.13) | copy-start | bytes 10616836
  29.1 19.6 %copy-start.2 = (f32[3,3,1024]{2,1,0:T(4,128)S(1)}, f32[3,3,1024]{2,1,0:T(4,128)}, u32[]{:S(2)}) copy-start(f32[3,3,1024]{2,1,0:T(4,128)} %refs_6_.3) | copy-start | bytes 110596
  29.1 19.6 %copy-start.3 = (s32[1024,1]{0,1:T(1,128)S(1)}, s32[1024,1]{0,1:T(1,128)}, u32[]{:S(2)}) copy-start(s32[1024,1]{0,1:T(1,128)} %param.11) | copy-start | bytes 12292
  29.1 19.6 %copy-start.4 = (s32[1024]{0:T(1024)S(1)}, s32[1024]{0:T(1024)}, u32[]{:S(2)}) copy-start(s32[1024]{0:T(1024)} %param.12) | copy-start | bytes 12292
  29.1 4.4 %collective-permute-start.1 = (f32[1,4736]{1,0:T(1,128)S(1)}, f32[1,4736]{1,0:T(1,128)S(1)}, u32[]{:S(2)}, u32[]{:S(2)}) collective-permute-start(f32[1,4736]{1,0:T(1,128)S(1)} %get-tuple-element.22.v0), channel_id=1, source_target_pairs={{0,1},{1,0},{2,3},{3,2},{4,5},{5,4},{6,7},{7,6},{8,9},{9,8},{10,11... | collective-permute-start | bytes 56840 | tf_op jit(solution)/shard_map/ppermute | solution.py:346
  29.5 4.1 %collective-permute-start.2 = (f32[1,4736]{1,0:T(1,128)S(1)}, f32[1,4736]{1,0:T(1,128)S(1)}, u32[]{:S(2)}, u32[]{:S(2)}) collective-permute-start(f32[1,4736]{1,0:T(1,128)S(1)} %get-tuple-element.22.v0), channel_id=1, source_target_pairs={{0,2},{1,3},{2,0},{3,1},{4,6},{5,7},{6,4},{7,5},{8,10},{9,11},{10,... | collective-permute-start | bytes 56840 | tf_op jit(solution)/shard_map/ppermute | solution.py:346
  31.3 3.8 %collective-permute-start.3 = (f32[1,4736]{1,0:T(1,128)S(1)}, f32[1,4736]{1,0:T(1,128)S(1)}, u32[]{:S(2)}, u32[]{:S(2)}) collective-permute-start(f32[1,4736]{1,0:T(1,128)S(1)} %get-tuple-element.22.v0), channel_id=1, source_target_pairs={{0,3},{1,2},{2,1},{3,0},{4,7},{5,6},{6,5},{7,4},{8,11},{9,10},{10,... | collective-permute-start | bytes 56840 | tf_op jit(solution)/shard_map/ppermute | solution.py:346

commit v12 on v11

--- a/solution.py
+++ b/solution.py
@@ -180,16 +180,16 @@
 
 
 def three_parts(vectors):
-    row = jnp.concatenate(vectors, 1)
+    row = jnp.concatenate([v[:, :CAM] for v in vectors], 1)
     high = row.astype(BF16).astype(F32)
     middle = (row - high).astype(BF16).astype(F32)
     low = row - high - middle
-    parts = [high, middle, low, jnp.zeros((13, ROUNDS * WIDE), F32)]
+    parts = [high, middle, low, jnp.zeros((13, ROUNDS * CAM), F32)]
     return jnp.concatenate(parts, 0).astype(BF16)
 
 
 def couple(vectors, blocks_ref, begin=0, end=CAM):
-    blocks = blocks_ref[:, :, begin:end].reshape(ROUNDS * WIDE, end - begin)
+    blocks = blocks_ref[:, :, begin:end].reshape(ROUNDS * CAM, end - begin)
     out = jnp.dot(three_parts(vectors), blocks, preferred_element_type=F32)
     return jnp.sum(out, 0, keepdims=True)
 
@@ -204,7 +204,6 @@
             pltpu.make_async_copy(piece, blocks_ref.at[:, pl.ds(at, SHARE), :], sems.at[i])
         )
         copies[i].start()
-    blocks_ref[:, CAM:, :] = jnp.zeros((ROUNDS, WIDE - CAM, CAM), BF16)
     for copy in copies:
         copy.wait()
 
@@ -408,7 +407,7 @@
         lay_out_kernel,
         in_specs=[pl.BlockSpec(memory_space=pl.ANY)] * COLS,
         out_specs=vmem(),
-        out_shape=shape(ROUNDS, WIDE, CAM, dtype=BF16),
+        out_shape=shape(ROUNDS, CAM, CAM, dtype=BF16),
         scratch_shapes=[pltpu.SemaphoreType.DMA((COLS,))],
         compiler_params=limit,
         name="lay_out",

time: 119 us -> 119 us (level)
  no operation moved by 1% of the time
where the time goes in v12:
time: 119 us; the launch traced here: 118 us
  blocking collectives  74.5 us (63%)
  starting transfers between devices  17.7 us (15%)
  Pallas kernels  13.8 us (12%)
  waiting for transfers between devices  11.6 us (10%)
    all_to_all x5, blocking collectives, over_clu(): return lax.all_to_all(v, 'clu', split_axis=0, concat_axis=0, tiled=True)  57.5 us
    all_to_all x1, blocking collectives, per_device(): lax.all_to_all(payload, ('clu', 'col'), split_axis=0, concat_axis=0, tile...  17 us
    all_to_all x1, waiting for transfers between devices, over_clu(): return lax.all_to_all(v, 'clu', split_axis=0, concat_axis=0, tiled=True)  10.1 us
    all_to_all x1, starting transfers between devices, over_clu(): return lax.all_to_all(v, 'clu', split_axis=0, concat_axis=0, tiled=True)  9.87 us
    pallas_call x5, Pallas kernels, update(): pl.pallas_call(functools.partial(step_kernel, number, has_recv), in_specs...  6.55 us
    pallas_call x1, Pallas kernels, per_device(): pl.pallas_call(rhs_kernel, in_specs=[pl.BlockSpec(memory_space=pl.ANY)] *...  4.27 us
    ppermute x3, starting transfers between devices, over_col(): lax.ppermute(v, 'col', [(i, i ^ k) for i in range(COLS)])  3.94 us
    ppermute x3, starting transfers between devices, swap(): return lax.ppermute(v, ('clu', 'col'), pairs)  3.86 us
  transfers between devices with their start and end apart: 7, of which 3 were waited for; matrix products, arithmetic and copies ran while one was open for 0% of the time, Pallas kernels for 4%

profile of v12, /device:TPU:1, one launch (start us, length us, event | category | flops | bytes accessed | tf_op | source)
XLA Modules:
  0.0 118.3 jit_solution(15044051806665767021)
XLA Ops:
  0.6 3.4 %collective-permute-start.4 = (bf16[4,144,576]{2,1,0:T(8,128)(2,1)}, bf16[4,144,576]{2,1,0:T(8,128)(2,1)S(1)}, u32[]{:S(2)}, u32[]{:S(2)}) collective-permute-start(bf16[4,144,576]{2,1,0:T(8,128)(2,1)} %bitcast.9), channel_id=1, source_target_pairs={{0,1},{1,0},{2,3},{3,2},{4,7},{5,6},{6,5},{7,4},{8,9},{9,8},{10,11... | collective-permute-start | bytes 1990664 | tf_op jit(solution)/shard_map/ppermute | solution.py:352
  4.0 4.3 %rhs.1 = (f32[32,1,3200]{2,1,0:T(1,128)}, bf16[4,144,576]{2,1,0:T(8,128)(2,1)}) custom-call(s32[32]{0:T(128)} %cc_hbm.1, s32[4,4,32]{2,1,0:T(4,128)} %rp_hbm.1, s32[1,1024]{1,0:T(1,128)} %bitcast.12, s32[1,1024]{1,0:T(1,128)} %bitcast.15, f32[3,3,1024]{2,1,0:T(4,128)} %refs_6_.3, f32[3,1024]{1,0:T(4,128)} %grad_hbm.1, f32[1,144]{1,0:T(1,128)} %cg_hbm.1, ...), custom_call_target="tpu_custom_call" | custom-call | tf_op jit(solution)/shard_map/rhs/pallas_call | solution.py:358
  8.4 9.9 %all-to-all-start = ((f32[32,1,3200]{2,1,0:T(1,128)}), f32[32,1,3200]{2,1,0:T(1,128)S(1)}, u32[]{:S(2)}, u32[]{:S(2)}) async-start(f32[32,1,3200]{2,1,0:T(1,128)} %get-tuple-element.19), calls=%async_computation | async-start | bytes 819200 | tf_op jit(solution)/shard_map/all_to_all | solution.py:391
  18.3 0.4 collective-permute-start.5
  18.7 10.1 %all-to-all-done.recv_ref = f32[32,1,3200]{2,1,0:T(1,128)S(1)} async-done(((f32[32,1,3200]{2,1,0:T(1,128)}), f32[32,1,3200]{2,1,0:T(1,128)S(1)}, u32[]{:S(2)}, u32[]{:S(2)}) %all-to-all-start) | async-done | bytes 409632 | tf_op jit(solution)/shard_map/all_to_all | solution.py:391
  28.7 0.3 gather.1
  29.1 0.4 collective-permute-start.1
  29.5 1.7 %collective-permute-start.2 = (f32[1,4736]{1,0:T(1,128)S(1)}, f32[1,4736]{1,0:T(1,128)S(1)}, u32[]{:S(2)}, u32[]{:S(2)}) collective-permute-start(f32[1,4736]{1,0:T(1,128)S(1)} %get-tuple-element.22.v0), channel_id=1, source_target_pairs={{0,2},{1,3},{2,0},{3,1},{4,6},{5,7},{6,4},{7,5},{8,10},{9,11},{10,... | collective-permute-start | bytes 56840 | tf_op jit(solution)/shard_map/ppermute | solution.py:345
  31.3 1.8 %collective-permute-start.3 = (f32[1,4736]{1,0:T(1,128)S(1)}, f32[1,4736]{1,0:T(1,128)S(1)}, u32[]{:S(2)}, u32[]{:S(2)}) collective-permute-start(f32[1,4736]{1,0:T(1,128)S(1)} %get-tuple-element.22.v0), channel_id=1, source_target_pairs={{0,3},{1,2},{2,1},{3,0},{4,7},{5,6},{6,5},{7,4},{8,11},{9,10},{10,... | collective-permute-start | bytes 56840 | tf_op jit(solution)/shard_map/ppermute | solution.py:345
  33.1 0.5 lay_out.1.blocks_ref.refs_3_
  33.6 1.4 %collective-permute-done.3.v3 = f32[1,4736]{1,0:T(1,128)S(1)} collective-permute-done((f32[1,4736]{1,0:T(1,128)S(1)}, f32[1,4736]{1,0:T(1,128)S(1)}, u32[]{:S(2)}, u32[]{:S(2)}) %collective-permute-start.3) | collective-permute-done | bytes 18976 | tf_op jit(solution)/shard_map/ppermute | solution.py:345
  35.1 1.1 first_step.1
  36.2 12.5 %all_to_all.35.refs_1_ = f32[32,1,640]{2,1,0:T(1,128)S(1)} all-to-all(f32[32,1,640]{2,1,0:T(1,128)S(1)} %get-tuple-element.23), channel_id=1, replica_groups=mesh['clu'=32,'col'=4] {'clu'}, dimensions={0} | all-to-all | bytes 163840 | tf_op jit(solution)/shard_map/all_to_all | solution.py:391
  48.7 2.3 %step.5 = (f32[8,640]{1,0:T(8,128)S(1)}, f32[32,1,1280]{2,1,0:T(1,128)S(1)}) custom-call(s32[1,128]{1,0:T(1,128)S(1)} %get-tuple-element.21.ids_ref.refs_0_, f32[32,1,640]{2,1,0:T(1,128)S(1)} %all_to_all.35.refs_1_, f32[8,640]{1,0:T(8,128)S(1)} %get-tuple-element.24.refs_2_, bf16[4,576,576]{2,1,0:T(8,128)(2,1)S(1)} %lay_out.1.blocks_ref.refs_3_, ...), custom_call_target="tpu_custom_call" | custom-call | tf_op jit(solution)/shard_map/step/pallas_call | solution.py:427
  51.0 11.5 %all_to_all.36.refs_1_ = f32[32,1,1280]{2,1,0:T(1,128)S(1)} all-to-all(f32[32,1,1280]{2,1,0:T(1,128)S(1)} %get-tuple-element.25), channel_id=1, replica_groups=mesh['clu'=32,'col'=4] {'clu'}, dimensions={0} | all-to-all | bytes 327680 | tf_op jit(solution)/shard_map/all_to_all | solution.py:391
  62.6 0.6 step.6
  63.2 11.0 %all_to_all.37.refs_1_ = f32[32,1,640]{2,1,0:T(1,128)S(1)} all-to-all(f32[32,1,640]{2,1,0:T(1,128)S(1)} %get-tuple-element.27), channel_id=1, replica_groups=mesh['clu'=32,'col'=4] {'clu'}, dimensions={0} | all-to-all | bytes 163840 | tf_op jit(solution)/shard_map/all_to_all | solution.py:391
  74.2 2.3 %step.7 = (f32[8,640]{1,0:T(8,128)S(1)}, f32[32,1,1280]{2,1,0:T(1,128)S(1)}) custom-call(s32[1,128]{1,0:T(1,128)S(1)} %get-tuple-element.21.ids_ref.refs_0_, f32[32,1,640]{2,1,0:T(1,128)S(1)} %all_to_all.37.refs_1_, f32[8,640]{1,0:T(8,128)S(1)} %get-tuple-element.28.refs_2_, bf16[4,576,576]{2,1,0:T(8,128)(2,1)S(1)} %lay_out.1.blocks_ref.refs_3_, ...), custom_call_target="tpu_custom_call" | custom-call | tf_op jit(solution)/shard_map/step/pallas_call | solution.py:427
  76.5 11.5 %all_to_all.38.refs_1_ = f32[32,1,1280]{2,1,0:T(1,128)S(1)} all-to-all(f32[32,1,1280]{2,1,0:T(1,128)S(1)} %get-tuple-element.29), channel_id=1, replica_groups=mesh['clu'=32,'col'=4] {'clu'}, dimensions={0} | all-to-all | bytes 327680 | tf_op jit(solution)/shard_map/all_to_all | solution.py:391
  88.0 0.6 step.8
  88.7 11.0 %all_to_all.39.refs_1_ = f32[32,1,640]{2,1,0:T(1,128)S(1)} all-to-all(f32[32,1,640]{2,1,0:T(1,128)S(1)} %get-tuple-element.31), channel_id=1, replica_groups=mesh['clu'=32,'col'=4] {'clu'}, dimensions={0} | all-to-all | bytes 163840 | tf_op jit(solution)/shard_map/all_to_all | solution.py:391
  99.6 0.6 step.9
  100.3 17.0 %all_to_all.40.recv_ref = f32[128,1,640]{2,1,0:T(1,128)S(1)} all-to-all(f32[128,1,640]{2,1,0:T(1,128)S(1)} %get-tuple-element.33), channel_id=1, replica_groups=mesh['clu'=32,'col'=4] {'clu','col'}, dimensions={0} | all-to-all | bytes 655360 | tf_op jit(solution)/shard_map/all_to_all | solution.py:446
  117.3 1.0 last_step.1
  (16 shorter events, 0.2 us)
Async XLA Ops:
  0.6 17.7 %collective-permute-start.4 = (bf16[4,144,576]{2,1,0:T(8,128)(2,1)}, bf16[4,144,576]{2,1,0:T(8,128)(2,1)S(1)}, u32[]{:S(2)}, u32[]{:S(2)}) collective-permute-start(bf16[4,144,576]{2,1,0:T(8,128)(2,1)} %bitcast.9), channel_id=1, source_target_pairs={{0,1},{1,0},{2,3},{3,2},{4,7},{5,6},{6,5},{7,4},{8,9},{9,8},{10,11... | collective-permute-start | bytes 1990664 | tf_op jit(solution)/shard_map/ppermute | solution.py:352
  8.3 20.4 %collective-permute-start = (bf16[4,144,576]{2,1,0:T(8,128)(2,1)}, bf16[4,144,576]{2,1,0:T(8,128)(2,1)S(1)}, u32[]{:S(2)}, u32[]{:S(2)}) collective-permute-start(bf16[4,144,576]{2,1,0:T(8,128)(2,1)} %get-tuple-element.20), channel_id=1, source_target_pairs={{0,3},{1,2},{2,1},{3,0},{4,5},{5,4},{6,7},{7,6},{8,11},{9,10},{10,... | collective-permute-start | bytes 1990664 | tf_op jit(solution)/shard_map/ppermute | solution.py:352
  8.4 20.3 %all-to-all-start = ((f32[32,1,3200]{2,1,0:T(1,128)}), f32[32,1,3200]{2,1,0:T(1,128)S(1)}, u32[]{:S(2)}, u32[]{:S(2)}) async-start(f32[32,1,3200]{2,1,0:T(1,128)} %get-tuple-element.19), calls=%async_computation | async-start | bytes 819200 | tf_op jit(solution)/shard_map/all_to_all | solution.py:391
  18.3 14.8 %copy-start.1 = (bf16[1,4,576,144]{2,3,1,0:T(8,128)(2,1)S(1)}, bf16[1,4,576,144]{2,3,1,0:T(8,128)(2,1)}, u32[]{:S(2)}) copy-start(bf16[1,4,576,144]{2,3,1,0:T(8,128)(2,1)} %param.19) | copy-start | bytes 1990660
  18.3 14.8 %collective-permute-start.5 = (bf16[4,144,576]{2,1,0:T(8,128)(2,1)S(1)}, bf16[4,144,576]{2,1,0:T(8,128)(2,1)S(1)}, u32[]{:S(2)}, u32[]{:S(2)}) collective-permute-start(bf16[4,144,576]{2,1,0:T(8,128)(2,1)S(1)} %collective-permute-done.4.refs_1_), channel_id=1, source_target_pairs={{0,3},{1,2},{2,1},{3,0},{4,5},{5,4},{6,7},{7,6},{8,11},{9,10},{10,... | collective-permute-start | bytes 1990664 | tf_op jit(solution)/shard_map/ppermute | solution.py:352
  29.1 19.6 %copy-start = (bf16[1024,1728]{0,1:T(8,128)(2,1)S(1)}, bf16[1024,1728]{0,1:T(8,128)(2,1)}, u32[]{:S(2)}) copy-start(bf16[1024,1728]{0,1:T(8,128)(2,1)} %param.13) | copy-start | bytes 10616836
  29.1 19.6 %copy-start.2 = (f32[3,3,1024]{2,1,0:T(4,128)S(1)}, f32[3,3,1024]{2,1,0:T(4,128)}, u32[]{:S(2)}) copy-start(f32[3,3,1024]{2,1,0:T(4,128)} %refs_6_.3) | copy-start | bytes 110596
  29.1 19.6 %copy-start.3 = (s32[1024,1]{0,1:T(1,128)S(1)}, s32[1024,1]{0,1:T(1,128)}, u32[]{:S(2)}) copy-start(s32[1024,1]{0,1:T(1,128)} %param.11) | copy-start | bytes 12292
  29.1 19.6 %copy-start.4 = (s32[1024]{0:T(1024)S(1)}, s32[1024]{0:T(1024)}, u32[]{:S(2)}) copy-start(s32[1024]{0:T(1024)} %param.12) | copy-start | bytes 12292
  29.1 4.4 %collective-permute-start.1 = (f32[1,4736]{1,0:T(1,128)S(1)}, f32[1,4736]{1,0:T(1,128)S(1)}, u32[]{:S(2)}, u32[]{:S(2)}) collective-permute-start(f32[1,4736]{1,0:T(1,128)S(1)} %get-tuple-element.22.v0), channel_id=1, source_target_pairs={{0,1},{1,0},{2,3},{3,2},{4,5},{5,4},{6,7},{7,6},{8,9},{9,8},{10,11... | collective-permute-start | bytes 56840 | tf_op jit(solution)/shard_map/ppermute | solution.py:345
  29.5 4.1 %collective-permute-start.2 = (f32[1,4736]{1,0:T(1,128)S(1)}, f32[1,4736]{1,0:T(1,128)S(1)}, u32[]{:S(2)}, u32[]{:S(2)}) collective-permute-start(f32[1,4736]{1,0:T(1,128)S(1)} %get-tuple-element.22.v0), channel_id=1, source_target_pairs={{0,2},{1,3},{2,0},{3,1},{4,6},{5,7},{6,4},{7,5},{8,10},{9,11},{10,... | collective-permute-start | bytes 56840 | tf_op jit(solution)/shard_map/ppermute | solution.py:345
  31.3 3.8 %collective-permute-start.3 = (f32[1,4736]{1,0:T(1,128)S(1)}, f32[1,4736]{1,0:T(1,128)S(1)}, u32[]{:S(2)}, u32[]{:S(2)}) collective-permute-start(f32[1,4736]{1,0:T(1,128)S(1)} %get-tuple-element.22.v0), channel_id=1, source_target_pairs={{0,3},{1,2},{2,1},{3,0},{4,7},{5,6},{6,5},{7,4},{8,11},{9,10},{10,... | collective-permute-start | bytes 56840 | tf_op jit(solution)/shard_map/ppermute | solution.py:345
